TPU v7x, 32 devices: a whole 2x2x4 slice. The times are simulated.
32 devices in a mesh: groups: 2 (over x), tiles: 16 (over z, y, core).
Axes of the slice: x: 2, y: 2, z: 4, core: 2. Of those that a mesh axis runs over, the one named last changes fastest.
Arguments:
- warmth_deviation: float32 [512, 32, 128], P(('groups', 'tiles')), parts along dimension 0, may hold values from -6 to 6
- brine_deviation: float32 [512, 32, 128], P(('groups', 'tiles')), parts along dimension 0, may hold values from -6 to 6
- marine_flag_grid: int32 [512, 32], P(('groups', 'tiles')), parts along dimension 0, may hold values 0 or 1
- flooded_tier_tally: int32 [512, 32], P(('groups', 'tiles')), parts along dimension 0, may hold values from 1 to 75
- assigned_trainer: int32 [512, 32], P(('groups', 'tiles')), parts along dimension 0, may hold values from 0 to 15, as said below
- desired_spreading_rates: bfloat16 [512, 32, 128], P(('groups', 'tiles')), parts along dimension 0, may hold values from -3 to 3
- leading_intercepts: float32 [32, 1024], P(('groups', 'tiles')), parts along dimension 0, may hold values from -3 to 3
- leading_map_values: bfloat16 [256, 1024], replicated, may hold values from -0.75 to 0.75
- interior_maps: bfloat16 [2, 1024, 1024], replicated, may hold values from -0.25 to 0.25
- readout_map_values: bfloat16 [1024, 128], replicated, may hold values from -0.25 to 0.25
Outputs:
- stepped_water_state: float32 [2, 512, 32, 128], P(None, ('groups', 'tiles')), parts along dimension 1
- inferred_spreading_rates: bfloat16 [512, 32, 128], P(('groups', 'tiles')), parts along dimension 0
- leading_grad_values: float32 [512, 1024], P('groups'), parts along dimension 0
- interior_grad_values: float32 [2, 2048, 1024], P(None, 'groups'), parts along dimension 1
- readout_grad_values: float32 [2048, 128], P('groups'), parts along dimension 0
- intercept_grad_values: float32 [32, 1024], P(('groups', 'tiles')), parts along dimension 0
There are 2 independent parts, one for each index of `groups`. A program takes and returns all parts, laid end to end along the dimension named above; an argument that names none is the same for every part. Nothing has to cross between parts.
Inputs may be any that keep to these rules, and one draw needn't show every extreme that they name: `assigned_trainer`: each tile has at most 64 columns assigned to one learner; in every draw one learner receives exactly 64 columns from every tile.
All inputs are finite; a program needn't handle non-finite values. No bound on the sum of `marine_flag_grid` on one device may be relied on, other than what follows from the above.
Results may differ from a plain program's by a relative error of at most 0.012.
Values may be sent and summed in bfloat16 or wider, within the bound.
No kernel may reach another device: no remote copies, remote signals or barrier semaphores. Data moves between devices by JAX's collectives and lax.ppermute only.
A program may use at most 128 MiB of HBM per device.

v0:
```python
import math

import jax
import jax.numpy as jnp
from jax import lax
from jax.sharding import PartitionSpec as P

KAPPA = 0.2


def extended(shard, sides, width):
    for axis, dim in sides:
        peers, length = (lax.axis_size(axis), shard.shape[dim])
        up = [(i, (i + 1) % peers) for i in range(peers)]
        down = [(j, i) for i, j in up]
        last = lax.slice_in_dim(shard, length - width, length, axis=dim)
        first = lax.slice_in_dim(shard, 0, width, axis=dim)
        before = lax.ppermute(last, axis, up)
        after = lax.ppermute(first, axis, down)
        shard = jnp.concatenate([before, shard, after], axis=dim)
    return shard


def silu_slope(pre_act):
    logistic = jax.nn.sigmoid(pre_act)
    return logistic * (1.0 + pre_act * (1.0 - logistic))


def contract_rows(left_rows, right_rows):
    return lax.dot_general(
        left_rows, right_rows, (((0,), (0,)), ((), ())), preferred_element_type=jnp.float32
    )


def times_transposed(left_rows, right_rows):
    return lax.dot_general(
        left_rows, right_rows, (((1,), (1,)), ((), ())), preferred_element_type=jnp.float32
    )


def wet_levels(marine_flag_grid, flooded_tier_tally, water_stratification):
    level_index = jnp.arange(water_stratification, dtype=jnp.int32)
    return (
        (level_index < flooded_tier_tally[..., None]) & (marine_flag_grid[..., None] > 0)
    ).astype(jnp.float32)


def spread_apart(bordered_with_ghosts):
    padded = jnp.pad(bordered_with_ghosts, ((0, 0), (0, 0), (1, 1), (0, 0)))
    centre = padded[:, 1:-1, 1:-1]
    summed = jnp.zeros_like(centre[:2])
    for beside in (
        padded[:, 2:, 1:-1],
        padded[:, :-2, 1:-1],
        padded[:, 1:-1, 2:],
        padded[:, 1:-1, :-2],
    ):
        summed = summed + beside[2] * (beside[:2] - centre[:2])
    return centre[:2] + KAPPA * centre[2] * summed


def keep_local(gradient):
    return gradient


def train_rows(
    descriptor_values,
    bias_rows,
    targets,
    wet_rows,
    leading_map_values,
    interior_maps,
    readout_map_values,
    loss_scale,
    finish,
):
    pre_act = (
        jnp.dot(descriptor_values, leading_map_values, preferred_element_type=jnp.float32)
        + bias_rows
    )
    pre_list = [pre_act]
    active = jax.nn.silu(pre_act).astype(jnp.bfloat16)
    active_list = [active]
    for layer_index in range(interior_maps.shape[0]):
        pre_act = jnp.dot(active, interior_maps[layer_index], preferred_element_type=jnp.float32)
        pre_list.append(pre_act)
        active = jax.nn.silu(pre_act).astype(jnp.bfloat16)
        active_list.append(active)
    output = jnp.dot(active, readout_map_values, preferred_element_type=jnp.float32)
    residual_rows = ((output - targets.astype(jnp.float32)) * wet_rows * loss_scale).astype(
        jnp.bfloat16
    )
    readout_grad_values = finish(contract_rows(active, residual_rows))
    upward = times_transposed(residual_rows, readout_map_values)
    grad_layers = []
    for layer_index in reversed(range(interior_maps.shape[0])):
        error_signals = (upward * silu_slope(pre_list[layer_index + 1])).astype(jnp.bfloat16)
        grad_layers.insert(0, finish(contract_rows(active_list[layer_index], error_signals)))
        upward = times_transposed(error_signals, interior_maps[layer_index])
    error_signals = (upward * silu_slope(pre_list[0])).astype(jnp.bfloat16)
    leading_grad_values = finish(contract_rows(descriptor_values, error_signals))
    return (
        output.astype(jnp.bfloat16),
        error_signals,
        leading_grad_values,
        jnp.stack(grad_layers),
        readout_grad_values,
    )


def local(
    warmth_deviation,
    brine_deviation,
    marine_flag_grid,
    flooded_tier_tally,
    assigned_trainer,
    desired_spreading_rates,
    leading_intercepts,
    leading_map_values,
    interior_maps,
    readout_map_values,
):
    water_stratification = warmth_deviation.shape[-1]
    upright_piles = warmth_deviation.shape[0] * warmth_deviation.shape[1]
    student_models = lax.axis_size("tiles")
    room_limit = 2 * upright_piles // student_models
    loss_scale = 1.0 / math.sqrt(upright_piles * student_models)
    marine_locations = wet_levels(marine_flag_grid, flooded_tier_tally, water_stratification)
    carried_fluid_state = jnp.stack([warmth_deviation, brine_deviation, marine_locations])
    bordered_with_ghosts = extended(carried_fluid_state, (("tiles", 1),), 1)
    stepped_water_state = spread_apart(bordered_with_ghosts)
    descriptor_values = (
        (stepped_water_state * marine_locations)
        .transpose(1, 2, 0, 3)
        .reshape(upright_piles, 2 * water_stratification)
        .astype(jnp.bfloat16)
    )
    target_rows = desired_spreading_rates.reshape(upright_piles, water_stratification)
    flat_assign = assigned_trainer.reshape(upright_piles)
    selector = flat_assign[:, None] == jnp.arange(student_models, dtype=jnp.int32)[None, :]
    running = jnp.cumsum(selector.astype(jnp.int32), axis=0)
    slot_index = jnp.sum(jnp.where(selector, running, 0), axis=1) - 1
    target_slot = flat_assign * room_limit + slot_index
    depth_count = (
        jnp.where(marine_flag_grid > 0, flooded_tier_tally, 0)
        .reshape(upright_piles)
        .astype(jnp.float32)
        .astype(jnp.bfloat16)
    )
    slot_rows = student_models * room_limit
    send_features = (
        jnp.zeros((slot_rows, 2 * water_stratification), jnp.bfloat16)
        .at[target_slot]
        .set(descriptor_values)
    )
    send_targets = (
        jnp.zeros((slot_rows, water_stratification), jnp.bfloat16).at[target_slot].set(target_rows)
    )
    send_counts = jnp.zeros((slot_rows,), jnp.bfloat16).at[target_slot].set(depth_count)
    got_features, got_targets, got_counts = (
        lax.all_to_all(
            send_features.reshape(student_models, room_limit, 2 * water_stratification),
            "tiles",
            split_axis=0,
            concat_axis=0,
            tiled=True,
        ),
        lax.all_to_all(
            send_targets.reshape(student_models, room_limit, water_stratification),
            "tiles",
            split_axis=0,
            concat_axis=0,
            tiled=True,
        ),
        lax.all_to_all(
            send_counts.reshape(student_models, room_limit),
            "tiles",
            split_axis=0,
            concat_axis=0,
            tiled=True,
        ),
    )
    level_index = jnp.arange(water_stratification, dtype=jnp.float32)
    wet_rows = (level_index[None, :] < got_counts.reshape(slot_rows, 1).astype(jnp.float32)).astype(
        jnp.float32
    )
    outcomes = train_rows(
        got_features.reshape(slot_rows, 2 * water_stratification),
        leading_intercepts,
        got_targets.reshape(slot_rows, water_stratification),
        wet_rows,
        leading_map_values,
        interior_maps,
        readout_map_values,
        loss_scale,
        keep_local,
    )
    (
        inferred_stirring_rate,
        error_signals,
        leading_grad_values,
        interior_grad_values,
        readout_grad_values,
    ) = outcomes
    intercept_grad_values = jnp.dot(
        jnp.ones((1, slot_rows), jnp.bfloat16), error_signals, preferred_element_type=jnp.float32
    )
    returned = lax.all_to_all(
        inferred_stirring_rate.reshape(student_models, room_limit, water_stratification),
        "tiles",
        split_axis=0,
        concat_axis=0,
        tiled=True,
    )
    inferred_spreading_rates = returned.reshape(slot_rows, water_stratification)[target_slot]
    leading_grad_values, interior_grad_values, readout_grad_values = (
        lax.psum(leading_grad_values.astype(jnp.bfloat16), "tiles").astype(jnp.float32),
        lax.psum(interior_grad_values.astype(jnp.bfloat16), "tiles").astype(jnp.float32),
        lax.psum(readout_grad_values.astype(jnp.bfloat16), "tiles").astype(jnp.float32),
    )
    return (
        stepped_water_state,
        inferred_spreading_rates.reshape(warmth_deviation.shape),
        leading_grad_values,
        interior_grad_values,
        readout_grad_values,
        intercept_grad_values,
    )


def solution(mesh):
    return jax.shard_map(
        local,
        mesh=mesh,
        in_specs=(
            P(("groups", "tiles"), None, None),
            P(("groups", "tiles"), None, None),
            P(("groups", "tiles"), None),
            P(("groups", "tiles"), None),
            P(("groups", "tiles"), None),
            P(("groups", "tiles"), None, None),
            P(("groups", "tiles"), None),
            P(),
            P(),
            P(),
        ),
        out_specs=(
            P(None, ("groups", "tiles"), None, None),
            P(("groups", "tiles"), None, None),
            P("groups", None),
            P(None, "groups", None),
            P("groups", None),
            P(("groups", "tiles"), None),
        ),
        check_vma=False,
    )
```

profile of v0, /device:TPU:0, one launch (start us, length us, event | category | flops | bytes accessed | tf_op | source)
XLA Modules:
  0.0 240.6 jit_solution(16538322084439100312)
XLA Ops:
  9.7 5.5 %collective-permute-start = (f32[3,1,32,128]{3,2,1,0:T(8,128)S(1)}, f32[3,1,32,128]{3,2,1,0:T(8,128)S(1)}, u32[]{:S(2)}, u32[]{:S(2)}) collective-permute-start(f32[3,1,32,128]{3,2,1,0:T(8,128)S(1)} %get-tuple-element.18), channel_id=1, source_target_pairs={{1,0},{2,1},{3,2},{4,3},{5,4},{6,5},{7,6},{8,7},{9,8},{10,9},{11,1... | collective-permute-start | bytes 147464 | tf_op jit(solution)/shard_map/ppermute | solution.py:19
  17.4 1.1 reduce-window.6
  19.1 3.8 %scatter_custom_fusion.1 = bf16[1024]{0:T(1024)(128)(2,1)S(1)} fusion(s32[512]{0:T(512)S(1)} %bitcast.90, bf16[512]{0:T(512)(128)(2,1)S(1)} %reshape.158, bf16[]{:T(256)} %constant.13.clone.1), kind=kCustom, calls=%fused_computation.97 | custom fusion | bytes 2050 | tf_op jit(solution)/shard_map/scatter | solution.py:159
  23.6 5.8 %all-to-all-start.2 = ((bf16[16,1,64]{2,1,0:T(2,128)(2,1)}), bf16[16,1,64]{2,1,0:T(2,128)(2,1)S(1)}, u32[]{:S(2)}, u32[]{:S(2)}) async-start(bf16[16,1,64]{2,1,0:T(2,128)(2,1)} %all_to_all.20), calls=%async_computation.2 | async-start | bytes 16384 | tf_op jit(solution)/shard_map/all_to_all | solution.py:175
  31.2 1.2 select_maximum_fusion
  32.6 1.1 fusion.25
  34.0 3.1 %scatter_custom_fusion = bf16[1024,256]{1,0:T(8,128)(2,1)} fusion(s32[512]{0:T(512)S(1)} %bitcast.91, bf16[64,8,2,128]{3,2,1,0:T(2,128)(2,1)S(1)} %bitcast.88, bf16[]{:T(256)} %constant.13.clone.1), kind=kCustom, calls=%fused_computation.61 | custom fusion | bytes 786434 | tf_op jit(solution)/shard_map/scatter | solution.py:154
  37.1 6.0 %all-to-all-start = ((bf16[16,64,256]{2,1,0:T(8,128)(2,1)}), bf16[16,64,256]{2,1,0:T(8,128)(2,1)S(1)}, u32[]{:S(2)}, u32[]{:S(2)}) async-start(bf16[16,64,256]{2,1,0:T(8,128)(2,1)} %bitcast.10), calls=%async_computation | async-start | bytes 1048576 | tf_op jit(solution)/shard_map/all_to_all | solution.py:161
  43.1 2.8 %scatter_custom_fusion.2 = bf16[1024,128]{1,0:T(8,128)(2,1)} fusion(s32[512]{0:T(512)S(1)} %bitcast.92, bf16[512,128]{1,0:T(8,128)(2,1)} %bitcast.95, bf16[]{:T(256)} %constant.13.clone.1), kind=kCustom, calls=%fused_computation.76 | custom fusion | bytes 262656 | tf_op jit(solution)/shard_map/scatter | solution.py:157
  46.0 11.6 %all-to-all-done = bf16[16,64,256]{2,1,0:T(8,128)(2,1)S(1)} async-done(((bf16[16,64,256]{2,1,0:T(8,128)(2,1)}), bf16[16,64,256]{2,1,0:T(8,128)(2,1)S(1)}, u32[]{:S(2)}, u32[]{:S(2)}) %all-to-all-start) | async-done | bytes 524320 | tf_op jit(solution)/shard_map/all_to_all | solution.py:161
  57.6 4.1 %all-to-all-start.3 = ((bf16[16,64,128]{2,1,0:T(8,128)(2,1)}), bf16[16,64,128]{2,1,0:T(8,128)(2,1)S(1)}, u32[]{:S(2)}, u32[]{:S(2)}) async-start(bf16[16,64,128]{2,1,0:T(8,128)(2,1)} %bitcast.19), calls=%async_computation.3 | async-start | bytes 524288 | tf_op jit(solution)/shard_map/all_to_all | solution.py:168
  62.7 2.0 copy-done.1
  65.4 2.4 fusion.4
  67.8 2.0 copy-done.12
  69.7 4.4 %multiply_convert_fusion.3 = (bf16[1024,1024]{1,0:T(8,128)(2,1)S(1)}, f32[1024,1024]{1,0:T(8,128)}) fusion(bf16[2,1024,1024]{2,1,0:T(8,128)(2,1)S(1)} %copy-done.7, f32[1024,1024]{1,0:T(8,128)S(1)} %fusion.4), kind=kOutput, calls=%fused_computation.8 | convolution fusion | flops 2157969408 | bytes 12582912 | tf_op jit(solution)/shard_map/dot_general | solution.py:85
  74.1 2.5 %fusion.24 = (bf16[1024,128]{1,0:T(8,128)(2,1)S(1)}, bf16[1024,128]{1,0:T(8,128)(2,1)}) fusion(bf16[16,64,128]{2,1,0:T(8,128)(2,1)S(1)} %all-to-all-done.3, f32[1024]{0:T(1024)S(1)} %reshape.136, bf16[1024,1024]{1,0:T(8,128)(2,1)S(1)} %get-tuple-element.21, bf16[1024,128]{1,0:T(8,128)(2,1)} %param.19), kind=kOutput, calls=%fused_computation.57 | convolution fusion | flops 269352960 | bytes 3149824 | tf_op jit(solution)/shard_map/dot_general | solution.py:89
  76.7 1.5 convolution_convert_fusion.1
  78.2 1.7 multiply_convert_fusion.2
  80.4 1.3 copy-done.13
  81.6 3.2 %multiply_convert_fusion.1 = bf16[1024,1024]{1,0:T(8,128)(2,1)S(1)} fusion(f32[1024,1024]{1,0:T(8,128)S(1)} %copy-done.13, bf16[1024,1024]{1,0:T(8,128)(2,1)S(1)} %multiply_convert_fusion.2, bf16[2,1024,1024]{2,1,0:T(8,128)(2,1)S(1)} %copy-done.8), kind=kOutput, calls=%fused_computation.6 | convolution fusion | flops 2156920832 | bytes 10485760 | tf_op jit(solution)/shard_map/dot_general | solution.py:36
  84.9 2.5 %convert_bitcast_fusion = bf16[1,1024,1024]{2,1,0:T(8,128)(2,1)S(1)} fusion(bf16[1024,1024]{1,0:T(8,128)(2,1)S(1)} %multiply_convert_fusion.2, f32[1024,1024]{1,0:T(8,128)S(1)} %copy-done.13), kind=kOutput, calls=%fused_computation.20 | convolution fusion | flops 2153775104 | bytes 8388608 | tf_op jit(solution)/shard_map/dot_general | solution.py:30
  87.4 2.6 %convert_bitcast_fusion.1 = bf16[1,1024,1024]{2,1,0:T(8,128)(2,1)S(1)} fusion(bf16[1024,1024]{1,0:T(8,128)(2,1)S(1)} %multiply_convert_fusion.1, f32[1024,1024]{1,0:T(8,128)S(1)} %copy-done.2, f32[1024]{0:T(1024)S(1)} %bitcast.97), kind=kOutput, calls=%fused_computation.21 | convolution fusion | flops 2154823680 | bytes 8392704 | tf_op jit(solution)/shard_map/dot_general | solution.py:30
  89.9 3.5 %multiply_convert_fusion = bf16[1024,1024]{1,0:T(8,128)(2,1)S(1)} fusion(f32[1024,1024]{1,0:T(8,128)S(1)} %copy-done.2, bf16[1024,1024]{1,0:T(8,128)(2,1)S(1)} %multiply_convert_fusion.1, f32[1024]{0:T(1024)S(1)} %bitcast.98, bf16[2,1024,1024]{2,1,0:T(8,128)(2,1)S(1)} %copy-done.8), kind=kOutput, calls=%fused_computation.5 | convolution fusion | flops 2157969408 | bytes 10489856 | tf_op jit(solution)/shard_map/dot_general | solution.py:36
  93.4 1.5 convolution_convert_fusion
  94.9 2.4 pad_maximum_fusion
  97.3 6.0 %all-to-all-start.1 = ((bf16[16,64,128]{2,1,0:T(8,128)(2,1)}), bf16[16,64,128]{2,1,0:T(8,128)(2,1)S(1)}, u32[]{:S(2)}, u32[]{:S(2)}) async-start(bf16[16,64,128]{2,1,0:T(8,128)(2,1)} %bitcast.15), calls=%async_computation.1 | async-start | bytes 524288 | tf_op jit(solution)/shard_map/all_to_all | solution.py:208
  103.4 1.0 fusion.40
  104.3 13.2 %all-to-all-done.1 = bf16[16,64,128]{2,1,0:T(8,128)(2,1)S(1)} async-done(((bf16[16,64,128]{2,1,0:T(8,128)(2,1)}), bf16[16,64,128]{2,1,0:T(8,128)(2,1)S(1)}, u32[]{:S(2)}, u32[]{:S(2)}) %all-to-all-start.1) | async-done | bytes 262176 | tf_op jit(solution)/shard_map/all_to_all | solution.py:208
  117.5 1.9 gather_fusion
  119.4 105.7 %all-reduce.4.cloned.1.call-done = (bf16[256,1024]{1,0:T(8,128)(2,1)}, bf16[2,1024,1024]{2,1,0:T(8,128)(2,1)}, bf16[1024,128]{1,0:T(8,128)(2,1)}) async-done(((bf16[256,1024]{1,0:T(8,128)(2,1)}, bf16[2,1024,1024]{2,1,0:T(8,128)(2,1)}, bf16[1024,128]{1,0:T(8,128)(2,1)}), (bf16[256,1024]{1,0:T(8,128)(2,1)}, bf16[2,1024,1024]{2,1,0:T(8,128)(2,1)}, bf16[1024,128]{1,0:T(8,128)(2,1)})) %all-reduce.4.cloned.1.call-update) | async-done | bytes 4980752 | tf_op jit(solution)/shard_map/psum | solution.py:217
  225.1 6.7 %convert_element_type.122 = f32[2,1024,1024]{2,1,0:T(8,128)} convert(bf16[2,1024,1024]{2,1,0:T(8,128)(2,1)} %get-tuple-element.7) | non-fusion elementwise | flops 2097152 | bytes 12582912 | tf_op jit(solution)/shard_map/convert_element_type | solution.py:218
  231.8 1.1 convert_element_type.121
  (57 shorter events, 11.2 us)
Async XLA Ops:
  7.2 54.8 %copy-start = (bf16[256,1024]{1,0:T(8,128)(2,1)S(1)}, bf16[256,1024]{1,0:T(8,128)(2,1)}, u32[]{:S(2)}) copy-start(bf16[256,1024]{1,0:T(8,128)(2,1)} %param.17) | copy-start | bytes 1572868
  7.2 25.4 %copy-start.4 = (f32[16,32,128]{2,1,0:T(8,128)S(1)}, f32[16,32,128]{2,1,0:T(8,128)}, u32[]{:S(2)}) copy-start(f32[16,32,128]{2,1,0:T(8,128)} %param.10) | copy-start | bytes 786436
  7.2 25.4 %copy-start.3 = (f32[16,32,128]{2,1,0:T(8,128)S(1)}, f32[16,32,128]{2,1,0:T(8,128)}, u32[]{:S(2)}) copy-start(f32[16,32,128]{2,1,0:T(8,128)} %param.11) | copy-start | bytes 786436
  9.7 21.5 %collective-permute-start = (f32[3,1,32,128]{3,2,1,0:T(8,128)S(1)}, f32[3,1,32,128]{3,2,1,0:T(8,128)S(1)}, u32[]{:S(2)}, u32[]{:S(2)}) collective-permute-start(f32[3,1,32,128]{3,2,1,0:T(8,128)S(1)} %get-tuple-element.18), channel_id=1, source_target_pairs={{1,0},{2,1},{3,2},{4,3},{5,4},{6,5},{7,6},{8,7},{9,8},{10,9},{11,1... | collective-permute-start | bytes 147464 | tf_op jit(solution)/shard_map/ppermute | solution.py:19
  15.2 16.0 %collective-permute-start.1 = (f32[3,1,32,128]{3,2,1,0:T(8,128)S(1)}, f32[3,1,32,128]{3,2,1,0:T(8,128)S(1)}, u32[]{:S(2)}, u32[]{:S(2)}) collective-permute-start(f32[3,1,32,128]{3,2,1,0:T(8,128)S(1)} %get-tuple-element.17), channel_id=1, source_target_pairs={{0,1},{1,2},{2,3},{3,4},{4,5},{5,6},{6,7},{7,8},{8,9},{9,10},{10,1... | collective-permute-start | bytes 147464 | tf_op jit(solution)/shard_map/ppermute | solution.py:18
  23.6 13.6 %all-to-all-start.2 = ((bf16[16,1,64]{2,1,0:T(2,128)(2,1)}), bf16[16,1,64]{2,1,0:T(2,128)(2,1)S(1)}, u32[]{:S(2)}, u32[]{:S(2)}) async-start(bf16[16,1,64]{2,1,0:T(2,128)(2,1)} %all_to_all.20), calls=%async_computation.2 | async-start | bytes 16384 | tf_op jit(solution)/shard_map/all_to_all | solution.py:175
  37.1 20.5 %all-to-all-start = ((bf16[16,64,256]{2,1,0:T(8,128)(2,1)}), bf16[16,64,256]{2,1,0:T(8,128)(2,1)S(1)}, u32[]{:S(2)}, u32[]{:S(2)}) async-start(bf16[16,64,256]{2,1,0:T(8,128)(2,1)} %bitcast.10), calls=%async_computation | async-start | bytes 1048576 | tf_op jit(solution)/shard_map/all_to_all | solution.py:161
  57.6 16.5 %all-to-all-start.3 = ((bf16[16,64,128]{2,1,0:T(8,128)(2,1)}), bf16[16,64,128]{2,1,0:T(8,128)(2,1)S(1)}, u32[]{:S(2)}, u32[]{:S(2)}) async-start(bf16[16,64,128]{2,1,0:T(8,128)(2,1)} %bitcast.19), calls=%async_computation.3 | async-start | bytes 524288 | tf_op jit(solution)/shard_map/all_to_all | solution.py:168
  61.7 163.4 %all-reduce.4.cloned.1.call-start = ((), (), s32[]{:S(2)}) async-start(), calls=%async_computation.4 | async-start | bytes 9961472 | tf_op jit(solution)/shard_map/psum | solution.py:217
  62.0 3.4 %copy-start.7 = (bf16[2,1024,1024]{2,1,0:T(8,128)(2,1)S(1)}, bf16[2,1024,1024]{2,1,0:T(8,128)(2,1)}, u32[]{:S(2)}) copy-start(bf16[2,1024,1024]{2,1,0:T(8,128)(2,1)} %param.18) | copy-start | bytes 12582916
  62.0 3.4 %copy-start.10 = (f32[1,1024]{1,0:T(1,128)S(1)}, f32[1,1024]{1,0:T(1,128)}, u32[]{:S(2)}) copy-start(f32[1,1024]{1,0:T(1,128)} %param.16) | copy-start | bytes 12292
  62.7 2.0 copy-start.1
  67.8 2.0 copy-start.12
  74.1 4.0 %copy-start.9 = (bf16[1024,128]{1,0:T(8,128)(2,1)S(1)}, bf16[1024,128]{1,0:T(8,128)(2,1)}, u32[]{:S(2)}) copy-start(bf16[1024,128]{1,0:T(8,128)(2,1)} %param.19) | copy-start | bytes 786436
  74.1 4.0 %copy-start.11 = (f32[1024,1024]{1,0:T(8,128)S(1)}, f32[1024,1024]{1,0:T(8,128)}, u32[]{:S(2)}) copy-start(f32[1024,1024]{1,0:T(8,128)} %get-tuple-element.22) | copy-start | bytes 12582916
  78.2 2.2 copy-start.8
  78.2 3.5 %copy-start.13 = (f32[1024,1024]{1,0:T(8,128)S(1)}, f32[1024,1024]{1,0:T(8,128)}, u32[]{:S(2)}) copy-start(f32[1024,1024]{1,0:T(8,128)} %copy-done.12) | copy-start | bytes 12582916
  84.8 2.5 %copy-start.2 = (f32[1024,1024]{1,0:T(8,128)S(1)}, f32[1024,1024]{1,0:T(8,128)}, u32[]{:S(2)}) copy-start(f32[1024,1024]{1,0:T(8,128)} %copy-done.1) | copy-start | bytes 12582916
  97.3 20.2 %all-to-all-start.1 = ((bf16[16,64,128]{2,1,0:T(8,128)(2,1)}), bf16[16,64,128]{2,1,0:T(8,128)(2,1)S(1)}, u32[]{:S(2)}, u32[]{:S(2)}) async-start(bf16[16,64,128]{2,1,0:T(8,128)(2,1)} %bitcast.15), calls=%async_computation.1 | async-start | bytes 524288 | tf_op jit(solution)/shard_map/all_to_all | solution.py:208
  225.1 6.7 %copy-start.5 = (bf16[256,1024]{1,0:T(8,128)(2,1)S(1)}, bf16[256,1024]{1,0:T(8,128)(2,1)}, u32[]{:S(2)}) copy-start(bf16[256,1024]{1,0:T(8,128)(2,1)} %get-tuple-element.6) | copy-start | bytes 1572868
  225.1 7.8 %copy-start.6 = (bf16[1024,128]{1,0:T(8,128)(2,1)S(1)}, bf16[1024,128]{1,0:T(8,128)(2,1)}, u32[]{:S(2)}) copy-start(bf16[1024,128]{1,0:T(8,128)(2,1)} %get-tuple-element.8) | copy-start | bytes 786436
Sparse Core Ops, SparseCore 0:
  97.4 127.6 all-reduce.3
where the time goes:
time: 242 us; the launch traced here: 241 us
  waiting for transfers between devices  130 us (54%)
  starting transfers between devices  27.6 us (11%)
  matrix products  27.4 us (11%)
  local copies, waits for them, and re-layouts  21 us (9%)
  other arithmetic  19.7 us (8%)
  between operations  14.3 us (6%)
    psum x1, waiting for transfers between devices, local(): lax.psum(leading_grad_values.astype(jnp.bfloat16), 'tiles')  106 us
    all_to_all x1, waiting for transfers between devices, local(): lax.all_to_all(inferred_stirring_rate.reshape(student_models, room_limit,...  13.2 us
    all_to_all x1, waiting for transfers between devices, local(): lax.all_to_all(send_features.reshape(student_models, room_limit, 2 * wate...  11.6 us
    dot_general x3, matrix products, times_transposed(): lax.dot_general(left_rows, right_rows, (((1,), (1,)), ((), ())), preferre...  8.34 us
    dot_general x4, matrix products, contract_rows(): lax.dot_general(left_rows, right_rows, (((0,), (0,)), ((), ())), preferre...  8.09 us
    dot_general x2, matrix products, train_rows(): jnp.dot(active, interior_maps[layer_index], preferred_element_type=jnp.fl...  6.75 us
    convert_element_type x1, other arithmetic, local(): lax.psum(interior_grad_values.astype(jnp.bfloat16), 'tiles')  6.71 us
    unnamed x28, local copies, waits for them, and re-layouts  6.49 us
  transfers between devices with their start and end apart: 7, of which 3 were waited for; matrix products, arithmetic and copies ran while one was open for 12% of the time, Pallas kernels for 0%

commit v1 on v0

v1 whole, which is shorter than its diff:
```python
import math

import jax
import jax.numpy as jnp
from jax import lax
from jax.sharding import PartitionSpec as P

KAPPA = 0.2
LEVELS = 75
KEPT = 80
BF = jnp.bfloat16
F32 = jnp.float32


def contract_rows(left, right):
    return lax.dot_general(left, right, (((0,), (0,)), ((), ())), preferred_element_type=F32)


def times_transposed(left, right):
    return lax.dot_general(left, right, (((1,), (1,)), ((), ())), preferred_element_type=F32)


def silu_slope(pre):
    s = jax.nn.sigmoid(pre)
    return s * (1.0 + pre * (1.0 - s))


def add(a, b):
    return (a.astype(F32) + b.astype(F32)).astype(BF)


def swap(x, stride):
    n = lax.axis_size("tiles")
    return lax.ppermute(x, "tiles", [(t, t ^ stride) for t in range(n)])


def bit_of(stride):
    return (lax.axis_index("tiles") // stride) % 2


def halve(x, stride):
    bit = bit_of(stride)
    parts = x.reshape(2, x.shape[0] // 2, x.shape[1])
    mine = lax.dynamic_index_in_dim(parts, bit, 0, False)
    other = lax.dynamic_index_in_dim(parts, 1 - bit, 0, False)
    return add(mine, swap(other, stride))


def join(x, stride):
    bit = bit_of(stride)
    got = swap(x, stride)
    return jnp.concatenate([jnp.where(bit == 0, x, got), jnp.where(bit == 0, got, x)], 0)


def reduce_tiles(x):
    n = lax.axis_size("tiles")
    x = halve(x, 1)
    rows = x.shape[0] // 2
    a, b = x[:rows], x[rows:]
    a, b = halve(a, 2), halve(b, 4)
    a, b = halve(a, 4), halve(b, 2)
    m = jnp.concatenate([a, b], 0)
    stride = 8
    while stride < n:
        m = add(m, swap(m, stride))
        stride *= 2
    rows = a.shape[0]
    a, b = m[:rows], m[rows:]
    a, b = join(a, 4), join(b, 2)
    a, b = join(a, 2), join(b, 4)
    return join(jnp.concatenate([a, b], 0), 1)


def local(
    warmth,
    brine,
    flags,
    tally,
    assigned,
    desired,
    intercepts,
    leading,
    interior,
    readout,
):
    n = lax.axis_size("tiles")
    lon, lat, levels = warmth.shape
    cols = lon * lat
    hid = leading.shape[1]
    scale = 1.0 / math.sqrt(cols * n)

    up = [(i, (i + 1) % n) for i in range(n)]
    down = [(j, i) for i, j in up]
    depth = jnp.where(flags > 0, tally, 0)
    depth_plane = jnp.broadcast_to(depth[:, :, None].astype(F32), (lon, lat, levels))
    state = jnp.stack([warmth, brine, depth_plane])
    before = lax.ppermute(state[:, -1:], "tiles", up)
    after = lax.ppermute(state[:, :1], "tiles", down)
    bias = lax.all_to_all(
        jnp.broadcast_to(intercepts, (n, hid)), "tiles", split_axis=0, concat_axis=0, tiled=True
    )
    level = lax.broadcasted_iota(jnp.int32, (1, 1, 1, levels), 3).astype(F32)
    wide = jnp.concatenate([before, state, after], 1)
    wet = (level[0] < wide[2]).astype(F32)
    q = wide[:2]
    centre = q[:, 1:-1]
    wet_c = wet[1:-1]
    zrow = jnp.zeros((lon, 1, levels), F32)
    zq = jnp.zeros((2, lon, 1, levels), F32)
    total = wet[2:] * (q[:, 2:] - centre)
    total = total + wet[:-2] * (q[:, :-2] - centre)
    total = total + jnp.concatenate([wet_c[:, 1:], zrow], 1) * (
        jnp.concatenate([centre[:, :, 1:], zq], 2) - centre
    )
    total = total + jnp.concatenate([zrow, wet_c[:, :-1]], 1) * (
        jnp.concatenate([zq, centre[:, :, :-1]], 2) - centre
    )
    stepped = centre + KAPPA * wet_c * total

    wet_rows = wet_c.reshape(cols, levels)
    lane = lax.broadcasted_iota(jnp.int32, (cols, levels), 1)
    own = lane == assigned.reshape(cols, 1) + KEPT
    feats = [
        jnp.where(own, 1.0, stepped[i].reshape(cols, levels) * wet_rows).astype(BF)
        for i in range(2)
    ]
    features = jnp.concatenate(feats, 1)
    bias_hi = bias.astype(BF)
    bias_lo = (bias - bias_hi.astype(F32)).astype(BF)
    first = jnp.concatenate(
        [
            leading[:KEPT],
            bias_hi,
            leading[KEPT + n : levels + KEPT],
            bias_lo,
            leading[levels + KEPT + n :],
        ],
        0,
    )

    pres = [jnp.dot(features, first, preferred_element_type=F32)]
    acts = [jax.nn.silu(pres[0]).astype(BF)]
    deep = interior.shape[0]
    for i in range(deep):
        pres.append(jnp.dot(acts[-1], interior[i], preferred_element_type=F32))
        acts.append(jax.nn.silu(pres[-1]).astype(BF))
    output = jnp.dot(acts[-1], readout, preferred_element_type=F32)
    err = (
        (output - desired.reshape(cols, levels).astype(F32)) * wet_rows * scale
    ).astype(BF)
    readout_t = contract_rows(err, acts[-1]).astype(BF)[:KEPT]
    back = times_transposed(err, readout)
    grads = [None] * deep
    for i in reversed(range(deep)):
        delta = (back * silu_slope(pres[i + 1])).astype(BF)
        grads[i] = contract_rows(acts[i], delta).astype(BF)
        if i > 0:
            grads[i] = reduce_tiles(grads[i])
        back = times_transposed(delta, interior[i])
    delta = (back * silu_slope(pres[0])).astype(BF)
    lead = contract_rows(features, delta).astype(BF)
    split = KEPT + n
    pad = (-(split + 2 * KEPT)) % 256
    last = jnp.concatenate(
        [
            grads[0],
            lead[:split],
            lead[levels : levels + KEPT],
            readout_t,
            jnp.zeros((pad, hid), BF),
        ],
        0,
    )
    last = reduce_tiles(last)
    grads[0] = last[:hid]
    low, mid, high = hid + KEPT, hid + split, hid + split + KEPT
    zeros = jnp.zeros((levels - KEPT, hid), F32)
    lead_out = jnp.concatenate(
        [last[hid:low].astype(F32), zeros, last[mid:high].astype(F32), zeros], 0
    )
    readout_out = jnp.pad(
        last[high : high + KEPT].astype(F32).T, ((0, 0), (0, levels - KEPT))
    )
    intercept_out = lax.dynamic_slice_in_dim(
        last, low + lax.axis_index("tiles"), 1, 0
    ).astype(F32)
    return (
        stepped,
        output.astype(BF).reshape(lon, lat, levels),
        lead_out,
        jnp.stack([g.astype(F32) for g in grads]),
        readout_out,
        intercept_out,
    )


def solution(mesh):
    part = ("groups", "tiles")
    return jax.shard_map(
        local,
        mesh=mesh,
        in_specs=(
            P(part, None, None),
            P(part, None, None),
            P(part, None),
            P(part, None),
            P(part, None),
            P(part, None, None),
            P(part, None),
            P(),
            P(),
            P(),
        ),
        out_specs=(
            P(None, part, None, None),
            P(part, None, None),
            P("groups", None),
            P(None, "groups", None),
            P("groups", None),
            P(part, None),
        ),
        check_vma=False,
    )
```

time: 242 us -> 133 us (0.55)
  waiting for transfers between devices: 130 us -> 48.8 us
  between operations: 14.3 us -> 1.4 us
  matrix products: 27.4 us -> 18 us
  local copies, waits for them, and re-layouts: 21 us -> 12.5 us
  other arithmetic: 19.7 us -> 24 us
    psum x1 -> x0, waiting for transfers between devices: 106 us -> none  [local(): lax.psum(leading_grad_values.astype(jnp.bfloat16), 'tiles')]
    ppermute x2 -> x24, waiting for transfers between devices: 0.01 us -> 46.2 us  [the longest x22 46.2 us: swap(): return lax.ppermute(x, 'tiles', [(t, t ^ stride) for t in range(n)])]
    all_to_all x4 -> x1, waiting for transfers between devices: 24.8 us -> 2.62 us  [local(): lax.all_to_all(jnp.broadcast_to(intercepts, (n, hid)), 'tiles', split_axi...]
    all_to_all x4 -> x1, starting transfers between devices: 21.9 us -> 3.62 us  [local(): lax.all_to_all(jnp.broadcast_to(intercepts, (n, hid)), 'tiles', split_axi...]
    ppermute x2 -> x24, starting transfers between devices: 5.49 us -> 23.5 us  [the longest x22 18 us: swap(): return lax.ppermute(x, 'tiles', [(t, t ^ stride) for t in range(n)])]
    scatter x3 -> x0, local copies, waits for them, and re-layouts: 9.69 us -> none  [the longest x1 3.77 us: local(): jnp.zeros((slot_rows,), jnp.bfloat16).at[target_slot].set(depth_count)]
    dot_general x12 -> x10, matrix products: 27.4 us -> 18 us  [the longest x4 8.74 us: contract_rows(): lax.dot_general(left, right, (((0,), (0,)), ((), ())), preferred_element_...]
    convert_element_type x9 -> x17, other arithmetic: 12.4 us -> 6.02 us  [the longest x12 4.42 us: add(): return (a.astype(F32) + b.astype(F32)).astype(BF)]
  transfers between devices with their start and end apart: 7 -> 25, of which waited for: 3 -> 13; matrix products, arithmetic and copies ran while one was open for 12% -> 11% of each run, Pallas kernels for 0% -> 0%
where the time goes in v1:
time: 133 us; the launch traced here: 132 us
  waiting for transfers between devices  48.8 us (37%)
  starting transfers between devices  27.2 us (20%)
  other arithmetic  24 us (18%)
  matrix products  18 us (14%)
  local copies, waits for them, and re-layouts  12.5 us (9%)
  between operations  1.4 us (1%)
    ppermute x22, waiting for transfers between devices, swap(): return lax.ppermute(x, 'tiles', [(t, t ^ stride) for t in range(n)])  46.2 us
    ppermute x22, starting transfers between devices, swap(): return lax.ppermute(x, 'tiles', [(t, t ^ stride) for t in range(n)])  18 us
    dot_general x4, matrix products, contract_rows(): lax.dot_general(left, right, (((0,), (0,)), ((), ())), preferred_element_...  8.74 us
    unnamed x44, local copies, waits for them, and re-layouts  8.15 us
    dot_general x2, matrix products, local(): pres.append(jnp.dot(acts[-1], interior[i], preferred_element_type=F32))  5.26 us
    another operation x2, other arithmetic, local(): jnp.stack([g.astype(F32) for g in grads])  5.22 us
    ppermute x1, starting transfers between devices, local(): after = lax.ppermute(state[:, :1], 'tiles', down)  5.06 us
    convert_element_type x12, other arithmetic, add(): return (a.astype(F32) + b.astype(F32)).astype(BF)  4.42 us
  transfers between devices with their start and end apart: 25, of which 13 were waited for; matrix products, arithmetic and copies ran while one was open for 11% of the time, Pallas kernels for 0%

profile of v1, /device:TPU:0, one launch (start us, length us, event | category | flops | bytes accessed | tf_op | source)
XLA Modules:
  0.0 131.9 jit_solution(4676289891892826743)
XLA Ops:
  2.9 5.1 %collective-permute-start.1 = (f32[3,1,32,128]{3,2,1,0:T(8,128)S(1)}, f32[3,1,32,128]{3,2,1,0:T(8,128)S(1)}, u32[]{:S(2)}, u32[]{:S(2)}) collective-permute-start(f32[3,1,32,128]{3,2,1,0:T(8,128)S(1)} %get-tuple-element.29), channel_id=1, source_target_pairs={{1,0},{2,1},{3,2},{4,3},{5,4},{6,5},{7,6},{8,7},{9,8},{10,9},{11,1... | collective-permute-start | bytes 147464 | tf_op jit(solution)/shard_map/ppermute | solution.py:98
  8.0 1.3 %broadcast_in_dim.11 = f32[16,1,1024]{2,1,0:T(1,128)} broadcast(f32[1024]{0:T(1024)} %bitcast.166), dimensions={2} | broadcast | bytes 69632 | tf_op jit(solution)/shard_map/broadcast_in_dim | solution.py:100
  9.3 3.6 %all-to-all-start = ((f32[16,1,1024]{2,1,0:T(1,128)}), f32[16,1,1024]{2,1,0:T(1,128)S(1)}, u32[]{:S(2)}, u32[]{:S(2)}) async-start(f32[16,1,1024]{2,1,0:T(1,128)} %broadcast_in_dim.11), calls=%async_computation | async-start | bytes 131072 | tf_op jit(solution)/shard_map/all_to_all | solution.py:99
  17.2 2.6 %all-to-all-done = f32[16,1,1024]{2,1,0:T(1,128)S(1)} async-done(((f32[16,1,1024]{2,1,0:T(1,128)}), f32[16,1,1024]{2,1,0:T(1,128)S(1)}, u32[]{:S(2)}, u32[]{:S(2)}) %all-to-all-start) | async-done | bytes 65568 | tf_op jit(solution)/shard_map/all_to_all | solution.py:99
  20.4 3.7 %fusion.10 = f32[512,1024]{1,0:T(8,128)S(1)} fusion(bf16[2,1024,1024]{2,1,0:T(8,128)(2,1)} %param.18, f32[512,1024]{1,0:T(8,128)S(1)} %fusion.55), kind=kOutput, calls=%fused_computation.18 | convolution fusion | flops 1076363264 | bytes 6291456 | tf_op jit(solution)/shard_map/dot_general | solution.py:145
  24.1 1.6 %multiply_convert_fusion.3 = (bf16[512,1024]{1,0:T(8,128)(2,1)S(1)}, f32[512,1024]{1,0:T(8,128)S(1)}) fusion(bf16[2,1024,1024]{2,1,0:T(8,128)(2,1)S(1)} %copy-done.16, f32[512,1024]{1,0:T(8,128)S(1)} %fusion.10), kind=kOutput, calls=%fused_computation.23 | convolution fusion | flops 1078984704 | bytes 7340032 | tf_op jit(solution)/shard_map/dot_general | solution.py:145
  27.7 1.6 %multiply_convert_fusion.1 = bf16[512,1024]{1,0:T(8,128)(2,1)S(1)} fusion(f32[512,1024]{1,0:T(8,128)S(1)} %fusion.10, bf16[512,1024]{1,0:T(8,128)(2,1)S(1)} %multiply_convert_fusion.2, bf16[2,1024,1024]{2,1,0:T(8,128)(2,1)S(1)} %copy-done.16), kind=kOutput, calls=%fused_computation.21 | convolution fusion | flops 1078460416 | bytes 6291456 | tf_op jit(solution)/shard_map/dot_general | solution.py:20
  30.3 2.7 %convolution_convert_fusion.1 = bf16[1024,1024]{1,0:T(8,128)(2,1)} fusion(bf16[512,1024]{1,0:T(8,128)(2,1)S(1)} %multiply_convert_fusion.1, f32[512,1024]{1,0:T(8,128)S(1)} %fusion.55), kind=kOutput, calls=%fused_computation.30 | convolution fusion | flops 1077411840 | bytes 5242880 | tf_op jit(solution)/shard_map/dot_general | solution.py:16
  33.0 4.4 %convolution_convert_fusion.2 = bf16[256,1024]{1,0:T(8,128)(2,1)S(1)} fusion(f32[512,1024]{1,0:T(8,128)} %copy-done.7, bf16[512,1024]{1,0:T(8,128)(2,1)} %copy-done.19, bf16[2,1024,1024]{2,1,0:T(8,128)(2,1)} %param.18, bf16[512,128]{1,0:T(8,128)(2,1)S(1)} %get-tuple-element.62, bf16[512,128]{1,0:T(8,128)(2,1)S(1)} %get-tuple-element.61), kind=kOutput, calls=%fused_computation.39 | convolution fusion | flops 1347682304 | bytes 6029312 | tf_op jit(solution)/shard_map/dot_general | solution.py:16
  37.8 1.4 %copy-done.18 = f32[512,1024]{1,0:T(8,128)S(1)} copy-done((f32[512,1024]{1,0:T(8,128)S(1)}, f32[512,1024]{1,0:T(8,128)}, u32[]{:S(2)}) %copy-start.18) | copy-done | bytes 2097176
  39.2 1.3 %convolution_convert_fusion = bf16[1024,1024]{1,0:T(8,128)(2,1)S(1)} fusion(bf16[512,1024]{1,0:T(8,128)(2,1)S(1)} %multiply_convert_fusion.2, f32[512,1024]{1,0:T(8,128)S(1)} %copy-done.18), kind=kOutput, calls=%fused_computation.29 | convolution fusion | flops 1077411840 | bytes 5242880 | tf_op jit(solution)/shard_map/dot_general | solution.py:16
  45.2 1.9 %fusion.3 = bf16[512,1024]{1,0:T(8,128)(2,1)S(1)} fusion(bf16[512,1024]{1,0:T(8,128)(2,1)} %collective-permute-done.13, bf16[2,512,1024]{2,1,0:T(8,128)(2,1)} %bitcast.152, s32[]{:T(128)S(6)} %select_n.249), kind=kLoop, calls=%fused_computation.11 | loop fusion | flops 2097152 | bytes 3145732 | tf_op jit(solution)/shard_map/convert_element_type | solution.py:29
  48.4 1.8 %fusion = bf16[640,1024]{1,0:T(8,128)(2,1)S(1)} fusion(bf16[640,1024]{1,0:T(8,128)(2,1)} %collective-permute-done.2, bf16[2,640,1024]{2,1,0:T(8,128)(2,1)S(1)} %bitcast.138, s32[]{:T(128)S(6)} %select_n.249), kind=kLoop, calls=%fused_computation.7 | loop fusion | flops 2621440 | bytes 3932164 | tf_op jit(solution)/shard_map/convert_element_type | solution.py:29
  51.7 2.0 %collective-permute-start.5 = (bf16[160,1024]{1,0:T(8,128)(2,1)S(1)}, bf16[160,1024]{1,0:T(8,128)(2,1)S(1)}, u32[]{:S(2)}, u32[]{:S(2)}) collective-permute-start(bf16[160,1024]{1,0:T(8,128)(2,1)S(1)} %dynamic-slice_bitcast_fusion.2), channel_id=1, source_target_pairs={{0,4},{1,5},{2,6},{3,7},{4,0},{5,1},{6,2},{7,3},{8,12},{9,13},{10,... | collective-permute-start | bytes 983048 | tf_op jit(solution)/shard_map/ppermute | solution.py:34
  53.6 2.8 %collective-permute-done.14 = bf16[128,1024]{1,0:T(8,128)(2,1)S(1)} collective-permute-done((bf16[128,1024]{1,0:T(8,128)(2,1)S(1)}, bf16[128,1024]{1,0:T(8,128)(2,1)S(1)}, u32[]{:S(2)}, u32[]{:S(2)}) %collective-permute-start.14) | collective-permute-done | bytes 262176 | tf_op jit(solution)/shard_map/ppermute | solution.py:34
  56.9 1.9 %collective-permute-start.17 = (bf16[64,1024]{1,0:T(8,128)(2,1)S(1)}, bf16[64,1024]{1,0:T(8,128)(2,1)S(1)}, u32[]{:S(2)}, u32[]{:S(2)}) collective-permute-start(bf16[64,1024]{1,0:T(8,128)(2,1)S(1)} %dynamic-slice_bitcast_fusion.8), channel_id=1, source_target_pairs={{0,2},{1,3},{2,0},{3,1},{4,6},{5,7},{6,4},{7,5},{8,10},{9,11},{10,... | collective-permute-start | bytes 393224 | tf_op jit(solution)/shard_map/ppermute | solution.py:34
  58.8 7.0 %collective-permute-done.15 = bf16[64,1024]{1,0:T(8,128)(2,1)S(1)} collective-permute-done((bf16[64,1024]{1,0:T(8,128)(2,1)S(1)}, bf16[64,1024]{1,0:T(8,128)(2,1)S(1)}, u32[]{:S(2)}, u32[]{:S(2)}) %collective-permute-start.15) | collective-permute-done | bytes 131104 | tf_op jit(solution)/shard_map/ppermute | solution.py:34
  65.9 1.4 %collective-permute-start.18 = (bf16[128,1024]{1,0:T(8,128)(2,1)S(1)}, bf16[128,1024]{1,0:T(8,128)(2,1)S(1)}, u32[]{:S(2)}, u32[]{:S(2)}) collective-permute-start(bf16[128,1024]{1,0:T(8,128)(2,1)S(1)} %pad_maximum_fusion.19), channel_id=1, source_target_pairs={{0,8},{1,9},{2,10},{3,11},{4,12},{5,13},{6,14},{7,15},{8,0},{9,1},... | collective-permute-start | bytes 786440 | tf_op jit(solution)/shard_map/ppermute | solution.py:34
  67.5 1.5 %collective-permute-start.4 = (bf16[80,1024]{1,0:T(8,128)(2,1)S(1)}, bf16[80,1024]{1,0:T(8,128)(2,1)S(1)}, u32[]{:S(2)}, u32[]{:S(2)}) collective-permute-start(bf16[80,1024]{1,0:T(8,128)(2,1)S(1)} %dynamic-slice_bitcast_fusion.7), channel_id=1, source_target_pairs={{0,4},{1,5},{2,6},{3,7},{4,0},{5,1},{6,2},{7,3},{8,12},{9,13},{10,... | collective-permute-start | bytes 491528 | tf_op jit(solution)/shard_map/ppermute | solution.py:34
  69.8 10.1 %collective-permute-done.18 = bf16[128,1024]{1,0:T(8,128)(2,1)S(1)} collective-permute-done((bf16[128,1024]{1,0:T(8,128)(2,1)S(1)}, bf16[128,1024]{1,0:T(8,128)(2,1)S(1)}, u32[]{:S(2)}, u32[]{:S(2)}) %collective-permute-start.18) | collective-permute-done | bytes 262176 | tf_op jit(solution)/shard_map/ppermute | solution.py:34
  80.0 1.6 %collective-permute-start.21 = (bf16[64,1024]{1,0:T(8,128)(2,1)S(1)}, bf16[64,1024]{1,0:T(8,128)(2,1)S(1)}, u32[]{:S(2)}, u32[]{:S(2)}) collective-permute-start(bf16[64,1024]{1,0:T(8,128)(2,1)S(1)} %get-tuple-element.66), channel_id=1, source_target_pairs={{0,2},{1,3},{2,0},{3,1},{4,6},{5,7},{6,4},{7,5},{8,10},{9,11},{10,... | collective-permute-start | bytes 393224 | tf_op jit(solution)/shard_map/ppermute | solution.py:34
  81.8 1.8 %collective-permute-start.7 = (bf16[160,1024]{1,0:T(8,128)(2,1)S(1)}, bf16[160,1024]{1,0:T(8,128)(2,1)S(1)}, u32[]{:S(2)}, u32[]{:S(2)}) collective-permute-start(bf16[160,1024]{1,0:T(8,128)(2,1)S(1)} %pad_maximum_fusion.11), channel_id=1, source_target_pairs={{0,8},{1,9},{2,10},{3,11},{4,12},{5,13},{6,14},{7,15},{8,0},{9,1},... | collective-permute-start | bytes 983048 | tf_op jit(solution)/shard_map/ppermute | solution.py:34
  83.6 3.0 %collective-permute-done.19 = bf16[64,1024]{1,0:T(8,128)(2,1)S(1)} collective-permute-done((bf16[64,1024]{1,0:T(8,128)(2,1)S(1)}, bf16[64,1024]{1,0:T(8,128)(2,1)S(1)}, u32[]{:S(2)}, u32[]{:S(2)}) %collective-permute-start.19) | collective-permute-done | bytes 131104 | tf_op jit(solution)/shard_map/ppermute | solution.py:34
  86.7 1.6 %collective-permute-start.20 = (bf16[128,1024]{1,0:T(8,128)(2,1)S(1)}, bf16[128,1024]{1,0:T(8,128)(2,1)S(1)}, u32[]{:S(2)}, u32[]{:S(2)}) collective-permute-start(bf16[128,1024]{1,0:T(8,128)(2,1)S(1)} %pad_maximum_fusion.20), channel_id=1, source_target_pairs={{0,2},{1,3},{2,0},{3,1},{4,6},{5,7},{6,4},{7,5},{8,10},{9,11},{10,... | collective-permute-start | bytes 786440 | tf_op jit(solution)/shard_map/ppermute | solution.py:34
  89.0 10.3 %collective-permute-done.7 = bf16[160,1024]{1,0:T(8,128)(2,1)S(1)} collective-permute-done((bf16[160,1024]{1,0:T(8,128)(2,1)S(1)}, bf16[160,1024]{1,0:T(8,128)(2,1)S(1)}, u32[]{:S(2)}, u32[]{:S(2)}) %collective-permute-start.7) | collective-permute-done | bytes 327712 | tf_op jit(solution)/shard_map/ppermute | solution.py:34
  100.1 4.7 %collective-permute-done.10 = bf16[80,1024]{1,0:T(8,128)(2,1)S(1)} collective-permute-done((bf16[80,1024]{1,0:T(8,128)(2,1)S(1)}, bf16[80,1024]{1,0:T(8,128)(2,1)S(1)}, u32[]{:S(2)}, u32[]{:S(2)}) %collective-permute-start.10) | collective-permute-done | bytes 163872 | tf_op jit(solution)/shard_map/ppermute | solution.py:34
  105.4 1.6 %collective-permute-start.9 = (bf16[160,1024]{1,0:T(8,128)(2,1)S(1)}, bf16[160,1024]{1,0:T(8,128)(2,1)S(1)}, u32[]{:S(2)}, u32[]{:S(2)}) collective-permute-start(bf16[160,1024]{1,0:T(8,128)(2,1)S(1)} %pad_maximum_fusion.12), channel_id=1, source_target_pairs={{0,2},{1,3},{2,0},{3,1},{4,6},{5,7},{6,4},{7,5},{8,10},{9,11},{10,... | collective-permute-start | bytes 983048 | tf_op jit(solution)/shard_map/ppermute | solution.py:34
  107.4 5.6 %collective-permute-done.9 = bf16[160,1024]{1,0:T(8,128)(2,1)S(1)} collective-permute-done((bf16[160,1024]{1,0:T(8,128)(2,1)S(1)}, bf16[160,1024]{1,0:T(8,128)(2,1)S(1)}, u32[]{:S(2)}, u32[]{:S(2)}) %collective-permute-start.9) | collective-permute-done | bytes 327712 | tf_op jit(solution)/shard_map/ppermute | solution.py:34
  115.6 2.8 %select_bitcast_fusion.1 = (bf16[1,512,1024]{2,1,0:T(8,128)(2,1)S(1)}, bf16[1,512,1024]{2,1,0:T(8,128)(2,1)}) fusion(bf16[512,1024]{1,0:T(8,128)(2,1)} %collective-permute-done.23, pred[]{:T(512)S(6)} %eq.57, bf16[128,1024]{1,0:T(8,128)(2,1)S(1)} %get-tuple-element.38, bf16[128,1024]{1,0:T(8,128)(2,1)S(1)} %get-tuple-element.37, ...), kind=kLoop, calls=%fused_computation.43 | loop fusion | flops 5242880 | bytes 4194305 | tf_op jit(solution)/shard_map/concatenate | solution.py:52
  119.0 2.1 %broadcast_select_fusion = (bf16[640,1024]{1,0:T(8,128)(2,1)S(1)}, bf16[640,1024]{1,0:T(8,128)(2,1)S(1)}) fusion(bf16[640,1024]{1,0:T(8,128)(2,1)} %collective-permute-done.12, pred[]{:T(512)S(6)} %eq.57, bf16[160,1024]{1,0:T(8,128)(2,1)S(1)} %get-tuple-element.34, bf16[160,1024]{1,0:T(8,128)(2,1)S(1)} %get-tuple-element.33, ...), kind=kLoop, calls=%fused_computation.37 | loop fusion | flops 6553600 | bytes 5242881 | tf_op jit(solution)/shard_map/jit(_where)/select_n | solution.py:52
  123.6 2.0 %copy.17 = f32[1024,128]{1,0:T(8,128)} copy(f32[1024,128]{0,1:T(8,128)} %pad_convert_fusion) | data formatting | bytes 1048576
  125.7 5.0 %maximum_convert_fusion = f32[2,1024,1024]{2,1,0:T(8,128)} fusion(bf16[1,512,1024]{2,1,0:T(8,128)(2,1)} %get-tuple-element.21, bf16[1,512,1024]{2,1,0:T(8,128)(2,1)S(1)} %get-tuple-element.20, bf16[1,1024,1024]{2,1,0:T(8,128)(2,1)S(1)} %fusion.2), kind=kLoop, calls=%fused_computation | loop fusion | flops 12582912 | bytes 12582912 | tf_op jit(solution)/shard_map/stack | solution.py:191
  (144 shorter events, 28.3 us)
Async XLA Ops:
  0.6 25.1 %copy-start = (bf16[1024,128]{1,0:T(8,128)(2,1)S(1)}, bf16[1024,128]{1,0:T(8,128)(2,1)}, u32[]{:S(2)}) copy-start(bf16[1024,128]{1,0:T(8,128)(2,1)} %param.19) | copy-start | bytes 786436
  0.7 14.4 %copy-start.3 = (f32[16,32,128]{2,1,0:T(8,128)S(1)}, f32[16,32,128]{2,1,0:T(8,128)}, u32[]{:S(2)}) copy-start(f32[16,32,128]{2,1,0:T(8,128)} %param.10) | copy-start | bytes 786436
  0.7 14.4 %copy-start.2 = (f32[16,32,128]{2,1,0:T(8,128)S(1)}, f32[16,32,128]{2,1,0:T(8,128)}, u32[]{:S(2)}) copy-start(f32[16,32,128]{2,1,0:T(8,128)} %param.11) | copy-start | bytes 786436
  0.7 13.6 %copy-start.15 = (s32[16,32]{1,0:T(8,128)S(1)}, s32[16,32]{1,0:T(8,128)}, u32[]{:S(2)}) copy-start(s32[16,32]{1,0:T(8,128)} %param.14) | copy-start | bytes 6148
  0.7 13.6 %copy-start.11 = (bf16[256,1024]{1,0:T(8,128)(2,1)S(1)}, bf16[256,1024]{1,0:T(8,128)(2,1)}, u32[]{:S(2)}) copy-start(bf16[256,1024]{1,0:T(8,128)(2,1)} %param.17) | copy-start | bytes 1572868
  2.4 12.0 %collective-permute-start = (f32[3,1,32,128]{3,2,1,0:T(8,128)S(1)}, f32[3,1,32,128]{3,2,1,0:T(8,128)S(1)}, u32[]{:S(2)}, u32[]{:S(2)}) collective-permute-start(f32[3,1,32,128]{3,2,1,0:T(8,128)S(1)} %get-tuple-element.30), channel_id=1, source_target_pairs={{0,1},{1,2},{2,3},{3,4},{4,5},{5,6},{6,7},{7,8},{8,9},{9,10},{10,1... | collective-permute-start | bytes 147464 | tf_op jit(solution)/shard_map/ppermute | solution.py:97
  2.9 11.5 %collective-permute-start.1 = (f32[3,1,32,128]{3,2,1,0:T(8,128)S(1)}, f32[3,1,32,128]{3,2,1,0:T(8,128)S(1)}, u32[]{:S(2)}, u32[]{:S(2)}) collective-permute-start(f32[3,1,32,128]{3,2,1,0:T(8,128)S(1)} %get-tuple-element.29), channel_id=1, source_target_pairs={{1,0},{2,1},{3,2},{4,3},{5,4},{6,5},{7,6},{8,7},{9,8},{10,9},{11,1... | collective-permute-start | bytes 147464 | tf_op jit(solution)/shard_map/ppermute | solution.py:98
  9.3 10.5 %all-to-all-start = ((f32[16,1,1024]{2,1,0:T(1,128)}), f32[16,1,1024]{2,1,0:T(1,128)S(1)}, u32[]{:S(2)}, u32[]{:S(2)}) async-start(f32[16,1,1024]{2,1,0:T(1,128)} %broadcast_in_dim.11), calls=%async_computation | async-start | bytes 131072 | tf_op jit(solution)/shard_map/all_to_all | solution.py:99
  20.4 9.0 %copy-start.7 = (f32[512,1024]{1,0:T(8,128)}, f32[512,1024]{1,0:T(8,128)S(1)}, u32[]{:S(2)}) copy-start(f32[512,1024]{1,0:T(8,128)S(1)} %fusion.55) | copy-start | bytes 6291460
  42.2 3.0 %collective-permute-start.13 = (bf16[512,1024]{1,0:T(8,128)(2,1)}, bf16[512,1024]{1,0:T(8,128)(2,1)}, u32[]{:S(2)}, u32[]{:S(2)}) collective-permute-start(bf16[512,1024]{1,0:T(8,128)(2,1)} %dynamic-slice_bitcast_fusion.1), channel_id=1, source_target_pairs={{0,1},{1,0},{2,3},{3,2},{4,5},{5,4},{6,7},{7,6},{8,9},{9,8},{10,11... | collective-permute-start | bytes 3145736 | tf_op jit(solution)/shard_map/ppermute | solution.py:34
  45.0 3.4 %collective-permute-start.2 = (bf16[640,1024]{1,0:T(8,128)(2,1)}, bf16[640,1024]{1,0:T(8,128)(2,1)}, u32[]{:S(2)}, u32[]{:S(2)}) collective-permute-start(bf16[640,1024]{1,0:T(8,128)(2,1)} %dynamic-slice_bitcast_fusion), channel_id=1, source_target_pairs={{0,1},{1,0},{2,3},{3,2},{4,5},{5,4},{6,7},{7,6},{8,9},{9,8},{10,11... | collective-permute-start | bytes 3932168 | tf_op jit(solution)/shard_map/ppermute | solution.py:34
  47.3 9.2 %collective-permute-start.14 = (bf16[128,1024]{1,0:T(8,128)(2,1)S(1)}, bf16[128,1024]{1,0:T(8,128)(2,1)S(1)}, u32[]{:S(2)}, u32[]{:S(2)}) collective-permute-start(bf16[128,1024]{1,0:T(8,128)(2,1)S(1)} %dynamic-slice_bitcast_fusion.5), channel_id=1, source_target_pairs={{0,2},{1,3},{2,0},{3,1},{4,6},{5,7},{6,4},{7,5},{8,10},{9,11},{10,... | collective-permute-start | bytes 786440 | tf_op jit(solution)/shard_map/ppermute | solution.py:34
  47.5 9.3 %collective-permute-start.16 = (bf16[128,1024]{1,0:T(8,128)(2,1)S(1)}, bf16[128,1024]{1,0:T(8,128)(2,1)S(1)}, u32[]{:S(2)}, u32[]{:S(2)}) collective-permute-start(bf16[128,1024]{1,0:T(8,128)(2,1)S(1)} %dynamic-slice_bitcast_fusion.4), channel_id=1, source_target_pairs={{0,4},{1,5},{2,6},{3,7},{4,0},{5,1},{6,2},{7,3},{8,12},{9,13},{10,... | collective-permute-start | bytes 786440 | tf_op jit(solution)/shard_map/ppermute | solution.py:34
  50.3 17.0 %collective-permute-start.3 = (bf16[160,1024]{1,0:T(8,128)(2,1)S(1)}, bf16[160,1024]{1,0:T(8,128)(2,1)S(1)}, u32[]{:S(2)}, u32[]{:S(2)}) collective-permute-start(bf16[160,1024]{1,0:T(8,128)(2,1)S(1)} %dynamic-slice_bitcast_fusion.3), channel_id=1, source_target_pairs={{0,2},{1,3},{2,0},{3,1},{4,6},{5,7},{6,4},{7,5},{8,10},{9,11},{10,... | collective-permute-start | bytes 983048 | tf_op jit(solution)/shard_map/ppermute | solution.py:34
  51.7 17.3 %collective-permute-start.5 = (bf16[160,1024]{1,0:T(8,128)(2,1)S(1)}, bf16[160,1024]{1,0:T(8,128)(2,1)S(1)}, u32[]{:S(2)}, u32[]{:S(2)}) collective-permute-start(bf16[160,1024]{1,0:T(8,128)(2,1)S(1)} %dynamic-slice_bitcast_fusion.2), channel_id=1, source_target_pairs={{0,4},{1,5},{2,6},{3,7},{4,0},{5,1},{6,2},{7,3},{8,12},{9,13},{10,... | collective-permute-start | bytes 983048 | tf_op jit(solution)/shard_map/ppermute | solution.py:34
  56.6 9.2 %collective-permute-start.15 = (bf16[64,1024]{1,0:T(8,128)(2,1)S(1)}, bf16[64,1024]{1,0:T(8,128)(2,1)S(1)}, u32[]{:S(2)}, u32[]{:S(2)}) collective-permute-start(bf16[64,1024]{1,0:T(8,128)(2,1)S(1)} %dynamic-slice_bitcast_fusion.9), channel_id=1, source_target_pairs={{0,4},{1,5},{2,6},{3,7},{4,0},{5,1},{6,2},{7,3},{8,12},{9,13},{10,... | collective-permute-start | bytes 393224 | tf_op jit(solution)/shard_map/ppermute | solution.py:34
  56.9 8.9 %collective-permute-start.17 = (bf16[64,1024]{1,0:T(8,128)(2,1)S(1)}, bf16[64,1024]{1,0:T(8,128)(2,1)S(1)}, u32[]{:S(2)}, u32[]{:S(2)}) collective-permute-start(bf16[64,1024]{1,0:T(8,128)(2,1)S(1)} %dynamic-slice_bitcast_fusion.8), channel_id=1, source_target_pairs={{0,2},{1,3},{2,0},{3,1},{4,6},{5,7},{6,4},{7,5},{8,10},{9,11},{10,... | collective-permute-start | bytes 393224 | tf_op jit(solution)/shard_map/ppermute | solution.py:34
  65.9 14.0 %collective-permute-start.18 = (bf16[128,1024]{1,0:T(8,128)(2,1)S(1)}, bf16[128,1024]{1,0:T(8,128)(2,1)S(1)}, u32[]{:S(2)}, u32[]{:S(2)}) collective-permute-start(bf16[128,1024]{1,0:T(8,128)(2,1)S(1)} %pad_maximum_fusion.19), channel_id=1, source_target_pairs={{0,8},{1,9},{2,10},{3,11},{4,12},{5,13},{6,14},{7,15},{8,0},{9,1},... | collective-permute-start | bytes 786440 | tf_op jit(solution)/shard_map/ppermute | solution.py:34
  67.5 14.2 %collective-permute-start.4 = (bf16[80,1024]{1,0:T(8,128)(2,1)S(1)}, bf16[80,1024]{1,0:T(8,128)(2,1)S(1)}, u32[]{:S(2)}, u32[]{:S(2)}) collective-permute-start(bf16[80,1024]{1,0:T(8,128)(2,1)S(1)} %dynamic-slice_bitcast_fusion.7), channel_id=1, source_target_pairs={{0,4},{1,5},{2,6},{3,7},{4,0},{5,1},{6,2},{7,3},{8,12},{9,13},{10,... | collective-permute-start | bytes 491528 | tf_op jit(solution)/shard_map/ppermute | solution.py:34
  69.1 12.6 %collective-permute-start.6 = (bf16[80,1024]{1,0:T(8,128)(2,1)S(1)}, bf16[80,1024]{1,0:T(8,128)(2,1)S(1)}, u32[]{:S(2)}, u32[]{:S(2)}) collective-permute-start(bf16[80,1024]{1,0:T(8,128)(2,1)S(1)} %dynamic-slice_bitcast_fusion.6), channel_id=1, source_target_pairs={{0,2},{1,3},{2,0},{3,1},{4,6},{5,7},{6,4},{7,5},{8,10},{9,11},{10,... | collective-permute-start | bytes 491528 | tf_op jit(solution)/shard_map/ppermute | solution.py:34
  80.0 6.6 %collective-permute-start.19 = (bf16[64,1024]{1,0:T(8,128)(2,1)S(1)}, bf16[64,1024]{1,0:T(8,128)(2,1)S(1)}, u32[]{:S(2)}, u32[]{:S(2)}) collective-permute-start(bf16[64,1024]{1,0:T(8,128)(2,1)S(1)} %get-tuple-element.65), channel_id=1, source_target_pairs={{0,4},{1,5},{2,6},{3,7},{4,0},{5,1},{6,2},{7,3},{8,12},{9,13},{10,... | collective-permute-start | bytes 393224 | tf_op jit(solution)/shard_map/ppermute | solution.py:34
  80.0 6.6 %collective-permute-start.21 = (bf16[64,1024]{1,0:T(8,128)(2,1)S(1)}, bf16[64,1024]{1,0:T(8,128)(2,1)S(1)}, u32[]{:S(2)}, u32[]{:S(2)}) collective-permute-start(bf16[64,1024]{1,0:T(8,128)(2,1)S(1)} %get-tuple-element.66), channel_id=1, source_target_pairs={{0,2},{1,3},{2,0},{3,1},{4,6},{5,7},{6,4},{7,5},{8,10},{9,11},{10,... | collective-permute-start | bytes 393224 | tf_op jit(solution)/shard_map/ppermute | solution.py:34
  81.8 17.5 %collective-permute-start.7 = (bf16[160,1024]{1,0:T(8,128)(2,1)S(1)}, bf16[160,1024]{1,0:T(8,128)(2,1)S(1)}, u32[]{:S(2)}, u32[]{:S(2)}) collective-permute-start(bf16[160,1024]{1,0:T(8,128)(2,1)S(1)} %pad_maximum_fusion.11), channel_id=1, source_target_pairs={{0,8},{1,9},{2,10},{3,11},{4,12},{5,13},{6,14},{7,15},{8,0},{9,1},... | collective-permute-start | bytes 983048 | tf_op jit(solution)/shard_map/ppermute | solution.py:34
  86.7 13.3 %collective-permute-start.20 = (bf16[128,1024]{1,0:T(8,128)(2,1)S(1)}, bf16[128,1024]{1,0:T(8,128)(2,1)S(1)}, u32[]{:S(2)}, u32[]{:S(2)}) collective-permute-start(bf16[128,1024]{1,0:T(8,128)(2,1)S(1)} %pad_maximum_fusion.20), channel_id=1, source_target_pairs={{0,2},{1,3},{2,0},{3,1},{4,6},{5,7},{6,4},{7,5},{8,10},{9,11},{10,... | collective-permute-start | bytes 786440 | tf_op jit(solution)/shard_map/ppermute | solution.py:34
  88.3 18.7 %collective-permute-start.22 = (bf16[128,1024]{1,0:T(8,128)(2,1)S(1)}, bf16[128,1024]{1,0:T(8,128)(2,1)S(1)}, u32[]{:S(2)}, u32[]{:S(2)}) collective-permute-start(bf16[128,1024]{1,0:T(8,128)(2,1)S(1)} %pad_maximum_fusion.21), channel_id=1, source_target_pairs={{0,4},{1,5},{2,6},{3,7},{4,0},{5,1},{6,2},{7,3},{8,12},{9,13},{10,... | collective-permute-start | bytes 786440 | tf_op jit(solution)/shard_map/ppermute | solution.py:34
  99.4 5.4 %collective-permute-start.10 = (bf16[80,1024]{1,0:T(8,128)(2,1)S(1)}, bf16[80,1024]{1,0:T(8,128)(2,1)S(1)}, u32[]{:S(2)}, u32[]{:S(2)}) collective-permute-start(bf16[80,1024]{1,0:T(8,128)(2,1)S(1)} %get-tuple-element.54), channel_id=1, source_target_pairs={{0,2},{1,3},{2,0},{3,1},{4,6},{5,7},{6,4},{7,5},{8,10},{9,11},{10,... | collective-permute-start | bytes 491528 | tf_op jit(solution)/shard_map/ppermute | solution.py:34
  100.0 5.3 %collective-permute-start.8 = (bf16[80,1024]{1,0:T(8,128)(2,1)S(1)}, bf16[80,1024]{1,0:T(8,128)(2,1)S(1)}, u32[]{:S(2)}, u32[]{:S(2)}) collective-permute-start(bf16[80,1024]{1,0:T(8,128)(2,1)S(1)} %get-tuple-element.53), channel_id=1, source_target_pairs={{0,4},{1,5},{2,6},{3,7},{4,0},{5,1},{6,2},{7,3},{8,12},{9,13},{10,... | collective-permute-start | bytes 491528 | tf_op jit(solution)/shard_map/ppermute | solution.py:34
  105.4 7.6 %collective-permute-start.9 = (bf16[160,1024]{1,0:T(8,128)(2,1)S(1)}, bf16[160,1024]{1,0:T(8,128)(2,1)S(1)}, u32[]{:S(2)}, u32[]{:S(2)}) collective-permute-start(bf16[160,1024]{1,0:T(8,128)(2,1)S(1)} %pad_maximum_fusion.12), channel_id=1, source_target_pairs={{0,2},{1,3},{2,0},{3,1},{4,6},{5,7},{6,4},{7,5},{8,10},{9,11},{10,... | collective-permute-start | bytes 983048 | tf_op jit(solution)/shard_map/ppermute | solution.py:34
  107.2 7.1 %collective-permute-start.11 = (bf16[160,1024]{1,0:T(8,128)(2,1)S(1)}, bf16[160,1024]{1,0:T(8,128)(2,1)S(1)}, u32[]{:S(2)}, u32[]{:S(2)}) collective-permute-start(bf16[160,1024]{1,0:T(8,128)(2,1)S(1)} %pad_maximum_fusion.13), channel_id=1, source_target_pairs={{0,4},{1,5},{2,6},{3,7},{4,0},{5,1},{6,2},{7,3},{8,12},{9,13},{10,... | collective-permute-start | bytes 983048 | tf_op jit(solution)/shard_map/ppermute | solution.py:34
  107.3 8.3 %collective-permute-start.23 = (bf16[512,1024]{1,0:T(8,128)(2,1)S(1)}, bf16[512,1024]{1,0:T(8,128)(2,1)}, u32[]{:S(2)}, u32[]{:S(2)}) collective-permute-start(bf16[512,1024]{1,0:T(8,128)(2,1)S(1)} %pad_maximum_fusion.3), channel_id=1, source_target_pairs={{0,1},{1,0},{2,3},{3,2},{4,5},{5,4},{6,7},{7,6},{8,9},{9,8},{10,11... | collective-permute-start | bytes 3145736 | tf_op jit(solution)/shard_map/ppermute | solution.py:34
  115.6 3.4 %collective-permute-start.12 = (bf16[640,1024]{1,0:T(8,128)(2,1)}, bf16[640,1024]{1,0:T(8,128)(2,1)}, u32[]{:S(2)}, u32[]{:S(2)}) collective-permute-start(bf16[640,1024]{1,0:T(8,128)(2,1)} %pad_maximum_fusion.1), channel_id=1, source_target_pairs={{0,1},{1,0},{2,3},{3,2},{4,5},{5,4},{6,7},{7,6},{8,9},{9,8},{10,11... | collective-permute-start | bytes 3932168 | tf_op jit(solution)/shard_map/ppermute | solution.py:34
  125.7 6.2 %copy-start.1 = (bf16[1024,128]{1,0:T(8,128)(2,1)S(1)}, bf16[1024,128]{1,0:T(8,128)(2,1)}, u32[]{:S(2)}) copy-start(bf16[1024,128]{1,0:T(8,128)(2,1)} %param.19) | copy-start | bytes 786436
  (14 other events, 34.3 us)

commit v2 on v1

v2 whole, which is shorter than its diff:
```python
import functools
import math

import jax
import jax.numpy as jnp
from jax import lax
from jax.experimental import pallas as pl
from jax.experimental.pallas import tpu as pltpu
from jax.sharding import PartitionSpec as P

KAPPA = 0.2
KEPT = 80
BLOCK = 256
TOP_SHARE = 0.5
ROOM = 44
LOW_SHARE = 0.6
BF = jnp.bfloat16
F32 = jnp.float32
VMEM = pl.BlockSpec(memory_space=pltpu.VMEM)
ANY = pl.BlockSpec(memory_space=pl.ANY)
HBM = pl.BlockSpec(memory_space=pltpu.HBM)
Shape = jax.ShapeDtypeStruct


def contract_rows(left, right):
    return lax.dot_general(left, right, (((0,), (0,)), ((), ())), preferred_element_type=F32)


def times_transposed(left, right):
    return lax.dot_general(left, right, (((1,), (1,)), ((), ())), preferred_element_type=F32)


def bit_of(stride):
    return (lax.axis_index("tiles") // stride) % 2


def rows_at(index, rows):
    return pl.ds(pl.multiple_of(index * rows, rows), rows)


def rest_rows(n):
    return -(-(n + 3 * KEPT) // 256) * 256


def call(
    body, outs, args, after=None, carry=(), specs=None, out_specs=None, scratch=(), aliases=None, room=12
):
    outs, args = tuple(outs), tuple(args)
    specs = list(specs or [VMEM] * len(args))
    out_specs = list(out_specs or [VMEM] * len(outs))
    count, made = len(args), len(outs)
    aliases = dict(aliases or {})
    extra = (() if after is None else (after,)) + tuple(carry)
    for i, array in enumerate(carry):
        aliases[count + len(extra) - len(carry) + i] = made + i
    plain = body

    def body(*refs):
        given = refs[:count]
        rest = refs[count + len(extra) :]
        plain(*given, *rest[:made], *rest[made + len(carry) :])

    return pl.pallas_call(
        body,
        out_shape=outs + tuple(Shape(a.shape, a.dtype) for a in carry),
        in_specs=specs + [ANY] * len(extra),
        out_specs=tuple(out_specs + [ANY] * len(carry)),
        scratch_shapes=scratch,
        input_output_aliases=aliases,
        compiler_params=pltpu.CompilerParams(vmem_limit_bytes=room * 2**20),
        cost_estimate=pl.CostEstimate(flops=1, bytes_accessed=1, transcendentals=0),
    )(*args, *extra)


def activate(v):
    s = 0.5 + 0.5 * jnp.tanh(0.5 * v)
    act = v * s
    return act.astype(BF), (s + act * (1.0 - s)).astype(BF)


def step_body(depth, before, after, owner, warm, brine, stepped, feat, wet_out):
    lon, lat, levels = warm.shape
    cols = lon * lat
    level = lax.broadcasted_iota(jnp.int32, (lon, lat, levels), 2).astype(F32)
    row = lax.broadcasted_iota(jnp.int32, (lon, lat, levels), 1)
    wet = (level < depth[...]).astype(F32)
    wet_b = (level[:1] < before[2]).astype(F32)
    wet_a = (level[:1] < after[2]).astype(F32)
    wet_e = jnp.concatenate([wet[1:], wet_a], 0)
    wet_w = jnp.concatenate([wet_b, wet[:-1]], 0)
    wet_n = jnp.where(row < lat - 1, pltpu.roll(wet, lat - 1, 1), 0.0)
    wet_s = jnp.where(row > 0, pltpu.roll(wet, 1, 1), 0.0)
    wet_out[...] = wet.reshape(cols, levels)
    lane = lax.broadcasted_iota(jnp.int32, (cols, levels), 1)
    own = lane == owner[...].reshape(cols, levels)
    for i, ref in enumerate((warm, brine)):
        q = ref[...]
        total = wet_e * (jnp.concatenate([q[1:], after[i]], 0) - q)
        total = total + wet_w * (jnp.concatenate([before[i], q[:-1]], 0) - q)
        total = total + wet_n * (pltpu.roll(q, lat - 1, 1) - q)
        total = total + wet_s * (pltpu.roll(q, 1, 1) - q)
        out = q + KAPPA * wet * total
        stepped[i] = out
        feat[:, i * levels : (i + 1) * levels] = jnp.where(
            own, 1.0, (out * wet).reshape(cols, levels)
        ).astype(BF)


def weight_grad(act, delta, half, out, rows):
    for j in range(0, rows, BLOCK):
        at = pl.ds(pl.multiple_of(half * rows + j, BLOCK), BLOCK)
        out[j : j + BLOCK] = contract_rows(act[:, at], delta[...]).astype(BF)


def back_through(delta, weights, slope, out):
    for j in range(0, out.shape[1], BLOCK):
        back = times_transposed(delta, weights[j : j + BLOCK])
        out[:, j : j + BLOCK] = (back * slope[:, j : j + BLOCK].astype(F32)).astype(BF)


def forward_body(
    n,
    scale,
    feat,
    wet,
    bias,
    desired,
    leading,
    interior,
    readout,
    inferred,
    act0,
    act1,
    slope0,
    slope1,
    delta2,
    other,
    rest,
    w_lead,
    w_int,
    act2,
    slope2,
    sems,
):
    cols, levels = wet.shape
    hid = readout.shape[0]
    copies = [
        pltpu.make_async_copy(interior.at[i], w_int.at[i], sems.at[i])
        for i in range(interior.shape[0])
    ]
    for copy in copies:
        copy.start()
    w_lead[...] = leading[...]
    for j in range(bias.shape[1]):
        value = bias[:, j]
        high = value.astype(BF)
        at = slice(j * bias.shape[2], (j + 1) * bias.shape[2])
        w_lead[KEPT : KEPT + n, at] = high
        w_lead[levels + KEPT : levels + KEPT + n, at] = (value - high.astype(F32)).astype(BF)
    for layer, (left, right, act, slope) in enumerate(
        (
            (feat, w_lead, act0, slope0),
            (act0, w_int.at[0], act1, slope1),
            (act1, w_int.at[1], act2, slope2),
        )
    ):
        if layer:
            copies[layer - 1].wait()
        for j in range(0, hid, BLOCK):
            pre = jnp.dot(left[...], right[:, j : j + BLOCK], preferred_element_type=F32)
            act[:, j : j + BLOCK], slope[:, j : j + BLOCK] = activate(pre)
    output = jnp.dot(act2[...], readout[...], preferred_element_type=F32)
    inferred[...] = output.astype(BF).reshape(inferred.shape)
    target = desired[...].reshape(cols, levels).astype(F32)
    err = ((output - target) * wet[...] * scale).astype(BF)
    back_through(err, readout, slope2, delta2)
    weight_grad(act1, delta2, 1 - bit_of(1), other, hid // 2)
    rest[...] = contract_rows(err, act2[...]).astype(BF)[:KEPT]


def middle_body(
    interior, act0, act1, slope1, delta2, mine, delta1, below_other, w_int, sems
):
    hid = act0.shape[1]
    copy = pltpu.make_async_copy(interior.at[1], w_int, sems.at[0])
    copy.start()
    bit = bit_of(1)
    weight_grad(act1, delta2, bit, mine, hid // 2)
    copy.wait()
    back_through(delta2[...], w_int, slope1, delta1)
    weight_grad(act0, delta1, 1 - bit, below_other, hid // 2)


def first_body(
    n,
    interior,
    feat,
    act0,
    slope0,
    delta1,
    readout_in,
    other_in,
    mine,
    other,
    delta0,
    rest,
    w_int,
    sems,
):
    levels = feat.shape[1] // 2
    hid = slope0.shape[1]
    half = hid // 2
    copy = pltpu.make_async_copy(interior.at[0], w_int, sems.at[0])
    copy.start()
    bit = bit_of(1)
    other[:half] = other_in[...]
    weight_grad(act0, delta1, bit, mine, half)
    copy.wait()
    back_through(delta1[...], w_int, slope0, delta0)
    lead = contract_rows(feat[...], delta0[...]).astype(BF)
    a = KEPT + n
    rest[:a] = lead[:a]
    rest[a : a + KEPT] = lead[levels : levels + KEPT]
    rest[a + KEPT : a + 2 * KEPT] = readout_in[...]
    rows = rest.shape[0]
    if rows > a + 2 * KEPT:
        rest[a + 2 * KEPT :] = jnp.zeros((rows - a - 2 * KEPT, hid), BF)
    for ref, b in ((other, 1 - bit), (mine, bit)):
        ref[half:] = rest[rows_at(b, rows // 2)]


def split_body(mine, got, a_mine, a_other, b_mine, b_other):
    base = 0
    for stride, keep, send in ((2, a_mine, a_other), (4, b_mine, b_other)):
        bit = bit_of(stride)
        rows = keep.shape[0]
        for ref, b in ((send, 1 - bit), (keep, bit)):
            at = pl.ds(pl.multiple_of(base + b * rows, 16), rows)
            ref[...] = mine[at] + got[at]
        base += 2 * rows


def halve_body(a, got_a, b, got_b, a_mine, a_other, b_mine, b_other):
    for stride, x, got, keep, send in (
        (4, a, got_a, a_mine, a_other),
        (2, b, got_b, b_mine, b_other),
    ):
        bit = bit_of(stride)
        rows = keep.shape[0]
        for ref, h in ((send, 1 - bit), (keep, bit)):
            ref[...] = x[rows_at(h, rows)] + got[rows_at(h, rows)]


def pair_body(a, got_a, b, got_b, out):
    rows = a.shape[0]
    out[:rows] = a[...] + got_a[...]
    out[rows:] = b[...] + got_b[...]


def unpair_body(x, got, a, b):
    rows = a.shape[0]
    a[...] = x[:rows] + got[:rows]
    b[...] = x[rows:] + got[rows:]


def join_body(a, got_a, b, got_b, a_out, b_out):
    for stride, x, got, out in ((4, a, got_a, a_out), (2, b, got_b, b_out)):
        bit = bit_of(stride)
        rows = x.shape[0]
        out[rows_at(bit, rows)] = x[...]
        out[rows_at(1 - bit, rows)] = got[...]


def join_pair_body(a, got_a, b, got_b, out):
    base = 0
    for stride, x, got in ((2, a, got_a), (4, b, got_b)):
        bit = bit_of(stride)
        rows = x.shape[0]
        for ref, h in ((x, bit), (got, 1 - bit)):
            out[pl.ds(pl.multiple_of(base + h * rows, 16), rows)] = ref[...]
        base += 2 * rows


def swap(x, stride):
    n = lax.axis_size("tiles")
    return lax.ppermute(x, "tiles", [(t, t ^ stride) for t in range(n)])


def bf(rows, like):
    return Shape((rows, like.shape[1]), BF)


class Sum:
    def __init__(self, mine, other, share):
        self.mine, self.got = mine, swap(other, 1)
        self.rows = mine.shape[0]
        self.a = int(share * self.rows / 64) * 64
        self.b = self.rows - self.a

    def step(self, body, rows, args, after, carry):
        outs = [bf(r, self.mine) for r in rows]
        made = call(body, outs, args, after, carry)
        return made[: len(rows)], made[len(rows) :]

    def split(self, after, carry=()):
        rows = [self.a // 2] * 2 + [self.b // 2] * 2
        (a, send_a, b, send_b), carry = self.step(
            split_body, rows, (self.mine, self.got), after, carry
        )
        self.parts = a, swap(send_a, 2), b, swap(send_b, 4)
        return a, *carry

    def halve(self, after, carry=()):
        rows = [self.a // 4] * 2 + [self.b // 4] * 2
        (a, send_a, b, send_b), carry = self.step(halve_body, rows, self.parts, after, carry)
        self.parts = a, swap(send_a, 4), b, swap(send_b, 2)
        return a, *carry

    def pair(self, after, carry=()):
        (m,), carry = self.step(pair_body, [self.rows // 4], self.parts, after, carry)
        token, stride = m, 8
        while 2 * stride < lax.axis_size("tiles"):
            m = m + swap(m, stride)
            stride *= 2
        self.parts = m, swap(m, stride)
        return token, *carry

    def unpair(self, after, carry=()):
        rows = [self.a // 4, self.b // 4]
        (a, b), carry = self.step(unpair_body, rows, self.parts, after, carry)
        self.parts = a, swap(a, 4), b, swap(b, 2)
        return a, *carry

    def join(self, after, carry=()):
        rows = [self.a // 2, self.b // 2]
        (a, b), carry = self.step(join_body, rows, self.parts, after, carry)
        self.parts = a, swap(a, 2), b, swap(b, 4)
        return a, *carry

    def whole(self, after, carry=()):
        (x,), carry = self.step(join_pair_body, [self.rows], self.parts, after, carry)
        return x, *carry


def place_body(slab, flip, *refs):
    x, out, token, wide, sems = refs[0], refs[-4], refs[-3], refs[-2], refs[-1]
    rows = wide.shape[0] // 2
    bit = bit_of(1)
    half = (bit + flip) % 2
    copies = []
    for i in range(2):
        at = slice(i * rows, (i + 1) * rows)
        wide[at] = x[at].astype(F32)
        to = pl.ds(pl.multiple_of(half * 2 * rows + i * rows, rows), rows)
        copies.append(pltpu.make_async_copy(wide.at[at], out.at[slab, to], sems.at[i]))
        copies[-1].start()
    token[...] = jnp.zeros(token.shape, F32)
    for copy in copies:
        copy.wait()


def place(slab, flip, x, shape, held, after):
    hid = shape.shape[1]
    return call(
        functools.partial(place_body, slab, flip),
        (shape, Shape((8, 128), F32)),
        (x,) if held is None else (x, held),
        after,
        specs=[VMEM] if held is None else [VMEM, HBM],
        out_specs=(HBM, VMEM),
        scratch=[pltpu.VMEM((hid // 2, hid), F32), pltpu.SemaphoreType.DMA((2,))],
        aliases={} if held is None else {1: 0},
    )


def finish_body(n, x, got, held, out, lead_out, readout_out, own_out, wide, rest, sems):
    hid = out.shape[1]
    half = hid // 2
    levels = lead_out.shape[0] // 2
    bit = bit_of(1)
    copies = []
    rows = rest.shape[0] // 2
    for i in range(2):
        at = slice(i * half // 2, (i + 1) * half // 2)
        wide[at] = got[at].astype(F32)
        to = pl.ds(pl.multiple_of((1 - bit) * half + i * half // 2, half // 2), half // 2)
        copies.append(pltpu.make_async_copy(wide.at[at], out.at[0, to], sems.at[i]))
        copies[-1].start()
    for ref, b in ((x, bit), (got, 1 - bit)):
        rest[rows_at(b, rows)] = ref[half:].astype(F32)
    a = KEPT + n
    zeros = jnp.zeros((levels - KEPT, hid), F32)
    lead_out[:KEPT] = rest[:KEPT]
    lead_out[KEPT:levels] = zeros
    lead_out[levels : levels + KEPT] = rest[a : a + KEPT]
    lead_out[levels + KEPT :] = zeros
    own_out[...] = rest[pl.ds(KEPT + lax.axis_index("tiles"), 1)]
    readout_out[...] = jnp.concatenate([rest[a + KEPT : a + 2 * KEPT], zeros], 0).T
    for copy in copies:
        copy.wait()


def local(
    warmth,
    brine,
    flags,
    tally,
    assigned,
    desired,
    intercepts,
    leading,
    interior,
    readout,
):
    n = lax.axis_size("tiles")
    lon, lat, levels = warmth.shape
    cols = lon * lat
    hid = leading.shape[1]
    scale = 1.0 / math.sqrt(cols * n)

    up = [(i, (i + 1) % n) for i in range(n)]
    down = [(j, i) for i, j in up]
    wide = (lon, lat, levels)
    depth = jnp.where(flags > 0, tally, 0).astype(F32)
    depth = jnp.broadcast_to(depth[:, :, None], wide)
    owner = jnp.broadcast_to(assigned[:, :, None] + KEPT, wide)
    first = jnp.stack([warmth[:1], brine[:1], depth[:1]])
    last = jnp.stack([warmth[-1:], brine[-1:], depth[-1:]])
    before = lax.ppermute(last, "tiles", up)
    after = lax.ppermute(first, "tiles", down)
    intercepts, _ = lax.optimization_barrier((intercepts, (first, last)))
    bias = lax.all_to_all(
        jnp.broadcast_to(intercepts.reshape(1, hid // 128, 128), (n, hid // 128, 128)),
        "tiles",
        split_axis=0,
        concat_axis=0,
        tiled=True,
    )
    act = Shape((cols, hid), BF)
    half = Shape((hid // 2, hid), BF)
    stepped, feat, wet = call(
        step_body,
        (Shape((2,) + wide, F32), Shape((cols, 2 * levels), BF), Shape((cols, levels), F32)),
        (depth, before, after, owner, warmth, brine),
    )
    weights = pltpu.VMEM((hid, hid), BF)
    sem = pltpu.SemaphoreType.DMA((interior.shape[0],))
    whole_act = pltpu.VMEM(act.shape, BF)
    inferred, act0, act1, slope0, slope1, delta2, other, rest = call(
        functools.partial(forward_body, n, scale),
        (Shape(wide, BF), act, act, act, act, act, half, Shape((KEPT, hid), BF)),
        (feat, wet, bias, desired, leading, interior, readout),
        specs=[VMEM] * 5 + [ANY, VMEM],
        scratch=[
            pltpu.VMEM(leading.shape, BF),
            pltpu.VMEM(interior.shape, BF),
            whole_act,
            whole_act,
            sem,
        ],
        room=ROOM,
    )
    rows = rest_rows(n)
    mine, delta1, below = call(
        middle_body,
        (half, act, half),
        (interior, act0, act1, slope1, delta2),
        specs=[ANY] + [VMEM] * 4,
        scratch=[weights, sem],
        room=ROOM,
    )
    top = Sum(mine, other, TOP_SHARE)
    (token,) = top.split(delta1)
    part = Shape((hid // 2 + rows // 2, hid), BF)
    mine, other = call(
        functools.partial(first_body, n),
        (part, part),
        (interior, feat, act0, slope0, delta1, rest, below),
        token,
        specs=[ANY] + [VMEM] * 6,
        scratch=[whole_act, pltpu.VMEM((rows, hid), BF), weights, sem],
        room=ROOM,
    )
    token, other = top.halve(mine, [other])
    low = Sum(mine, other, LOW_SHARE)
    (token,) = top.pair(token)
    (token,) = low.split(token)
    (token,) = low.halve(token)
    (token,) = top.unpair(token)
    (token,) = low.pair(token)
    (token,) = top.join(token)
    (x,) = top.whole(token)
    token, x = low.unpair(None, [x])
    got = swap(x, 1)
    (token,) = low.join(token)
    grads = Shape((interior.shape[0], hid, hid), F32)
    held, token = place(1, 0, x, grads, None, token)
    held, token = place(1, 1, got, grads, held, token)
    (x,) = low.whole(token)
    held, _ = place(0, 0, x, grads, held, None)
    interior_out, lead_out, readout_out, own_out = call(
        functools.partial(finish_body, n),
        (
            grads,
            Shape((2 * levels, hid), F32),
            Shape((hid, levels), F32),
            Shape((1, hid), F32),
        ),
        (x, swap(x, 1), held),
        specs=[VMEM, VMEM, HBM],
        out_specs=(HBM, VMEM, VMEM, VMEM),
        scratch=[
            pltpu.VMEM((hid // 2, hid), F32),
            pltpu.VMEM((rows, hid), F32),
            pltpu.SemaphoreType.DMA((2,)),
        ],
        aliases={2: 0},
    )
    return stepped, inferred, lead_out, interior_out, readout_out, own_out


def solution(mesh):
    part = ("groups", "tiles")
    return jax.shard_map(
        local,
        mesh=mesh,
        in_specs=(
            P(part, None, None),
            P(part, None, None),
            P(part, None),
            P(part, None),
            P(part, None),
            P(part, None, None),
            P(part, None),
            P(),
            P(),
            P(),
        ),
        out_specs=(
            P(None, part, None, None),
            P(part, None, None),
            P("groups", None),
            P(None, "groups", None),
            P("groups", None),
            P(part, None),
        ),
        check_vma=False,
    )
```

time: 133 us -> 106 us (0.80)
  Pallas kernels: 0 us -> 22.7 us
  other arithmetic: 24 us -> 1.53 us
  matrix products: 18 us -> 0 us
  local copies, waits for them, and re-layouts: 12.5 us -> 2.51 us
  waiting for transfers between devices: 48.8 us -> 54.2 us
  starting transfers between devices: 27.2 us -> 23.8 us
    pallas_call x0 -> x20, Pallas kernels: none -> 22.7 us  [call(): pl.pallas_call(body, out_shape=outs + tuple((Shape(a.shape, a.dtype) for...]
    dot_general x10 -> x0, matrix products: 18 us -> none  [the longest x4 8.74 us: contract_rows(): lax.dot_general(left, right, (((0,), (0,)), ((), ())), preferred_element_...]
    unnamed x44 -> x10, local copies, waits for them, and re-layouts: 8.15 us -> 0.03 us
    another operation x4 -> x2, other arithmetic: 7.32 us -> 0.01 us  [the longest x1 0.01 us: local(): last = jnp.stack([warmth[-1:], brine[-1:], depth[-1:]])]
    concatenate x11 -> x0, other arithmetic: 5.7 us -> none  [the longest x5 2.86 us: join(): jnp.concatenate([jnp.where(bit == 0, x, got), jnp.where(bit == 0, got, x)...]
    convert_element_type x17 -> x1, other arithmetic: 6.02 us -> 0.82 us  [local(): depth = jnp.where(flags > 0, tally, 0).astype(F32)]
    ppermute x22, starting transfers between devices: 18 us -> 14.6 us  [swap(): return lax.ppermute(x, 'tiles', [(t, t ^ stride) for t in range(n)])]
    ppermute x22, waiting for transfers between devices: 46.2 us -> 49.5 us  [swap(): return lax.ppermute(x, 'tiles', [(t, t ^ stride) for t in range(n)])]
  transfers between devices with their start and end apart: 25 -> 25, of which waited for: 13 -> 18; matrix products, arithmetic and copies ran while one was open for 11% -> 2% of each run, Pallas kernels for 0% -> 12%
where the time goes in v2:
time: 106 us
  waiting for transfers between devices  54.2 us (51%)
  starting transfers between devices  23.8 us (22%)
  Pallas kernels  22.7 us (21%)
  local copies, waits for them, and re-layouts  2.51 us (2%)
  other arithmetic  1.53 us (1%)
    ppermute x22, waiting for transfers between devices, swap(): return lax.ppermute(x, 'tiles', [(t, t ^ stride) for t in range(n)])  49.5 us
    pallas_call x20, Pallas kernels, call(): pl.pallas_call(body, out_shape=outs + tuple((Shape(a.shape, a.dtype) for...  22.7 us
    ppermute x22, starting transfers between devices, swap(): return lax.ppermute(x, 'tiles', [(t, t ^ stride) for t in range(n)])  14.6 us
    ppermute x1, starting transfers between devices, local(): after = lax.ppermute(first, 'tiles', down)  5 us
    all_to_all x1, waiting for transfers between devices, local(): lax.all_to_all(jnp.broadcast_to(intercepts.reshape(1, hid // 128, 128), (...  4.73 us
    all_to_all x1, starting transfers between devices, local(): lax.all_to_all(jnp.broadcast_to(intercepts.reshape(1, hid // 128, 128), (...  3.68 us
  transfers between devices with their start and end apart: 25, of which 18 were waited for; matrix products, arithmetic and copies ran while one was open for 2% of the time, Pallas kernels for 12%

profile of v2, /device:TPU:0, one launch (start us, length us, event | category | flops | bytes accessed | tf_op | source)
XLA Modules:
  0.0 105.6 jit_solution(10082531775604158424)
XLA Ops:
  2.9 5.0 %collective-permute-start.1 = (f32[3,1,32,128]{3,2,1,0:T(8,128)S(1)}, f32[3,1,32,128]{3,2,1,0:T(8,128)S(1)}, u32[]{:S(2)}, u32[]{:S(2)}) collective-permute-start(f32[3,1,32,128]{3,2,1,0:T(8,128)S(1)} %pad_maximum_fusion.1), channel_id=1, source_target_pairs={{1,0},{2,1},{3,2},{4,3},{5,4},{6,5},{7,6},{8,7},{9,8},{10,9},{11,1... | collective-permute-start | bytes 147464 | tf_op jit(solution)/shard_map/ppermute | solution.py:430
  7.9 1.3 %broadcast_in_dim.24 = f32[16,8,128]{2,1,0:T(8,128)} broadcast(f32[8,128]{1,0:T(8,128)} %bitcast.13), dimensions={1,2} | broadcast | bytes 69632 | tf_op jit(solution)/shard_map/broadcast_in_dim | solution.py:433
  9.2 3.7 %all-to-all-start = ((f32[16,8,128]{2,1,0:T(8,128)}), f32[16,8,128]{2,1,0:T(8,128)S(1)}, u32[]{:S(2)}, u32[]{:S(2)}) async-start(f32[16,8,128]{2,1,0:T(8,128)} %broadcast_in_dim.24), calls=%async_computation | async-start | bytes 131072 | tf_op jit(solution)/shard_map/all_to_all | solution.py:432
  13.9 1.2 %shard_map.145 = (f32[2,16,32,128]{3,2,1,0:T(8,128)}, bf16[512,256]{1,0:T(8,128)(2,1)S(1)}, f32[512,128]{1,0:T(8,128)S(1)}) custom-call(f32[16,32,128]{2,1,0:T(8,128)S(1)} %broadcast_in_dim.10.refs_0_, f32[3,1,32,128]{3,2,1,0:T(8,128)S(1)} %collective-permute-done.refs_1_, f32[3,1,32,128]{3,2,1,0:T(8,128)S(1)} %collective-permute-done.1.refs_2_, ...), custom_call_target="tpu_custom_call" | custom-call | flops 1 | bytes 1 | tf_op jit(solution)/shard_map/pallas_call | solution.py:63
  15.1 4.7 %all-to-all-done.refs_2_ = f32[16,8,128]{2,1,0:T(8,128)S(1)} async-done(((f32[16,8,128]{2,1,0:T(8,128)}), f32[16,8,128]{2,1,0:T(8,128)S(1)}, u32[]{:S(2)}, u32[]{:S(2)}) %all-to-all-start) | async-done | bytes 65568 | tf_op jit(solution)/shard_map/all_to_all | solution.py:432
  19.8 6.4 %shard_map.146 = (bf16[16,32,128]{2,1,0:T(8,128)(2,1)}, bf16[512,1024]{1,0:T(8,128)(2,1)S(1)}, bf16[512,1024]{1,0:T(8,128)(2,1)S(1)}, bf16[512,1024]{1,0:T(8,128...) custom-call(bf16[512,256]{1,0:T(8,128)(2,1)S(1)} %get-tuple-element., ...), custom_call_target="tpu_custom_call" | custom-call | flops 1 | bytes 1 | tf_op jit(solution)/shard_map/pallas_call | solution.py:63
  26.3 3.5 %shard_map.147 = (bf16[512,1024]{1,0:T(8,128)(2,1)S(1)}, bf16[512,1024]{1,0:T(8,128)(2,1)S(1)}, bf16[512,1024]{1,0:T(8,128)(2,1)S(1)}) custom-call(bf16[2,1024,1024]{2,1,0:T(8,128)(2,1)} %refs_0_.3, bf16[512,1024]{1,0:T(8,128)(2,1)S(1)} %get-tuple-element.63.refs_1_.refs_2_, bf16[512,1024]{1,0:T(8,128)(2,1)S(1)} %get-tuple-element.65.refs_2_, ...), custom_call_target="tpu_custom_call" | custom-call | flops 1 | bytes 1 | tf_op jit(solution)/shard_map/pallas_call | solution.py:63
  30.9 3.2 %shard_map.149 = (bf16[640,1024]{1,0:T(8,128)(2,1)S(1)}, bf16[640,1024]{1,0:T(8,128)(2,1)S(1)}) custom-call(bf16[2,1024,1024]{2,1,0:T(8,128)(2,1)} %refs_0_.3, bf16[512,256]{1,0:T(8,128)(2,1)S(1)} %get-tuple-element.59.refs_0_.refs_1_, bf16[512,1024]{1,0:T(8,128)(2,1)S(1)} %get-tuple-element.63.refs_1_.refs_2_, ...), custom_call_target="tpu_custom_call" | custom-call | flops 1 | bytes 1 | tf_op jit(solution)/shard_map/pallas_call | solution.py:63
  34.1 4.6 %collective-permute-done.3.refs_1_ = bf16[128,1024]{1,0:T(8,128)(2,1)S(1)} collective-permute-done((bf16[128,1024]{1,0:T(8,128)(2,1)S(1)}, bf16[128,1024]{1,0:T(8,128)(2,1)S(1)}, u32[]{:S(2)}, u32[]{:S(2)}) %collective-permute-start.3) | collective-permute-done | bytes 262176 | tf_op jit(solution)/shard_map/ppermute | solution.py:286
  39.5 1.5 %collective-permute-start.7 = (bf16[64,1024]{1,0:T(8,128)(2,1)S(1)}, bf16[64,1024]{1,0:T(8,128)(2,1)S(1)}, u32[]{:S(2)}, u32[]{:S(2)}) collective-permute-start(bf16[64,1024]{1,0:T(8,128)(2,1)S(1)} %get-tuple-element.83), channel_id=1, source_target_pairs={{0,2},{1,3},{2,0},{3,1},{4,6},{5,7},{6,4},{7,5},{8,10},{9,11},{10,... | collective-permute-start | bytes 393224 | tf_op jit(solution)/shard_map/ppermute | solution.py:286
  41.0 3.9 %collective-permute-done.6.refs_1_ = bf16[64,1024]{1,0:T(8,128)(2,1)S(1)} collective-permute-done((bf16[64,1024]{1,0:T(8,128)(2,1)S(1)}, bf16[64,1024]{1,0:T(8,128)(2,1)S(1)}, u32[]{:S(2)}, u32[]{:S(2)}) %collective-permute-start.6) | collective-permute-done | bytes 131104 | tf_op jit(solution)/shard_map/ppermute | solution.py:286
  45.2 1.6 %collective-permute-start.8 = (bf16[192,1024]{1,0:T(8,128)(2,1)S(1)}, bf16[192,1024]{1,0:T(8,128)(2,1)S(1)}, u32[]{:S(2)}, u32[]{:S(2)}) collective-permute-start(bf16[192,1024]{1,0:T(8,128)(2,1)S(1)} %get-tuple-element.85), channel_id=1, source_target_pairs={{0,2},{1,3},{2,0},{3,1},{4,6},{5,7},{6,4},{7,5},{8,10},{9,11},{10,... | collective-permute-start | bytes 1179656 | tf_op jit(solution)/shard_map/ppermute | solution.py:286
  46.8 1.7 %collective-permute-start.9 = (bf16[128,1024]{1,0:T(8,128)(2,1)S(1)}, bf16[128,1024]{1,0:T(8,128)(2,1)S(1)}, u32[]{:S(2)}, u32[]{:S(2)}) collective-permute-start(bf16[128,1024]{1,0:T(8,128)(2,1)S(1)} %get-tuple-element.87), channel_id=1, source_target_pairs={{0,4},{1,5},{2,6},{3,7},{4,0},{5,1},{6,2},{7,3},{8,12},{9,13},{10,... | collective-permute-start | bytes 786440 | tf_op jit(solution)/shard_map/ppermute | solution.py:286
  48.8 9.2 %collective-permute-done.9.refs_3_ = bf16[128,1024]{1,0:T(8,128)(2,1)S(1)} collective-permute-done((bf16[128,1024]{1,0:T(8,128)(2,1)S(1)}, bf16[128,1024]{1,0:T(8,128)(2,1)S(1)}, u32[]{:S(2)}, u32[]{:S(2)}) %collective-permute-start.9) | collective-permute-done | bytes 262176 | tf_op jit(solution)/shard_map/ppermute | solution.py:286
  59.0 3.2 %collective-permute-done.12.refs_1_ = bf16[128,1024]{1,0:T(8,128)(2,1)S(1)} collective-permute-done((bf16[128,1024]{1,0:T(8,128)(2,1)S(1)}, bf16[128,1024]{1,0:T(8,128)(2,1)S(1)}, u32[]{:S(2)}, u32[]{:S(2)}) %collective-permute-start.12) | collective-permute-done | bytes 262176 | tf_op jit(solution)/shard_map/ppermute | solution.py:286
  63.4 3.1 %collective-permute-done.10.refs_1_ = bf16[96,1024]{1,0:T(8,128)(2,1)S(1)} collective-permute-done((bf16[96,1024]{1,0:T(8,128)(2,1)S(1)}, bf16[96,1024]{1,0:T(8,128)(2,1)S(1)}, u32[]{:S(2)}, u32[]{:S(2)}) %collective-permute-start.10) | collective-permute-done | bytes 196640 | tf_op jit(solution)/shard_map/ppermute | solution.py:286
  67.3 1.1 %collective-permute-done.14.refs_1_ = bf16[64,1024]{1,0:T(8,128)(2,1)S(1)} collective-permute-done((bf16[64,1024]{1,0:T(8,128)(2,1)S(1)}, bf16[64,1024]{1,0:T(8,128)(2,1)S(1)}, u32[]{:S(2)}, u32[]{:S(2)}) %collective-permute-start.14) | collective-permute-done | bytes 131104 | tf_op jit(solution)/shard_map/ppermute | solution.py:286
  68.4 1.0 collective-permute-start.16
  69.4 1.3 %collective-permute-start.17 = (bf16[128,1024]{1,0:T(8,128)(2,1)S(1)}, bf16[128,1024]{1,0:T(8,128)(2,1)S(1)}, u32[]{:S(2)}, u32[]{:S(2)}) collective-permute-start(bf16[128,1024]{1,0:T(8,128)(2,1)S(1)} %get-tuple-element.95.refs_2_), channel_id=1, source_target_pairs={{0,4},{1,5},{2,6},{3,7},{4,0},{5,1},{6,2},{7,3},{8,12},{9,13},{10,... | collective-permute-start | bytes 786440 | tf_op jit(solution)/shard_map/ppermute | solution.py:286
  70.8 4.5 %collective-permute-done.16.refs_1_ = bf16[128,1024]{1,0:T(8,128)(2,1)S(1)} collective-permute-done((bf16[128,1024]{1,0:T(8,128)(2,1)S(1)}, bf16[128,1024]{1,0:T(8,128)(2,1)S(1)}, u32[]{:S(2)}, u32[]{:S(2)}) %collective-permute-start.16) | collective-permute-done | bytes 262176 | tf_op jit(solution)/shard_map/ppermute | solution.py:286
  75.2 6.1 %collective-permute-done.17.refs_3_ = bf16[128,1024]{1,0:T(8,128)(2,1)S(1)} collective-permute-done((bf16[128,1024]{1,0:T(8,128)(2,1)S(1)}, bf16[128,1024]{1,0:T(8,128)(2,1)S(1)}, u32[]{:S(2)}, u32[]{:S(2)}) %collective-permute-start.17) | collective-permute-done | bytes 262176 | tf_op jit(solution)/shard_map/ppermute | solution.py:286
  81.6 1.7 %collective-permute-start.19 = (bf16[64,1024]{1,0:T(8,128)(2,1)S(1)}, bf16[64,1024]{1,0:T(8,128)(2,1)S(1)}, u32[]{:S(2)}, u32[]{:S(2)}) collective-permute-start(bf16[64,1024]{1,0:T(8,128)(2,1)S(1)} %get-tuple-element.97.refs_2_), channel_id=1, source_target_pairs={{0,2},{1,3},{2,0},{3,1},{4,6},{5,7},{6,4},{7,5},{8,10},{9,11},{10,... | collective-permute-start | bytes 393224 | tf_op jit(solution)/shard_map/ppermute | solution.py:286
  83.3 4.2 %collective-permute-done.19.refs_3_ = bf16[64,1024]{1,0:T(8,128)(2,1)S(1)} collective-permute-done((bf16[64,1024]{1,0:T(8,128)(2,1)S(1)}, bf16[64,1024]{1,0:T(8,128)(2,1)S(1)}, u32[]{:S(2)}, u32[]{:S(2)}) %collective-permute-start.19) | collective-permute-done | bytes 131104 | tf_op jit(solution)/shard_map/ppermute | solution.py:286
  87.5 1.4 %collective-permute-done.18.refs_1_ = bf16[96,1024]{1,0:T(8,128)(2,1)S(1)} collective-permute-done((bf16[96,1024]{1,0:T(8,128)(2,1)S(1)}, bf16[96,1024]{1,0:T(8,128)(2,1)S(1)}, u32[]{:S(2)}, u32[]{:S(2)}) %collective-permute-start.18) | collective-permute-done | bytes 196640 | tf_op jit(solution)/shard_map/ppermute | solution.py:286
  88.9 1.7 %collective-permute-start.20 = (bf16[192,1024]{1,0:T(8,128)(2,1)S(1)}, bf16[192,1024]{1,0:T(8,128)(2,1)S(1)}, u32[]{:S(2)}, u32[]{:S(2)}) collective-permute-start(bf16[192,1024]{1,0:T(8,128)(2,1)S(1)} %get-tuple-element.98.refs_1_.refs_0_), channel_id=1, source_target_pairs={{0,2},{1,3},{2,0},{3,1},{4,6},{5,7},{6,4},{7,5},{8,10},{9,11},{10,... | collective-permute-start | bytes 1179656 | tf_op jit(solution)/shard_map/ppermute | solution.py:286
  90.9 1.4 %shard_map.160 = (f32[2,1024,1024]{2,1,0:T(8,128)}, f32[8,128]{1,0:T(8,128)S(1)}) custom-call(bf16[512,1024]{1,0:T(8,128)(2,1)S(1)} %get-tuple-element.100.refs_0_, bf16[192,1024]{1,0:T(8,128)(2,1)S(1)} %get-tuple-element.98.refs_1_.refs_0_), custom_call_target="tpu_custom_call" | custom-call | flops 1 | bytes 1 | tf_op jit(solution)/shard_map/pallas_call | solution.py:63
  92.4 1.4 %shard_map.161 = (f32[2,1024,1024]{2,1,0:T(8,128)}, f32[8,128]{1,0:T(8,128)S(1)}) custom-call(bf16[512,1024]{1,0:T(8,128)(2,1)S(1)} %collective-permute-done.22.refs_0_, f32[2,1024,1024]{2,1,0:T(8,128)} %get-tuple-element.101.refs_1_, f32[8,128]{1,0:T(8,128)S(1)} %get-tuple-element.102.refs_2_), custom_call_target="tpu_custom_call", output_to_operand_aliasing={{0}: (1, {})} | custom-call | flops 1 | bytes 1 | tf_op jit(solution)/shard_map/pallas_call | solution.py:63
  93.8 4.4 %collective-permute-done.21.refs_3_ = bf16[128,1024]{1,0:T(8,128)(2,1)S(1)} collective-permute-done((bf16[128,1024]{1,0:T(8,128)(2,1)S(1)}, bf16[128,1024]{1,0:T(8,128)(2,1)S(1)}, u32[]{:S(2)}, u32[]{:S(2)}) %collective-permute-start.21) | collective-permute-done | bytes 262176 | tf_op jit(solution)/shard_map/ppermute | solution.py:286
  98.2 1.5 %collective-permute-done.20.refs_1_ = bf16[192,1024]{1,0:T(8,128)(2,1)S(1)} collective-permute-done((bf16[192,1024]{1,0:T(8,128)(2,1)S(1)}, bf16[192,1024]{1,0:T(8,128)(2,1)S(1)}, u32[]{:S(2)}, u32[]{:S(2)}) %collective-permute-start.20) | collective-permute-done | bytes 393248 | tf_op jit(solution)/shard_map/ppermute | solution.py:286
  99.9 2.0 %shard_map.163 = (f32[2,1024,1024]{2,1,0:T(8,128)}, f32[8,128]{1,0:T(8,128)}) custom-call(bf16[640,1024]{1,0:T(8,128)(2,1)S(1)} %shard_map.162.refs_0_, f32[2,1024,1024]{2,1,0:T(8,128)} %get-tuple-element.104.refs_1_), custom_call_target="tpu_custom_call", output_to_operand_aliasing={{0}: (1, {})} | custom-call | flops 1 | bytes 1 | tf_op jit(solution)/shard_map/pallas_call | solution.py:63
  101.9 1.0 collective-permute-done.23.refs_1_
  102.9 2.7 %shard_map.164 = (f32[2,1024,1024]{2,1,0:T(8,128)}, f32[256,1024]{1,0:T(8,128)}, f32[1024,128]{1,0:T(8,128)}, f32[1,1024]{1,0:T(1,128)}) custom-call(bf16[640,1024]{1,0:T(8,128)(2,1)S(1)} %shard_map.162.refs_0_, bf16[640,1024]{1,0:T(8,128)(2,1)S(1)} %collective-permute-done.23.refs_1_, ...), custom_call_target="tpu_custom_call", output_to_operand_aliasing={{0}: (2, {})} | custom-call | flops 1 | bytes 1 | tf_op jit(solution)/shard_map/pallas_call | solution.py:63
  (59 shorter events, 9.5 us)
Async XLA Ops:
  0.6 13.2 %copy-start.1 = (f32[16,32,128]{2,1,0:T(8,128)S(1)}, f32[16,32,128]{2,1,0:T(8,128)}, u32[]{:S(2)}) copy-start(f32[16,32,128]{2,1,0:T(8,128)} %refs_5_.2) | copy-start | bytes 786436
  0.6 13.2 %copy-start.2 = (f32[16,32,128]{2,1,0:T(8,128)S(1)}, f32[16,32,128]{2,1,0:T(8,128)}, u32[]{:S(2)}) copy-start(f32[16,32,128]{2,1,0:T(8,128)} %refs_4_.2) | copy-start | bytes 786436
  0.7 19.1 %copy-start.3 = (bf16[1024,128]{1,0:T(8,128)(2,1)S(1)}, bf16[1024,128]{1,0:T(8,128)(2,1)}, u32[]{:S(2)}) copy-start(bf16[1024,128]{1,0:T(8,128)(2,1)} %refs_6_.1) | copy-start | bytes 786436
  0.7 19.1 %copy-start = (bf16[256,1024]{1,0:T(8,128)(2,1)S(1)}, bf16[256,1024]{1,0:T(8,128)(2,1)}, u32[]{:S(2)}) copy-start(bf16[256,1024]{1,0:T(8,128)(2,1)} %refs_4_.3) | copy-start | bytes 1572868
  0.7 19.1 %copy-start.4 = (bf16[16,32,128]{2,1,0:T(8,128)(2,1)S(1)}, bf16[16,32,128]{2,1,0:T(8,128)(2,1)}, u32[]{:S(2)}) copy-start(bf16[16,32,128]{2,1,0:T(8,128)(2,1)} %refs_3_.1) | copy-start | bytes 393220
  2.4 11.2 %collective-permute-start = (f32[3,1,32,128]{3,2,1,0:T(8,128)S(1)}, f32[3,1,32,128]{3,2,1,0:T(8,128)S(1)}, u32[]{:S(2)}, u32[]{:S(2)}) collective-permute-start(f32[3,1,32,128]{3,2,1,0:T(8,128)S(1)} %pad_maximum_fusion), channel_id=1, source_target_pairs={{0,1},{1,2},{2,3},{3,4},{4,5},{5,6},{6,7},{7,8},{8,9},{9,10},{10,1... | collective-permute-start | bytes 147464 | tf_op jit(solution)/shard_map/ppermute | solution.py:429
  2.9 10.7 %collective-permute-start.1 = (f32[3,1,32,128]{3,2,1,0:T(8,128)S(1)}, f32[3,1,32,128]{3,2,1,0:T(8,128)S(1)}, u32[]{:S(2)}, u32[]{:S(2)}) collective-permute-start(f32[3,1,32,128]{3,2,1,0:T(8,128)S(1)} %pad_maximum_fusion.1), channel_id=1, source_target_pairs={{1,0},{2,1},{3,2},{4,3},{5,4},{6,5},{7,6},{8,7},{9,8},{10,9},{11,1... | collective-permute-start | bytes 147464 | tf_op jit(solution)/shard_map/ppermute | solution.py:430
  9.2 10.6 %all-to-all-start = ((f32[16,8,128]{2,1,0:T(8,128)}), f32[16,8,128]{2,1,0:T(8,128)S(1)}, u32[]{:S(2)}, u32[]{:S(2)}) async-start(f32[16,8,128]{2,1,0:T(8,128)} %broadcast_in_dim.24), calls=%async_computation | async-start | bytes 131072 | tf_op jit(solution)/shard_map/all_to_all | solution.py:432
  26.3 3.6 %collective-permute-start.2 = (bf16[512,1024]{1,0:T(8,128)(2,1)S(1)}, bf16[512,1024]{1,0:T(8,128)(2,1)S(1)}, u32[]{:S(2)}, u32[]{:S(2)}) collective-permute-start(bf16[512,1024]{1,0:T(8,128)(2,1)S(1)} %get-tuple-element.72), channel_id=1, source_target_pairs={{0,1},{1,0},{2,3},{3,2},{4,5},{5,4},{6,7},{7,6},{8,9},{9,8},{10,11... | collective-permute-start | bytes 3145736 | tf_op jit(solution)/shard_map/ppermute | solution.py:286
  30.0 8.8 %collective-permute-start.3 = (bf16[128,1024]{1,0:T(8,128)(2,1)S(1)}, bf16[128,1024]{1,0:T(8,128)(2,1)S(1)}, u32[]{:S(2)}, u32[]{:S(2)}) collective-permute-start(bf16[128,1024]{1,0:T(8,128)(2,1)S(1)} %get-tuple-element.75), channel_id=1, source_target_pairs={{0,2},{1,3},{2,0},{3,1},{4,6},{5,7},{6,4},{7,5},{8,10},{9,11},{10,... | collective-permute-start | bytes 786440 | tf_op jit(solution)/shard_map/ppermute | solution.py:286
  30.2 8.6 %collective-permute-start.4 = (bf16[128,1024]{1,0:T(8,128)(2,1)S(1)}, bf16[128,1024]{1,0:T(8,128)(2,1)S(1)}, u32[]{:S(2)}, u32[]{:S(2)}) collective-permute-start(bf16[128,1024]{1,0:T(8,128)(2,1)S(1)} %get-tuple-element.77), channel_id=1, source_target_pairs={{0,4},{1,5},{2,6},{3,7},{4,0},{5,1},{6,2},{7,3},{8,12},{9,13},{10,... | collective-permute-start | bytes 786440 | tf_op jit(solution)/shard_map/ppermute | solution.py:286
  38.9 6.2 %collective-permute-start.5 = (bf16[640,1024]{1,0:T(8,128)(2,1)S(1)}, bf16[640,1024]{1,0:T(8,128)(2,1)S(1)}, u32[]{:S(2)}, u32[]{:S(2)}) collective-permute-start(bf16[640,1024]{1,0:T(8,128)(2,1)S(1)} %get-tuple-element.79), channel_id=1, source_target_pairs={{0,1},{1,0},{2,3},{3,2},{4,5},{5,4},{6,7},{7,6},{8,9},{9,8},{10,11... | collective-permute-start | bytes 3932168 | tf_op jit(solution)/shard_map/ppermute | solution.py:286
  39.0 5.9 %collective-permute-start.6 = (bf16[64,1024]{1,0:T(8,128)(2,1)S(1)}, bf16[64,1024]{1,0:T(8,128)(2,1)S(1)}, u32[]{:S(2)}, u32[]{:S(2)}) collective-permute-start(bf16[64,1024]{1,0:T(8,128)(2,1)S(1)} %get-tuple-element.81), channel_id=1, source_target_pairs={{0,4},{1,5},{2,6},{3,7},{4,0},{5,1},{6,2},{7,3},{8,12},{9,13},{10,... | collective-permute-start | bytes 393224 | tf_op jit(solution)/shard_map/ppermute | solution.py:286
  39.5 5.6 %collective-permute-start.7 = (bf16[64,1024]{1,0:T(8,128)(2,1)S(1)}, bf16[64,1024]{1,0:T(8,128)(2,1)S(1)}, u32[]{:S(2)}, u32[]{:S(2)}) collective-permute-start(bf16[64,1024]{1,0:T(8,128)(2,1)S(1)} %get-tuple-element.83), channel_id=1, source_target_pairs={{0,2},{1,3},{2,0},{3,1},{4,6},{5,7},{6,4},{7,5},{8,10},{9,11},{10,... | collective-permute-start | bytes 393224 | tf_op jit(solution)/shard_map/ppermute | solution.py:286
  45.2 12.8 %collective-permute-start.8 = (bf16[192,1024]{1,0:T(8,128)(2,1)S(1)}, bf16[192,1024]{1,0:T(8,128)(2,1)S(1)}, u32[]{:S(2)}, u32[]{:S(2)}) collective-permute-start(bf16[192,1024]{1,0:T(8,128)(2,1)S(1)} %get-tuple-element.85), channel_id=1, source_target_pairs={{0,2},{1,3},{2,0},{3,1},{4,6},{5,7},{6,4},{7,5},{8,10},{9,11},{10,... | collective-permute-start | bytes 1179656 | tf_op jit(solution)/shard_map/ppermute | solution.py:286
  46.8 11.2 %collective-permute-start.9 = (bf16[128,1024]{1,0:T(8,128)(2,1)S(1)}, bf16[128,1024]{1,0:T(8,128)(2,1)S(1)}, u32[]{:S(2)}, u32[]{:S(2)}) collective-permute-start(bf16[128,1024]{1,0:T(8,128)(2,1)S(1)} %get-tuple-element.87), channel_id=1, source_target_pairs={{0,4},{1,5},{2,6},{3,7},{4,0},{5,1},{6,2},{7,3},{8,12},{9,13},{10,... | collective-permute-start | bytes 786440 | tf_op jit(solution)/shard_map/ppermute | solution.py:286
  48.6 13.7 %collective-permute-start.12 = (bf16[128,1024]{1,0:T(8,128)(2,1)S(1)}, bf16[128,1024]{1,0:T(8,128)(2,1)S(1)}, u32[]{:S(2)}, u32[]{:S(2)}) collective-permute-start(bf16[128,1024]{1,0:T(8,128)(2,1)S(1)} %shard_map.151.refs_2_.refs_0_), channel_id=1, source_target_pairs={{0,8},{1,9},{2,10},{3,11},{4,12},{5,13},{6,14},{7,15},{8,0},{9,1},... | collective-permute-start | bytes 786440 | tf_op jit(solution)/shard_map/ppermute | solution.py:286
  58.1 8.4 %collective-permute-start.10 = (bf16[96,1024]{1,0:T(8,128)(2,1)S(1)}, bf16[96,1024]{1,0:T(8,128)(2,1)S(1)}, u32[]{:S(2)}, u32[]{:S(2)}) collective-permute-start(bf16[96,1024]{1,0:T(8,128)(2,1)S(1)} %get-tuple-element.89), channel_id=1, source_target_pairs={{0,4},{1,5},{2,6},{3,7},{4,0},{5,1},{6,2},{7,3},{8,12},{9,13},{10,... | collective-permute-start | bytes 589832 | tf_op jit(solution)/shard_map/ppermute | solution.py:286
  58.2 5.2 %collective-permute-start.11 = (bf16[64,1024]{1,0:T(8,128)(2,1)S(1)}, bf16[64,1024]{1,0:T(8,128)(2,1)S(1)}, u32[]{:S(2)}, u32[]{:S(2)}) collective-permute-start(bf16[64,1024]{1,0:T(8,128)(2,1)S(1)} %get-tuple-element.91), channel_id=1, source_target_pairs={{0,2},{1,3},{2,0},{3,1},{4,6},{5,7},{6,4},{7,5},{8,10},{9,11},{10,... | collective-permute-start | bytes 393224 | tf_op jit(solution)/shard_map/ppermute | solution.py:286
  62.2 5.0 %collective-permute-start.15 = (bf16[64,1024]{1,0:T(8,128)(2,1)S(1)}, bf16[64,1024]{1,0:T(8,128)(2,1)S(1)}, u32[]{:S(2)}, u32[]{:S(2)}) collective-permute-start(bf16[64,1024]{1,0:T(8,128)(2,1)S(1)} %get-tuple-element.93.refs_2_), channel_id=1, source_target_pairs={{0,2},{1,3},{2,0},{3,1},{4,6},{5,7},{6,4},{7,5},{8,10},{9,11},{10,... | collective-permute-start | bytes 393224 | tf_op jit(solution)/shard_map/ppermute | solution.py:286
  62.7 5.7 %collective-permute-start.14 = (bf16[64,1024]{1,0:T(8,128)(2,1)S(1)}, bf16[64,1024]{1,0:T(8,128)(2,1)S(1)}, u32[]{:S(2)}, u32[]{:S(2)}) collective-permute-start(bf16[64,1024]{1,0:T(8,128)(2,1)S(1)} %get-tuple-element.92.refs_4_.refs_0_), channel_id=1, source_target_pairs={{0,4},{1,5},{2,6},{3,7},{4,0},{5,1},{6,2},{7,3},{8,12},{9,13},{10,... | collective-permute-start | bytes 393224 | tf_op jit(solution)/shard_map/ppermute | solution.py:286
  66.5 14.9 %collective-permute-start.13 = (bf16[160,1024]{1,0:T(8,128)(2,1)S(1)}, bf16[160,1024]{1,0:T(8,128)(2,1)S(1)}, u32[]{:S(2)}, u32[]{:S(2)}) collective-permute-start(bf16[160,1024]{1,0:T(8,128)(2,1)S(1)} %shard_map.155.refs_4_.refs_0_), channel_id=1, source_target_pairs={{0,8},{1,9},{2,10},{3,11},{4,12},{5,13},{6,14},{7,15},{8,0},{9,1},... | collective-permute-start | bytes 983048 | tf_op jit(solution)/shard_map/ppermute | solution.py:286
  68.4 6.8 %collective-permute-start.16 = (bf16[128,1024]{1,0:T(8,128)(2,1)S(1)}, bf16[128,1024]{1,0:T(8,128)(2,1)S(1)}, u32[]{:S(2)}, u32[]{:S(2)}) collective-permute-start(bf16[128,1024]{1,0:T(8,128)(2,1)S(1)} %get-tuple-element.94.refs_0_.refs_4_), channel_id=1, source_target_pairs={{0,2},{1,3},{2,0},{3,1},{4,6},{5,7},{6,4},{7,5},{8,10},{9,11},{10,... | collective-permute-start | bytes 786440 | tf_op jit(solution)/shard_map/ppermute | solution.py:286
  69.4 11.9 %collective-permute-start.17 = (bf16[128,1024]{1,0:T(8,128)(2,1)S(1)}, bf16[128,1024]{1,0:T(8,128)(2,1)S(1)}, u32[]{:S(2)}, u32[]{:S(2)}) collective-permute-start(bf16[128,1024]{1,0:T(8,128)(2,1)S(1)} %get-tuple-element.95.refs_2_), channel_id=1, source_target_pairs={{0,4},{1,5},{2,6},{3,7},{4,0},{5,1},{6,2},{7,3},{8,12},{9,13},{10,... | collective-permute-start | bytes 786440 | tf_op jit(solution)/shard_map/ppermute | solution.py:286
  81.5 10.9 %collective-permute-start.22 = (bf16[512,1024]{1,0:T(8,128)(2,1)S(1)}, bf16[512,1024]{1,0:T(8,128)(2,1)S(1)}, u32[]{:S(2)}, u32[]{:S(2)}) collective-permute-start(bf16[512,1024]{1,0:T(8,128)(2,1)S(1)} %get-tuple-element.100.refs_0_), channel_id=1, source_target_pairs={{0,1},{1,0},{2,3},{3,2},{4,5},{5,4},{6,7},{7,6},{8,9},{9,8},{10,11... | collective-permute-start | bytes 3145736 | tf_op jit(solution)/shard_map/ppermute | solution.py:286
  81.5 7.3 %collective-permute-start.18 = (bf16[96,1024]{1,0:T(8,128)(2,1)S(1)}, bf16[96,1024]{1,0:T(8,128)(2,1)S(1)}, u32[]{:S(2)}, u32[]{:S(2)}) collective-permute-start(bf16[96,1024]{1,0:T(8,128)(2,1)S(1)} %get-tuple-element.96.refs_0_.refs_4_), channel_id=1, source_target_pairs={{0,4},{1,5},{2,6},{3,7},{4,0},{5,1},{6,2},{7,3},{8,12},{9,13},{10,... | collective-permute-start | bytes 589832 | tf_op jit(solution)/shard_map/ppermute | solution.py:286
  81.6 5.8 %collective-permute-start.19 = (bf16[64,1024]{1,0:T(8,128)(2,1)S(1)}, bf16[64,1024]{1,0:T(8,128)(2,1)S(1)}, u32[]{:S(2)}, u32[]{:S(2)}) collective-permute-start(bf16[64,1024]{1,0:T(8,128)(2,1)S(1)} %get-tuple-element.97.refs_2_), channel_id=1, source_target_pairs={{0,2},{1,3},{2,0},{3,1},{4,6},{5,7},{6,4},{7,5},{8,10},{9,11},{10,... | collective-permute-start | bytes 393224 | tf_op jit(solution)/shard_map/ppermute | solution.py:286
  88.9 10.7 %collective-permute-start.20 = (bf16[192,1024]{1,0:T(8,128)(2,1)S(1)}, bf16[192,1024]{1,0:T(8,128)(2,1)S(1)}, u32[]{:S(2)}, u32[]{:S(2)}) collective-permute-start(bf16[192,1024]{1,0:T(8,128)(2,1)S(1)} %get-tuple-element.98.refs_1_.refs_0_), channel_id=1, source_target_pairs={{0,2},{1,3},{2,0},{3,1},{4,6},{5,7},{6,4},{7,5},{8,10},{9,11},{10,... | collective-permute-start | bytes 1179656 | tf_op jit(solution)/shard_map/ppermute | solution.py:286
  90.6 7.6 %collective-permute-start.21 = (bf16[128,1024]{1,0:T(8,128)(2,1)S(1)}, bf16[128,1024]{1,0:T(8,128)(2,1)S(1)}, u32[]{:S(2)}, u32[]{:S(2)}) collective-permute-start(bf16[128,1024]{1,0:T(8,128)(2,1)S(1)} %get-tuple-element.99.refs_2_), channel_id=1, source_target_pairs={{0,4},{1,5},{2,6},{3,7},{4,0},{5,1},{6,2},{7,3},{8,12},{9,13},{10,... | collective-permute-start | bytes 786440 | tf_op jit(solution)/shard_map/ppermute | solution.py:286
  99.8 3.1 %collective-permute-start.23 = (bf16[640,1024]{1,0:T(8,128)(2,1)S(1)}, bf16[640,1024]{1,0:T(8,128)(2,1)S(1)}, u32[]{:S(2)}, u32[]{:S(2)}) collective-permute-start(bf16[640,1024]{1,0:T(8,128)(2,1)S(1)} %shard_map.162.refs_0_), channel_id=1, source_target_pairs={{0,1},{1,0},{2,3},{3,2},{4,5},{5,4},{6,7},{7,6},{8,9},{9,8},{10,11... | collective-permute-start | bytes 3932168 | tf_op jit(solution)/shard_map/ppermute | solution.py:286

commit v3 on v2

v3 whole, which is shorter than its diff:
```python
import functools
import math

import jax
import jax.numpy as jnp
from jax import lax
from jax.experimental import pallas as pl
from jax.experimental.pallas import tpu as pltpu
from jax.sharding import PartitionSpec as P

KAPPA = 0.2
KEPT = 80
PACKED = 48
BLOCK = 256
ROOM = 28
BF = jnp.bfloat16
F32 = jnp.float32
VMEM = pl.BlockSpec(memory_space=pltpu.VMEM)
ANY = pl.BlockSpec(memory_space=pl.ANY)
HBM = pl.BlockSpec(memory_space=pltpu.HBM)
Shape = jax.ShapeDtypeStruct


def contract_rows(left, right):
    return lax.dot_general(left, right, (((0,), (0,)), ((), ())), preferred_element_type=F32)


def times_transposed(left, right):
    return lax.dot_general(left, right, (((1,), (1,)), ((), ())), preferred_element_type=F32)


def bit_of(stride):
    return (lax.axis_index("tiles") // stride) % 2


def rows_at(index, rows):
    return pl.ds(pl.multiple_of(index * rows, rows), rows)


def rest_rows(n):
    return -(-(n + 3 * KEPT) // 256) * 256


def call(
    body, outs, args, after=None, carry=(), specs=None, out_specs=None, scratch=(), aliases=None, room=12
):
    outs, args = tuple(outs), tuple(args)
    specs = list(specs or [VMEM] * len(args))
    out_specs = list(out_specs or [VMEM] * len(outs))
    count, made = len(args), len(outs)
    aliases = dict(aliases or {})
    extra = (() if after is None else (after,)) + tuple(carry)
    for i, array in enumerate(carry):
        aliases[count + len(extra) - len(carry) + i] = made + i
    plain = body

    def body(*refs):
        given = refs[:count]
        rest = refs[count + len(extra) :]
        plain(*given, *rest[:made], *rest[made + len(carry) :])

    return pl.pallas_call(
        body,
        out_shape=outs + tuple(Shape(a.shape, a.dtype) for a in carry),
        in_specs=specs + [ANY] * len(extra),
        out_specs=tuple(out_specs + [ANY] * len(carry)),
        scratch_shapes=scratch,
        input_output_aliases=aliases,
        compiler_params=pltpu.CompilerParams(vmem_limit_bytes=room * 2**20),
        cost_estimate=pl.CostEstimate(flops=1, bytes_accessed=1, transcendentals=0),
    )(*args, *extra)


def activate(v):
    s = 0.5 + 0.5 * jnp.tanh(0.5 * v)
    act = v * s
    return act.astype(BF), (s + act * (1.0 - s)).astype(BF)


def step_body(
    depth, near, far, owner, warm_in, brine_in, desired_in, stepped, pack, warm, brine, desired, sems
):
    lon, lat, levels = warm.shape
    cols = lon * lat
    copies = [
        pltpu.make_async_copy(source, ref, sems.at[i])
        for i, (source, ref) in enumerate(
            ((warm_in, warm), (brine_in, brine), (desired_in, desired))
        )
    ]
    for copy in copies:
        copy.start()
    odd = bit_of(1) == 1
    before = jnp.where(odd, near[...], far[...])
    after = jnp.where(odd, far[...], near[...])
    level = lax.broadcasted_iota(jnp.int32, (lon, lat, levels), 2).astype(F32)
    row = lax.broadcasted_iota(jnp.int32, (lon, lat, levels), 1)
    wet = (level < depth[...]).astype(F32)
    wet_b = (level[:1] < before[2]).astype(F32)
    wet_a = (level[:1] < after[2]).astype(F32)
    wet_e = jnp.concatenate([wet[1:], wet_a], 0)
    wet_w = jnp.concatenate([wet_b, wet[:-1]], 0)
    wet_n = jnp.where(row < lat - 1, pltpu.roll(wet, lat - 1, 1), 0.0)
    wet_s = jnp.where(row > 0, pltpu.roll(wet, 1, 1), 0.0)
    lane = lax.broadcasted_iota(jnp.int32, (cols, levels), 1)
    for copy in copies:
        copy.wait()
    target = desired[...].reshape(cols, levels).astype(F32)
    for i, ref in enumerate((warm, brine)):
        q = ref[...]
        total = wet_e * (jnp.concatenate([q[1:], after[i]], 0) - q)
        total = total + wet_w * (jnp.concatenate([before[i], q[:-1]], 0) - q)
        total = total + wet_n * (pltpu.roll(q, lat - 1, 1) - q)
        total = total + wet_s * (pltpu.roll(q, 1, 1) - q)
        out = q + KAPPA * wet * total
        stepped[i] = out
        group = (out * wet).reshape(cols, levels)
        if i == 0:
            group = jnp.where(lane == KEPT - 2, owner[...].reshape(cols, levels), group)
            group = jnp.where(lane == KEPT - 1, depth[...].reshape(cols, levels), group)
        beside = pltpu.roll(target, (KEPT - i * PACKED) % levels, 1)
        group = jnp.where(lane >= KEPT, beside, group)
        pack[:, i * levels : (i + 1) * levels] = group.astype(BF)


def weight_grad(pairs, at):
    total = None
    for act, delta in pairs:
        term = contract_rows(act[:, at], delta[...])
        total = term if total is None else total + term
    return total.astype(BF)


def back_through(delta, weights, slope, out):
    for j in range(0, out.shape[1], BLOCK):
        back = times_transposed(delta, weights[j : j + BLOCK])
        out[:, j : j + BLOCK] = (back * slope[:, j : j + BLOCK].astype(F32)).astype(BF)


def train(scale, pack, interior, readout, inferred, outs, scratch, weights):
    act0, act1, slope0, slope1, delta2, feat, rest = outs
    w_int, w_out, act2, slope2, sems = scratch
    cols = pack.shape[0]
    levels = pack.shape[1] // 2
    hid = readout.shape[0]
    deep = interior.shape[0]
    start_weights, w_lead = weights
    start_weights()
    copies = [
        pltpu.make_async_copy(interior.at[i], w_int.at[i], sems.at[i]) for i in range(deep)
    ]
    copies.append(pltpu.make_async_copy(readout, w_out, sems.at[deep]))
    for copy in copies:
        copy.start()
    groups = [pack[:, i * levels : (i + 1) * levels].astype(F32) for i in range(2)]
    lane = lax.broadcasted_iota(jnp.int32, (cols, levels), 1)
    own = lane.astype(F32) == groups[0][:, KEPT - 2 : KEPT - 1] + KEPT
    wet = lane.astype(F32) < groups[0][:, KEPT - 1 : KEPT]
    target = jnp.where(
        lane < PACKED,
        pltpu.roll(groups[0], levels - KEPT, 1),
        pltpu.roll(groups[1], levels - KEPT + PACKED, 1),
    )
    for i, group in enumerate(groups):
        hot = jnp.where(own, 1.0, 0.0)
        feat[:, i * levels : (i + 1) * levels] = jnp.where(lane < KEPT - 2, group, hot).astype(BF)
    w_lead = w_lead()
    for layer, (left, right, act, slope) in enumerate(
        (
            (feat, w_lead, act0, slope0),
            (act0, w_int.at[0], act1, slope1),
            (act1, w_int.at[1], act2, slope2),
        )
    ):
        if layer:
            copies[layer - 1].wait()
        for j in range(0, hid, BLOCK):
            pre = jnp.dot(left[...], right[:, j : j + BLOCK], preferred_element_type=F32)
            act[:, j : j + BLOCK], slope[:, j : j + BLOCK] = activate(pre)
    copies[deep].wait()
    output = jnp.dot(act2[...], w_out[...], preferred_element_type=F32)
    if inferred is not None:
        inferred[...] = output.astype(BF).reshape(inferred.shape)
    err = jnp.where(wet, (output - target) * scale, 0.0).astype(BF)
    back_through(err, w_out, slope2, delta2)
    rest[...] = contract_rows(err, act2[...])[:KEPT]


def forward_body(n, scale, pack, bias, leading, interior, readout, *refs):
    inferred, w_lead, refs = refs[0], refs[1], refs[2:]
    copy = pltpu.make_async_copy(leading, w_lead, refs[-1].at[interior.shape[0] + 1])

    def weights():
        copy.wait()
        for j in range(bias.shape[1]):
            value = bias[:, j]
            high = value.astype(BF)
            at = slice(j * bias.shape[2], (j + 1) * bias.shape[2])
            low = (value - high.astype(F32)).astype(BF)
            w_lead[KEPT : KEPT + n, at] = high
            w_lead[bias.shape[2] + KEPT : bias.shape[2] + KEPT + n, at] = low
        return w_lead

    train(scale, pack, interior, readout, inferred, refs[:7], refs[7:], (copy.start, weights))


def partner_body(
    scale, pack, w_lead, interior, readout, act1, delta2, *refs
):
    outs, other, scratch = refs[:7], refs[7], refs[8:]
    train(
        scale, pack, interior, readout, None, outs, scratch, (lambda: None, lambda: w_lead)
    )
    rows = other.shape[0]
    at = pl.ds(pl.multiple_of((1 - bit_of(1)) * 2 * rows + bit_of(4) * rows, rows), rows)
    other[...] = weight_grad(((act1, delta2), (outs[1], outs[4])), at)


def middle_body(
    interior, act1, delta2, act1_p, delta2_p, slope1, mine, delta1, w_int, sems
):
    copy = pltpu.make_async_copy(interior.at[1], w_int, sems.at[0])
    copy.start()
    rows = mine.shape[0]
    at = pl.ds(pl.multiple_of(bit_of(1) * 2 * rows + bit_of(4) * rows, rows), rows)
    mine[...] = weight_grad(((act1, delta2), (act1_p, delta2_p)), at)
    copy.wait()
    back_through(delta2[...], w_int, slope1, delta1)


def first_body(
    n,
    interior,
    feat,
    act0,
    slope0,
    delta1,
    rest_in,
    feat_p,
    act0_p,
    slope0_p,
    slope1_p,
    delta2_p,
    rest_p,
    mine,
    other_0,
    other_1,
    other_2,
    other_3,
    delta1_p,
    delta0,
    delta0_p,
    rest,
    spare,
    w_int,
    sems,
):
    levels = feat.shape[1] // 2
    hid = slope0.shape[1]
    copies = [
        pltpu.make_async_copy(interior.at[i], w_int.at[i], sems.at[i])
        for i in range(interior.shape[0])
    ]
    for copy in reversed(copies):
        copy.start()
    copies[1].wait()
    back_through(delta2_p[...], w_int.at[1], slope1_p, delta1_p)
    copies[0].wait()
    back_through(delta1[...], w_int.at[0], slope0, delta0)
    back_through(delta1_p[...], w_int.at[0], slope0_p, delta0_p)
    total = contract_rows(feat[...], delta0[...]) + contract_rows(feat_p[...], delta0_p[...])
    lead = total.astype(BF)
    a = KEPT + n
    rest[:a] = lead[:a]
    rest[a : a + KEPT] = lead[levels : levels + KEPT]
    rest[a + KEPT : a + 2 * KEPT] = (rest_in[...] + rest_p[...]).astype(BF)
    rows = rest.shape[0]
    if rows > a + 2 * KEPT:
        rest[a + 2 * KEPT :] = jnp.zeros((rows - a - 2 * KEPT, hid), BF)
    bit, z = bit_of(1), bit_of(4)
    quarter, part = hid // 8, rows // 8
    for ref, b in ((spare, 1 - bit), (mine, bit)):
        at = pl.ds(pl.multiple_of((b * 2 + z) * 2 * quarter, 2 * quarter), 2 * quarter)
        got = weight_grad(((act0, delta1), (act0_p, delta1_p)), at)
        for y in range(2):
            base = y * (quarter + part)
            ref[base : base + quarter] = got[y * quarter : (y + 1) * quarter]
            from_rest = pl.ds(pl.multiple_of((b * 2 + z) * 2 * part + y * part, part), part)
            ref[base + quarter : base + quarter + part] = rest[from_rest]
    for i, ref in enumerate((other_0, other_1, other_2, other_3)):
        ref[...] = spare[i * ref.shape[0] : (i + 1) * ref.shape[0]]


def split_body(count, mine, *refs):
    got, keep, sends, total = refs[:count], refs[count], refs[count + 1 : -1], refs[-1]
    base = 0
    for ref in got:
        at = slice(base, base + ref.shape[0])
        total[at] = mine[at] + ref[...]
        base += ref.shape[0]
    bit = bit_of(2)
    rows = keep.shape[0]
    keep[...] = total[rows_at(bit, rows)]
    for i, send in enumerate(sends):
        part = send.shape[0]
        at = pl.ds(pl.multiple_of((1 - bit) * rows + i * part, 16), part)
        send[...] = total[at]


def pair_body(keep, *refs):
    got, out = refs[:-1], refs[-1]
    base = 0
    for ref in got:
        at = slice(base, base + ref.shape[0])
        out[at] = keep[at] + ref[...]
        base += ref.shape[0]


def unpair_body(x, got, a, b):
    rows = a.shape[0]
    a[...] = x[:rows] + got[:rows]
    b[...] = x[rows:] + got[rows:]


def join_body(a, got_a, b, got_b, a_out, b_out):
    for stride, x, got, out in ((4, a, got_a, a_out), (2, b, got_b, b_out)):
        bit = bit_of(stride)
        rows = x.shape[0]
        out[rows_at(bit, rows)] = x[...]
        out[rows_at(1 - bit, rows)] = got[...]


def whole_body(a, got_a, b, got_b, out):
    rows = a.shape[0] // 2
    y, z = bit_of(2), bit_of(4)

    def at(z, y, low):
        return pl.ds(pl.multiple_of((z * 2 + y) * 2 * rows + low * rows, 16), rows)

    for i in range(2):
        own = slice(i * rows, (i + 1) * rows)
        out[at(i, y, 0)] = a[own]
        out[at(i, 1 - y, 0)] = got_a[own]
        out[at(z, i, 1)] = b[own]
        out[at(1 - z, i, 1)] = got_b[own]


def swap(x, stride):
    n = lax.axis_size("tiles")
    return lax.ppermute(x, "tiles", [(t, t ^ stride) for t in range(n)])


def bf(rows, like):
    return Shape((rows, like.shape[1]), BF)


class Sum:
    def __init__(self, mine, others, sends):
        self.mine, self.got = mine, [swap(other, 1) for other in others]
        self.rows, self.sends = mine.shape[0], sends

    def step(self, body, rows, args, after, carry=(), scratch=()):
        outs = [bf(r, self.mine) for r in rows]
        made = call(body, outs, args, after, carry, scratch=scratch)
        return made[: len(rows)], made[len(rows) :]

    def split(self, after, carry=()):
        half = self.rows // 2
        (keep, *sends), carry = self.step(
            functools.partial(split_body, len(self.got)),
            [half] + [half // self.sends] * self.sends,
            (self.mine, *self.got),
            after,
            carry,
            [pltpu.VMEM(self.mine.shape, BF)],
        )
        self.parts = (keep, *[swap(send, 2) for send in sends])
        return keep, *carry

    def pair(self, after, carry=()):
        (m,), carry = self.step(pair_body, [self.rows // 2], self.parts, after, carry)
        token, stride = m, 8
        while 2 * stride < lax.axis_size("tiles"):
            m = m + swap(m, stride)
            stride *= 2
        self.parts = m, swap(m, stride)
        return token, *carry

    def unpair(self, after, carry=()):
        (a, b), carry = self.step(unpair_body, [self.rows // 4] * 2, self.parts, after, carry)
        self.parts = a, swap(a, 4), b, swap(b, 2)
        return a, *carry

    def join(self, after, carry=()):
        (a, b), carry = self.step(join_body, [self.rows // 2] * 2, self.parts, after, carry)
        self.parts = a, swap(a, 2), b, swap(b, 4)
        return a, *carry

    def whole(self, after, carry=()):
        (x,), carry = self.step(whole_body, [2 * self.rows], self.parts, after, carry)
        return x, *carry


def place_rows(x, half, slab, out, wide, sems):
    count = x.shape[0] // 4
    rows = wide.shape[0] // 4
    copies = []
    for i in range(4):
        at = slice(i * rows, (i + 1) * rows)
        wide[at] = x[i * count : i * count + rows].astype(F32)
        to = pl.ds(pl.multiple_of(half * 4 * rows + i * rows, rows), rows)
        copies.append(pltpu.make_async_copy(wide.at[at], out.at[slab, to], sems.at[i]))
        copies[-1].start()
    return copies


def place_body(slab, flip, *refs):
    x, out, token, wide, sems = refs[0], refs[-4], refs[-3], refs[-2], refs[-1]
    copies = place_rows(x, (bit_of(1) + flip) % 2, slab, out, wide, sems)
    token[...] = jnp.zeros(token.shape, F32)
    for copy in copies:
        copy.wait()


def place(slab, flip, x, shape, held, after):
    hid = shape.shape[1]
    return call(
        functools.partial(place_body, slab, flip),
        (shape, Shape((8, 128), F32)),
        (x,) if held is None else (x, held),
        after,
        specs=[VMEM] if held is None else [VMEM, HBM],
        out_specs=(HBM, VMEM),
        scratch=[pltpu.VMEM((hid // 2, hid), F32), pltpu.SemaphoreType.DMA((4,))],
        aliases={} if held is None else {1: 0},
    )


def finish_body(n, x, got, held, out, lead_out, readout_out, own_out, wide, rest, sems):
    hid = out.shape[1]
    levels = lead_out.shape[0] // 2
    bit = bit_of(1)
    copies = place_rows(got, 1 - bit, 0, out, wide, sems)
    quarter, part = hid // 8, rest.shape[0] // 8
    for ref, b in ((x, bit), (got, 1 - bit)):
        for i in range(4):
            at = pl.ds(pl.multiple_of(b * 4 * part + i * part, part), part)
            base = i * (quarter + part) + quarter
            rest[at] = ref[base : base + part].astype(F32)
    a = KEPT + n
    zeros = jnp.zeros((levels - KEPT, hid), F32)
    lead_out[: KEPT - 2] = rest[: KEPT - 2]
    lead_out[KEPT - 2 : levels] = jnp.zeros((levels - KEPT + 2, hid), F32)
    lead_out[levels : levels + KEPT] = rest[a : a + KEPT]
    lead_out[levels + KEPT :] = zeros
    own_out[...] = rest[pl.ds(KEPT + lax.axis_index("tiles"), 1)]
    readout_out[...] = jnp.concatenate([rest[a + KEPT : a + 2 * KEPT], zeros], 0).T
    for copy in copies:
        copy.wait()


def local(
    warmth,
    brine,
    flags,
    tally,
    assigned,
    desired,
    intercepts,
    leading,
    interior,
    readout,
):
    n = lax.axis_size("tiles")
    lon, lat, levels = warmth.shape
    cols = lon * lat
    hid = leading.shape[1]
    scale = 1.0 / math.sqrt(cols * n)

    wide = (lon, lat, levels)
    depth = jnp.where(flags > 0, tally, 0).astype(F32)
    depth = jnp.broadcast_to(depth[:, :, None], wide)
    owner = jnp.broadcast_to(assigned[:, :, None].astype(F32), wide)
    odd = bit_of(1) == 1
    first = jnp.stack([warmth[:1], brine[:1], depth[:1]])
    last = jnp.stack([warmth[-1:], brine[-1:], depth[-1:]])
    near = swap(jnp.where(odd, first, last), 1)
    pairs = [(t, (t + 1) % n if t % 2 else (t - 1) % n) for t in range(n)]
    far = lax.ppermute(jnp.where(odd, last, first), "tiles", pairs)
    bias = lax.all_to_all(
        jnp.broadcast_to(intercepts.reshape(1, hid // 128, 128), (n, hid // 128, 128)),
        "tiles",
        split_axis=0,
        concat_axis=0,
        tiled=True,
    )
    warmth, brine, desired, leading, interior, readout = [
        pltpu.with_memory_space_constraint(a, pltpu.HBM)
        for a in (warmth, brine, desired, leading, interior, readout)
    ]
    stepped, pack = call(
        step_body,
        (Shape((2,) + wide, F32), Shape((cols, 2 * levels), BF)),
        (depth, near, far, owner, warmth, brine, desired),
        bias,
        specs=[VMEM] * 4 + [HBM] * 3,
        scratch=[
            pltpu.VMEM(wide, F32),
            pltpu.VMEM(wide, F32),
            pltpu.VMEM(wide, BF),
            pltpu.SemaphoreType.DMA((3,)),
        ],
    )
    pack_p = swap(pack, 4)
    act = Shape((cols, hid), BF)
    one = pltpu.VMEM(act.shape, BF)
    sem = pltpu.SemaphoreType.DMA((interior.shape[0] + 2,))
    trained = (act,) * 5 + (Shape(pack.shape, BF), Shape((KEPT, hid), F32))
    scratch = [pltpu.VMEM(interior.shape, BF), pltpu.VMEM(readout.shape, BF), one, one, sem]
    inferred, w_lead, act0, act1, slope0, slope1, delta2, feat, rest = call(
        functools.partial(forward_body, n, scale),
        (Shape(wide, BF), Shape(leading.shape, BF)) + trained,
        (pack, bias, leading, interior, readout),
        specs=[VMEM] * 2 + [HBM] * 3,
        scratch=scratch,
        room=ROOM,
    )
    half = Shape((hid // 4, hid), BF)
    act0_p, act1_p, slope0_p, slope1_p, delta2_p, feat_p, rest_p, other = call(
        functools.partial(partner_body, scale),
        trained + (half,),
        (pack_p, w_lead, interior, readout, act1, delta2),
        specs=[VMEM] * 2 + [HBM] * 2 + [VMEM] * 2,
        scratch=scratch,
        room=ROOM,
    )
    mine, delta1 = call(
        middle_body,
        (half, act),
        (interior, act1, delta2, act1_p, delta2_p, slope1),
        specs=[HBM] + [VMEM] * 5,
        scratch=[pltpu.VMEM((hid, hid), BF), sem],
        room=ROOM,
    )
    top = Sum(mine, [other], 1)
    (token,) = top.split(delta1)
    rows = rest_rows(n)
    part = Shape((hid // 4 + rows // 4, hid), BF)
    mine, *others = call(
        functools.partial(first_body, n),
        (part,) + (bf(part.shape[0] // 4, part),) * 4,
        (
            interior,
            feat,
            act0,
            slope0,
            delta1,
            rest,
            feat_p,
            act0_p,
            slope0_p,
            slope1_p,
            delta2_p,
            rest_p,
        ),
        token,
        specs=[HBM] + [VMEM] * 11,
        scratch=[
            *[one] * 3,
            pltpu.VMEM((rows, hid), BF),
            pltpu.VMEM(part.shape, BF),
            pltpu.VMEM(interior.shape, BF),
            sem,
        ],
        room=ROOM,
    )
    low = Sum(mine, others, 2)
    (token,) = top.pair(mine)
    (token,) = low.split(token)
    (token,) = top.unpair(token)
    (token,) = low.pair(token)
    (token,) = top.join(token)
    (token,) = low.unpair(token)
    (x,) = top.whole(token)
    grads = Shape((interior.shape[0], hid, hid), F32)
    token, x = low.join(None, [x])
    held, token = place(1, 0, x, grads, None, token)
    held, token = place(1, 1, swap(x, 1), grads, held, token)
    (y,) = low.whole(token)
    held, _ = place(0, 0, y, grads, held, None)
    interior_out, lead_out, readout_out, own_out = call(
        functools.partial(finish_body, n),
        (
            grads,
            Shape((2 * levels, hid), F32),
            Shape((hid, levels), F32),
            Shape((1, hid), F32),
        ),
        (y, swap(y, 1), held),
        specs=[VMEM, VMEM, HBM],
        out_specs=(HBM, VMEM, VMEM, VMEM),
        scratch=[
            pltpu.VMEM((hid // 2, hid), F32),
            pltpu.VMEM((rows, hid), F32),
            pltpu.SemaphoreType.DMA((4,)),
        ],
        aliases={2: 0},
    )
    return stepped, inferred, lead_out, interior_out, readout_out, own_out


def solution(mesh):
    part = ("groups", "tiles")
    return jax.shard_map(
        local,
        mesh=mesh,
        in_specs=(
            P(part, None, None),
            P(part, None, None),
            P(part, None),
            P(part, None),
            P(part, None),
            P(part, None, None),
            P(part, None),
            P(),
            P(),
            P(),
        ),
        out_specs=(
            P(None, part, None, None),
            P(part, None, None),
            P("groups", None),
            P(None, "groups", None),
            P("groups", None),
            P(part, None),
        ),
        check_vma=False,
    )
```

time: 106 us -> 106 us (level)
  waiting for transfers between devices: 54.2 us -> 39.7 us
  Pallas kernels: 22.7 us -> 34.3 us
  starting transfers between devices: 23.8 us -> 26.3 us
    pallas_call x20 -> x19, Pallas kernels: 22.7 us -> 34.3 us  [call(): pl.pallas_call(body, out_shape=outs + tuple((Shape(a.shape, a.dtype) for...]
    ppermute x22, waiting for transfers between devices: 49.5 us -> 38.5 us  [swap(): return lax.ppermute(x, 'tiles', [(t, t ^ stride) for t in range(n)])]
    all_to_all x1, waiting for transfers between devices: 4.73 us -> 0.01 us  [local(): lax.all_to_all(jnp.broadcast_to(intercepts.reshape(1, hid // 128, 128), (...]
    all_to_all x1, starting transfers between devices: 3.68 us -> 7.39 us  [local(): lax.all_to_all(jnp.broadcast_to(intercepts.reshape(1, hid // 128, 128), (...]
    ppermute x2 -> x1, waiting for transfers between devices: 0.01 us -> 1.14 us  [local(): far = lax.ppermute(jnp.where(odd, last, first), 'tiles', pairs)]
    ppermute x2 -> x1, starting transfers between devices: 5.46 us -> 4.43 us  [local(): far = lax.ppermute(jnp.where(odd, last, first), 'tiles', pairs)]
  transfers between devices with their start and end apart: 25 -> 24, of which waited for: 18 -> 12; matrix products, arithmetic and copies ran while one was open for 2% -> 2% of each run, Pallas kernels for 12% -> 21%
where the time goes in v3:
time: 106 us; the launch traced here: 105 us
  waiting for transfers between devices  39.7 us (37%)
  Pallas kernels  34.3 us (32%)
  starting transfers between devices  26.3 us (25%)
  local copies, waits for them, and re-layouts  2.49 us (2%)
  other arithmetic  1.43 us (1%)
  between operations  1.07 us (1%)
    ppermute x22, waiting for transfers between devices, swap(): return lax.ppermute(x, 'tiles', [(t, t ^ stride) for t in range(n)])  38.5 us
    pallas_call x19, Pallas kernels, call(): pl.pallas_call(body, out_shape=outs + tuple((Shape(a.shape, a.dtype) for...  34.3 us
    ppermute x22, starting transfers between devices, swap(): return lax.ppermute(x, 'tiles', [(t, t ^ stride) for t in range(n)])  14.5 us
    all_to_all x1, starting transfers between devices, local(): lax.all_to_all(jnp.broadcast_to(intercepts.reshape(1, hid // 128, 128), (...  7.39 us
    ppermute x1, starting transfers between devices, local(): far = lax.ppermute(jnp.where(odd, last, first), 'tiles', pairs)  4.43 us
  transfers between devices with their start and end apart: 24, of which 12 were waited for; matrix products, arithmetic and copies ran while one was open for 2% of the time, Pallas kernels for 21%

profile of v3, /device:TPU:0, one launch (start us, length us, event | category | flops | bytes accessed | tf_op | source)
XLA Modules:
  0.0 105.2 jit_solution(12128700940350415998)
XLA Ops:
  0.6 1.3 %broadcast_in_dim.24 = f32[16,8,128]{2,1,0:T(8,128)} broadcast(f32[8,128]{1,0:T(8,128)} %bitcast.13), dimensions={1,2} | broadcast | bytes 69632 | tf_op jit(solution)/shard_map/broadcast_in_dim | solution.py:491
  2.0 7.4 %all-to-all-start = ((f32[16,8,128]{2,1,0:T(8,128)}), f32[16,8,128]{2,1,0:T(8,128)S(1)}, u32[]{:S(2)}, u32[]{:S(2)}) async-start(f32[16,8,128]{2,1,0:T(8,128)} %broadcast_in_dim.24), calls=%async_computation | async-start | bytes 131072 | tf_op jit(solution)/shard_map/all_to_all | solution.py:490
  9.4 0.7 select_convert_fusion
  10.1 0.8 slice_bitcast_fusion.2
  11.0 4.4 %collective-permute-start.1 = (f32[3,1,32,128]{3,2,1,0:T(8,128)S(1)}, f32[3,1,32,128]{3,2,1,0:T(8,128)S(1)}, u32[]{:S(2)}, u32[]{:S(2)}) collective-permute-start(f32[3,1,32,128]{3,2,1,0:T(8,128)S(1)} %get-tuple-element.108), channel_id=1, source_target_pairs={{0,15},{1,2},{2,1},{3,4},{4,3},{5,6},{6,5},{7,8},{8,7},{9,10},{10,... | collective-permute-start | bytes 147464 | tf_op jit(solution)/shard_map/ppermute | solution.py:489
  15.5 0.7 convert_element_type.8
  16.2 1.1 %collective-permute-done.1.refs_2_ = f32[3,1,32,128]{3,2,1,0:T(8,128)S(1)} collective-permute-done((f32[3,1,32,128]{3,2,1,0:T(8,128)S(1)}, f32[3,1,32,128]{3,2,1,0:T(8,128)S(1)}, u32[]{:S(2)}, u32[]{:S(2)}) %collective-permute-start.1) | collective-permute-done | bytes 49184 | tf_op jit(solution)/shard_map/ppermute | solution.py:489
  17.6 2.3 %shard_map.145 = (f32[2,16,32,128]{3,2,1,0:T(8,128)}, bf16[512,256]{1,0:T(8,128)(2,1)S(1)}) custom-call(f32[16,32,128]{2,1,0:T(8,128)S(1)} %broadcast_in_dim.10.refs_0_, f32[3,1,32,128]{3,2,1,0:T(8,128)S(1)} %collective-permute-done.refs_1_, f32[3,1,32,128]{3,2,1,0:T(8,128)S(1)} %collective-permute-done.1.refs_2_, ...), custom_call_target="tpu_custom_call" | custom-call | flops 1 | bytes 1 | tf_op jit(solution)/shard_map/pallas_call | solution.py:62
  20.1 6.8 %shard_map.146 = (bf16[16,32,128]{2,1,0:T(8,128)(2,1)}, bf16[256,1024]{1,0:T(8,128)(2,1)S(1)}, bf16[512,1024]{1,0:T(8,128)(2,1)S(1)}, bf16[512,1024]{1,0:T(8,128...) custom-call(bf16[512,256]{1,0:T(8,128)(2,1)S(1)} %get-tuple-element., ...), custom_call_target="tpu_custom_call" | custom-call | flops 1 | bytes 1 | tf_op jit(solution)/shard_map/pallas_call | solution.py:62
  26.9 0.8 collective-permute-done.2.refs_0_
  27.7 6.9 %shard_map.147 = (bf16[512,1024]{1,0:T(8,128)(2,1)S(1)}, bf16[512,1024]{1,0:T(8,128)(2,1)S(1)}, bf16[512,1024]{1,0:T(8,128)(2,1)S(1)}, bf16[512,1024]{1,0:T(8,12...) custom-call(bf16[512,256]{1,0:T(8,128)(2,1)S(1)} %collective-permute, ...), custom_call_target="tpu_custom_call" | custom-call | flops 1 | bytes 1 | tf_op jit(solution)/shard_map/pallas_call | solution.py:62
  34.7 3.2 %shard_map.148 = (bf16[256,1024]{1,0:T(8,128)(2,1)S(1)}, bf16[512,1024]{1,0:T(8,128)(2,1)S(1)}) custom-call(bf16[2,1024,1024]{2,1,0:T(8,128)(2,1)} %refs_0_.3, bf16[512,1024]{1,0:T(8,128)(2,1)S(1)} %get-tuple-element.61.refs_4_.refs_1_, bf16[512,1024]{1,0:T(8,128)(2,1)S(1)} %get-tuple-element.62.refs_5_.refs_2_, ...), custom_call_target="tpu_custom_call" | custom-call | flops 1 | bytes 1 | tf_op jit(solution)/shard_map/pallas_call | solution.py:62
  38.0 0.8 collective-permute-start.8
  38.8 7.0 %shard_map.150 = (bf16[320,1024]{1,0:T(8,128)(2,1)S(1)}, bf16[80,1024]{1,0:T(8,128)(2,1)S(1)}, bf16[80,1024]{1,0:T(8,128)(2,1)S(1)}, bf16[80,1024]{1,0:T(8,128)(2,1)S(1)}, bf16[80,1024]{1,0:T(8,128)(2,1)S(1)}) custom-call(bf16[2,1024,1024]{2,1,0:T(8,128)(2,1)} %refs_0_.3, bf16[512,256]{1,0:T(8,128)(2,1)S(1)} %get-tuple-element.58.refs_1_, ...), custom_call_target="tpu_custom_call" | custom-call | flops 1 | bytes 1 | tf_op jit(solution)/shard_map/pallas_call | solution.py:62
  46.9 3.9 %collective-permute-start.11 = (bf16[128,1024]{1,0:T(8,128)(2,1)S(1)}, bf16[128,1024]{1,0:T(8,128)(2,1)S(1)}, u32[]{:S(2)}, u32[]{:S(2)}) collective-permute-start(bf16[128,1024]{1,0:T(8,128)(2,1)S(1)} %shard_map.151.refs_5_.refs_0_), channel_id=1, source_target_pairs={{0,8},{1,9},{2,10},{3,11},{4,12},{5,13},{6,14},{7,15},{8,0},{9,1},... | collective-permute-start | bytes 786440 | tf_op jit(solution)/shard_map/ppermute | solution.py:350
  51.2 1.8 %collective-permute-start.10 = (bf16[80,1024]{1,0:T(8,128)(2,1)S(1)}, bf16[80,1024]{1,0:T(8,128)(2,1)S(1)}, u32[]{:S(2)}, u32[]{:S(2)}) collective-permute-start(bf16[80,1024]{1,0:T(8,128)(2,1)S(1)} %get-tuple-element.85), channel_id=1, source_target_pairs={{0,2},{1,3},{2,0},{3,1},{4,6},{5,7},{6,4},{7,5},{8,10},{9,11},{10,... | collective-permute-start | bytes 491528 | tf_op jit(solution)/shard_map/ppermute | solution.py:350
  53.1 9.7 %collective-permute-done.11.refs_1_ = bf16[128,1024]{1,0:T(8,128)(2,1)S(1)} collective-permute-done((bf16[128,1024]{1,0:T(8,128)(2,1)S(1)}, bf16[128,1024]{1,0:T(8,128)(2,1)S(1)}, u32[]{:S(2)}, u32[]{:S(2)}) %collective-permute-start.11) | collective-permute-done | bytes 262176 | tf_op jit(solution)/shard_map/ppermute | solution.py:350
  63.4 2.7 %collective-permute-start.13 = (bf16[64,1024]{1,0:T(8,128)(2,1)S(1)}, bf16[64,1024]{1,0:T(8,128)(2,1)S(1)}, u32[]{:S(2)}, u32[]{:S(2)}) collective-permute-start(bf16[64,1024]{1,0:T(8,128)(2,1)S(1)} %get-tuple-element.86.refs_3_.refs_0_), channel_id=1, source_target_pairs={{0,4},{1,5},{2,6},{3,7},{4,0},{5,1},{6,2},{7,3},{8,12},{9,13},{10,... | collective-permute-start | bytes 393224 | tf_op jit(solution)/shard_map/ppermute | solution.py:350
  66.2 2.3 %collective-permute-done.14.refs_3_ = bf16[64,1024]{1,0:T(8,128)(2,1)S(1)} collective-permute-done((bf16[64,1024]{1,0:T(8,128)(2,1)S(1)}, bf16[64,1024]{1,0:T(8,128)(2,1)S(1)}, u32[]{:S(2)}, u32[]{:S(2)}) %collective-permute-start.14) | collective-permute-done | bytes 131104 | tf_op jit(solution)/shard_map/ppermute | solution.py:350
  68.5 4.8 %collective-permute-done.13.refs_1_ = bf16[64,1024]{1,0:T(8,128)(2,1)S(1)} collective-permute-done((bf16[64,1024]{1,0:T(8,128)(2,1)S(1)}, bf16[64,1024]{1,0:T(8,128)(2,1)S(1)}, u32[]{:S(2)}, u32[]{:S(2)}) %collective-permute-start.13) | collective-permute-done | bytes 131104 | tf_op jit(solution)/shard_map/ppermute | solution.py:350
  73.3 2.5 %collective-permute-start.18 = (bf16[128,1024]{1,0:T(8,128)(2,1)S(1)}, bf16[128,1024]{1,0:T(8,128)(2,1)S(1)}, u32[]{:S(2)}, u32[]{:S(2)}) collective-permute-start(bf16[128,1024]{1,0:T(8,128)(2,1)S(1)} %get-tuple-element.91.refs_2_), channel_id=1, source_target_pairs={{0,4},{1,5},{2,6},{3,7},{4,0},{5,1},{6,2},{7,3},{8,12},{9,13},{10,... | collective-permute-start | bytes 786440 | tf_op jit(solution)/shard_map/ppermute | solution.py:350
  75.9 3.9 %collective-permute-done.12.refs_1_ = bf16[160,1024]{1,0:T(8,128)(2,1)S(1)} collective-permute-done((bf16[160,1024]{1,0:T(8,128)(2,1)S(1)}, bf16[160,1024]{1,0:T(8,128)(2,1)S(1)}, u32[]{:S(2)}, u32[]{:S(2)}) %collective-permute-start.12) | collective-permute-done | bytes 327712 | tf_op jit(solution)/shard_map/ppermute | solution.py:350
  80.0 5.4 %collective-permute-done.18.refs_3_ = bf16[128,1024]{1,0:T(8,128)(2,1)S(1)} collective-permute-done((bf16[128,1024]{1,0:T(8,128)(2,1)S(1)}, bf16[128,1024]{1,0:T(8,128)(2,1)S(1)}, u32[]{:S(2)}, u32[]{:S(2)}) %collective-permute-start.18) | collective-permute-done | bytes 262176 | tf_op jit(solution)/shard_map/ppermute | solution.py:350
  85.5 1.3 %collective-permute-done.16.refs_3_ = bf16[80,1024]{1,0:T(8,128)(2,1)S(1)} collective-permute-done((bf16[80,1024]{1,0:T(8,128)(2,1)S(1)}, bf16[80,1024]{1,0:T(8,128)(2,1)S(1)}, u32[]{:S(2)}, u32[]{:S(2)}) %collective-permute-start.16) | collective-permute-done | bytes 163872 | tf_op jit(solution)/shard_map/ppermute | solution.py:350
  86.8 2.0 %collective-permute-done.15.refs_1_ = bf16[80,1024]{1,0:T(8,128)(2,1)S(1)} collective-permute-done((bf16[80,1024]{1,0:T(8,128)(2,1)S(1)}, bf16[80,1024]{1,0:T(8,128)(2,1)S(1)}, u32[]{:S(2)}, u32[]{:S(2)}) %collective-permute-start.15) | collective-permute-done | bytes 163872 | tf_op jit(solution)/shard_map/ppermute | solution.py:350
  89.1 1.4 %shard_map.159 = (f32[2,1024,1024]{2,1,0:T(8,128)}, f32[8,128]{1,0:T(8,128)S(1)}) custom-call(bf16[512,1024]{1,0:T(8,128)(2,1)S(1)} %get-tuple-element.94.refs_0_, bf16[160,1024]{1,0:T(8,128)(2,1)S(1)} %get-tuple-element.92.refs_1_.refs_0_), custom_call_target="tpu_custom_call" | custom-call | flops 1 | bytes 1 | tf_op jit(solution)/shard_map/pallas_call | solution.py:62
  90.5 1.1 %collective-permute-done.21.refs_0_ = bf16[512,1024]{1,0:T(8,128)(2,1)S(1)} collective-permute-done((bf16[512,1024]{1,0:T(8,128)(2,1)S(1)}, bf16[512,1024]{1,0:T(8,128)(2,1)S(1)}, u32[]{:S(2)}, u32[]{:S(2)}) %collective-permute-start.21) | collective-permute-done | bytes 1048608 | tf_op jit(solution)/shard_map/ppermute | solution.py:350
  91.6 1.4 %shard_map.160 = (f32[2,1024,1024]{2,1,0:T(8,128)}, f32[8,128]{1,0:T(8,128)S(1)}) custom-call(bf16[512,1024]{1,0:T(8,128)(2,1)S(1)} %collective-permute-done.21.refs_0_, f32[2,1024,1024]{2,1,0:T(8,128)} %get-tuple-element.95.refs_1_, f32[8,128]{1,0:T(8,128)S(1)} %get-tuple-element.96.refs_2_), custom_call_target="tpu_custom_call", output_to_operand_aliasing={{0}: (1, {})} | custom-call | flops 1 | bytes 1 | tf_op jit(solution)/shard_map/pallas_call | solution.py:62
  93.0 6.1 %collective-permute-done.20.refs_3_ = bf16[160,1024]{1,0:T(8,128)(2,1)S(1)} collective-permute-done((bf16[160,1024]{1,0:T(8,128)(2,1)S(1)}, bf16[160,1024]{1,0:T(8,128)(2,1)S(1)}, u32[]{:S(2)}, u32[]{:S(2)}) %collective-permute-start.20) | collective-permute-done | bytes 327712 | tf_op jit(solution)/shard_map/ppermute | solution.py:350
  99.3 2.0 %shard_map.162 = (f32[2,1024,1024]{2,1,0:T(8,128)}, f32[8,128]{1,0:T(8,128)}) custom-call(bf16[640,1024]{1,0:T(8,128)(2,1)S(1)} %shard_map.161.refs_0_, f32[2,1024,1024]{2,1,0:T(8,128)} %get-tuple-element.98.refs_1_), custom_call_target="tpu_custom_call", output_to_operand_aliasing={{0}: (1, {})} | custom-call | flops 1 | bytes 1 | tf_op jit(solution)/shard_map/pallas_call | solution.py:62
  101.3 1.0 collective-permute-done.22.refs_1_
  102.3 2.8 %shard_map.163 = (f32[2,1024,1024]{2,1,0:T(8,128)}, f32[256,1024]{1,0:T(8,128)}, f32[1024,128]{1,0:T(8,128)}, f32[1,1024]{1,0:T(1,128)}) custom-call(bf16[640,1024]{1,0:T(8,128)(2,1)S(1)} %shard_map.161.refs_0_, bf16[640,1024]{1,0:T(8,128)(2,1)S(1)} %collective-permute-done.22.refs_1_, ...), custom_call_target="tpu_custom_call", output_to_operand_aliasing={{0}: (2, {})} | custom-call | flops 1 | bytes 1 | tf_op jit(solution)/shard_map/pallas_call | solution.py:62
  (45 shorter events, 3.7 us)
Async XLA Ops:
  2.0 15.3 %all-to-all-start = ((f32[16,8,128]{2,1,0:T(8,128)}), f32[16,8,128]{2,1,0:T(8,128)S(1)}, u32[]{:S(2)}, u32[]{:S(2)}) async-start(f32[16,8,128]{2,1,0:T(8,128)} %broadcast_in_dim.24), calls=%async_computation | async-start | bytes 131072 | tf_op jit(solution)/shard_map/all_to_all | solution.py:490
  11.0 6.3 %collective-permute-start.1 = (f32[3,1,32,128]{3,2,1,0:T(8,128)S(1)}, f32[3,1,32,128]{3,2,1,0:T(8,128)S(1)}, u32[]{:S(2)}, u32[]{:S(2)}) collective-permute-start(f32[3,1,32,128]{3,2,1,0:T(8,128)S(1)} %get-tuple-element.108), channel_id=1, source_target_pairs={{0,15},{1,2},{2,1},{3,4},{4,3},{5,6},{6,5},{7,8},{8,7},{9,10},{10,... | collective-permute-start | bytes 147464 | tf_op jit(solution)/shard_map/ppermute | solution.py:489
  15.4 1.8 %collective-permute-start = (f32[3,1,32,128]{3,2,1,0:T(8,128)S(1)}, f32[3,1,32,128]{3,2,1,0:T(8,128)S(1)}, u32[]{:S(2)}, u32[]{:S(2)}) collective-permute-start(f32[3,1,32,128]{3,2,1,0:T(8,128)S(1)} %get-tuple-element.109), channel_id=1, source_target_pairs={{0,1},{1,0},{2,3},{3,2},{4,5},{5,4},{6,7},{7,6},{8,9},{9,8},{10,11... | collective-permute-start | bytes 147464 | tf_op jit(solution)/shard_map/ppermute | solution.py:350
  19.9 7.8 %collective-permute-start.2 = (bf16[512,256]{1,0:T(8,128)(2,1)S(1)}, bf16[512,256]{1,0:T(8,128)(2,1)S(1)}, u32[]{:S(2)}, u32[]{:S(2)}) collective-permute-start(bf16[512,256]{1,0:T(8,128)(2,1)S(1)} %get-tuple-element.56.refs_0_), channel_id=1, source_target_pairs={{0,4},{1,5},{2,6},{3,7},{4,0},{5,1},{6,2},{7,3},{8,12},{9,13},{10,... | collective-permute-start | bytes 786440 | tf_op jit(solution)/shard_map/ppermute | solution.py:350
  34.6 3.2 %collective-permute-start.3 = (bf16[256,1024]{1,0:T(8,128)(2,1)S(1)}, bf16[256,1024]{1,0:T(8,128)(2,1)S(1)}, u32[]{:S(2)}, u32[]{:S(2)}) collective-permute-start(bf16[256,1024]{1,0:T(8,128)(2,1)S(1)} %get-tuple-element.75), channel_id=1, source_target_pairs={{0,1},{1,0},{2,3},{3,2},{4,5},{5,4},{6,7},{7,6},{8,9},{9,8},{10,11... | collective-permute-start | bytes 1572872 | tf_op jit(solution)/shard_map/ppermute | solution.py:350
  38.0 8.9 %collective-permute-start.8 = (bf16[128,1024]{1,0:T(8,128)(2,1)S(1)}, bf16[128,1024]{1,0:T(8,128)(2,1)S(1)}, u32[]{:S(2)}, u32[]{:S(2)}) collective-permute-start(bf16[128,1024]{1,0:T(8,128)(2,1)S(1)} %get-tuple-element.82), channel_id=1, source_target_pairs={{0,2},{1,3},{2,0},{3,1},{4,6},{5,7},{6,4},{7,5},{8,10},{9,11},{10,... | collective-permute-start | bytes 786440 | tf_op jit(solution)/shard_map/ppermute | solution.py:350
  45.8 5.1 %collective-permute-start.4 = (bf16[80,1024]{1,0:T(8,128)(2,1)S(1)}, bf16[80,1024]{1,0:T(8,128)(2,1)S(1)}, u32[]{:S(2)}, u32[]{:S(2)}) collective-permute-start(bf16[80,1024]{1,0:T(8,128)(2,1)S(1)} %get-tuple-element.78), channel_id=1, source_target_pairs={{0,1},{1,0},{2,3},{3,2},{4,5},{5,4},{6,7},{7,6},{8,9},{9,8},{10,11... | collective-permute-start | bytes 491528 | tf_op jit(solution)/shard_map/ppermute | solution.py:350
  46.0 4.8 %collective-permute-start.5 = (bf16[80,1024]{1,0:T(8,128)(2,1)S(1)}, bf16[80,1024]{1,0:T(8,128)(2,1)S(1)}, u32[]{:S(2)}, u32[]{:S(2)}) collective-permute-start(bf16[80,1024]{1,0:T(8,128)(2,1)S(1)} %get-tuple-element.79), channel_id=1, source_target_pairs={{0,1},{1,0},{2,3},{3,2},{4,5},{5,4},{6,7},{7,6},{8,9},{9,8},{10,11... | collective-permute-start | bytes 491528 | tf_op jit(solution)/shard_map/ppermute | solution.py:350
  46.4 4.5 %collective-permute-start.6 = (bf16[80,1024]{1,0:T(8,128)(2,1)S(1)}, bf16[80,1024]{1,0:T(8,128)(2,1)S(1)}, u32[]{:S(2)}, u32[]{:S(2)}) collective-permute-start(bf16[80,1024]{1,0:T(8,128)(2,1)S(1)} %get-tuple-element.80), channel_id=1, source_target_pairs={{0,1},{1,0},{2,3},{3,2},{4,5},{5,4},{6,7},{7,6},{8,9},{9,8},{10,11... | collective-permute-start | bytes 491528 | tf_op jit(solution)/shard_map/ppermute | solution.py:350
  46.5 4.3 %collective-permute-start.7 = (bf16[80,1024]{1,0:T(8,128)(2,1)S(1)}, bf16[80,1024]{1,0:T(8,128)(2,1)S(1)}, u32[]{:S(2)}, u32[]{:S(2)}) collective-permute-start(bf16[80,1024]{1,0:T(8,128)(2,1)S(1)} %get-tuple-element.81), channel_id=1, source_target_pairs={{0,1},{1,0},{2,3},{3,2},{4,5},{5,4},{6,7},{7,6},{8,9},{9,8},{10,11... | collective-permute-start | bytes 491528 | tf_op jit(solution)/shard_map/ppermute | solution.py:350
  46.9 15.9 %collective-permute-start.11 = (bf16[128,1024]{1,0:T(8,128)(2,1)S(1)}, bf16[128,1024]{1,0:T(8,128)(2,1)S(1)}, u32[]{:S(2)}, u32[]{:S(2)}) collective-permute-start(bf16[128,1024]{1,0:T(8,128)(2,1)S(1)} %shard_map.151.refs_5_.refs_0_), channel_id=1, source_target_pairs={{0,8},{1,9},{2,10},{3,11},{4,12},{5,13},{6,14},{7,15},{8,0},{9,1},... | collective-permute-start | bytes 786440 | tf_op jit(solution)/shard_map/ppermute | solution.py:350
  51.0 11.8 %collective-permute-start.9 = (bf16[80,1024]{1,0:T(8,128)(2,1)S(1)}, bf16[80,1024]{1,0:T(8,128)(2,1)S(1)}, u32[]{:S(2)}, u32[]{:S(2)}) collective-permute-start(bf16[80,1024]{1,0:T(8,128)(2,1)S(1)} %get-tuple-element.84), channel_id=1, source_target_pairs={{0,2},{1,3},{2,0},{3,1},{4,6},{5,7},{6,4},{7,5},{8,10},{9,11},{10,... | collective-permute-start | bytes 491528 | tf_op jit(solution)/shard_map/ppermute | solution.py:350
  51.2 11.6 %collective-permute-start.10 = (bf16[80,1024]{1,0:T(8,128)(2,1)S(1)}, bf16[80,1024]{1,0:T(8,128)(2,1)S(1)}, u32[]{:S(2)}, u32[]{:S(2)}) collective-permute-start(bf16[80,1024]{1,0:T(8,128)(2,1)S(1)} %get-tuple-element.85), channel_id=1, source_target_pairs={{0,2},{1,3},{2,0},{3,1},{4,6},{5,7},{6,4},{7,5},{8,10},{9,11},{10,... | collective-permute-start | bytes 491528 | tf_op jit(solution)/shard_map/ppermute | solution.py:350
  62.9 16.9 %collective-permute-start.12 = (bf16[160,1024]{1,0:T(8,128)(2,1)S(1)}, bf16[160,1024]{1,0:T(8,128)(2,1)S(1)}, u32[]{:S(2)}, u32[]{:S(2)}) collective-permute-start(bf16[160,1024]{1,0:T(8,128)(2,1)S(1)} %shard_map.154.refs_4_.refs_0_), channel_id=1, source_target_pairs={{0,8},{1,9},{2,10},{3,11},{4,12},{5,13},{6,14},{7,15},{8,0},{9,1},... | collective-permute-start | bytes 983048 | tf_op jit(solution)/shard_map/ppermute | solution.py:350
  62.9 5.5 %collective-permute-start.14 = (bf16[64,1024]{1,0:T(8,128)(2,1)S(1)}, bf16[64,1024]{1,0:T(8,128)(2,1)S(1)}, u32[]{:S(2)}, u32[]{:S(2)}) collective-permute-start(bf16[64,1024]{1,0:T(8,128)(2,1)S(1)} %get-tuple-element.87.refs_2_), channel_id=1, source_target_pairs={{0,2},{1,3},{2,0},{3,1},{4,6},{5,7},{6,4},{7,5},{8,10},{9,11},{10,... | collective-permute-start | bytes 393224 | tf_op jit(solution)/shard_map/ppermute | solution.py:350
  63.4 9.8 %collective-permute-start.13 = (bf16[64,1024]{1,0:T(8,128)(2,1)S(1)}, bf16[64,1024]{1,0:T(8,128)(2,1)S(1)}, u32[]{:S(2)}, u32[]{:S(2)}) collective-permute-start(bf16[64,1024]{1,0:T(8,128)(2,1)S(1)} %get-tuple-element.86.refs_3_.refs_0_), channel_id=1, source_target_pairs={{0,4},{1,5},{2,6},{3,7},{4,0},{5,1},{6,2},{7,3},{8,12},{9,13},{10,... | collective-permute-start | bytes 393224 | tf_op jit(solution)/shard_map/ppermute | solution.py:350
  73.3 12.1 %collective-permute-start.18 = (bf16[128,1024]{1,0:T(8,128)(2,1)S(1)}, bf16[128,1024]{1,0:T(8,128)(2,1)S(1)}, u32[]{:S(2)}, u32[]{:S(2)}) collective-permute-start(bf16[128,1024]{1,0:T(8,128)(2,1)S(1)} %get-tuple-element.91.refs_2_), channel_id=1, source_target_pairs={{0,4},{1,5},{2,6},{3,7},{4,0},{5,1},{6,2},{7,3},{8,12},{9,13},{10,... | collective-permute-start | bytes 786440 | tf_op jit(solution)/shard_map/ppermute | solution.py:350
  75.8 9.6 %collective-permute-start.17 = (bf16[128,1024]{1,0:T(8,128)(2,1)S(1)}, bf16[128,1024]{1,0:T(8,128)(2,1)S(1)}, u32[]{:S(2)}, u32[]{:S(2)}) collective-permute-start(bf16[128,1024]{1,0:T(8,128)(2,1)S(1)} %get-tuple-element.88.refs_2_.refs_0_), channel_id=1, source_target_pairs={{0,2},{1,3},{2,0},{3,1},{4,6},{5,7},{6,4},{7,5},{8,10},{9,11},{10,... | collective-permute-start | bytes 786440 | tf_op jit(solution)/shard_map/ppermute | solution.py:350
  79.8 7.0 %collective-permute-start.16 = (bf16[80,1024]{1,0:T(8,128)(2,1)S(1)}, bf16[80,1024]{1,0:T(8,128)(2,1)S(1)}, u32[]{:S(2)}, u32[]{:S(2)}) collective-permute-start(bf16[80,1024]{1,0:T(8,128)(2,1)S(1)} %get-tuple-element.90.refs_2_), channel_id=1, source_target_pairs={{0,2},{1,3},{2,0},{3,1},{4,6},{5,7},{6,4},{7,5},{8,10},{9,11},{10,... | collective-permute-start | bytes 491528 | tf_op jit(solution)/shard_map/ppermute | solution.py:350
  79.9 8.9 %collective-permute-start.15 = (bf16[80,1024]{1,0:T(8,128)(2,1)S(1)}, bf16[80,1024]{1,0:T(8,128)(2,1)S(1)}, u32[]{:S(2)}, u32[]{:S(2)}) collective-permute-start(bf16[80,1024]{1,0:T(8,128)(2,1)S(1)} %get-tuple-element.89.refs_4_.refs_0_), channel_id=1, source_target_pairs={{0,4},{1,5},{2,6},{3,7},{4,0},{5,1},{6,2},{7,3},{8,12},{9,13},{10,... | collective-permute-start | bytes 491528 | tf_op jit(solution)/shard_map/ppermute | solution.py:350
  88.9 2.7 %collective-permute-start.21 = (bf16[512,1024]{1,0:T(8,128)(2,1)S(1)}, bf16[512,1024]{1,0:T(8,128)(2,1)S(1)}, u32[]{:S(2)}, u32[]{:S(2)}) collective-permute-start(bf16[512,1024]{1,0:T(8,128)(2,1)S(1)} %get-tuple-element.94.refs_0_), channel_id=1, source_target_pairs={{0,1},{1,0},{2,3},{3,2},{4,5},{5,4},{6,7},{7,6},{8,9},{9,8},{10,11... | collective-permute-start | bytes 3145736 | tf_op jit(solution)/shard_map/ppermute | solution.py:350
  89.0 10.1 %collective-permute-start.20 = (bf16[160,1024]{1,0:T(8,128)(2,1)S(1)}, bf16[160,1024]{1,0:T(8,128)(2,1)S(1)}, u32[]{:S(2)}, u32[]{:S(2)}) collective-permute-start(bf16[160,1024]{1,0:T(8,128)(2,1)S(1)} %get-tuple-element.93.refs_2_), channel_id=1, source_target_pairs={{0,4},{1,5},{2,6},{3,7},{4,0},{5,1},{6,2},{7,3},{8,12},{9,13},{10,... | collective-permute-start | bytes 983048 | tf_op jit(solution)/shard_map/ppermute | solution.py:350
  89.0 10.1 %collective-permute-start.19 = (bf16[160,1024]{1,0:T(8,128)(2,1)S(1)}, bf16[160,1024]{1,0:T(8,128)(2,1)S(1)}, u32[]{:S(2)}, u32[]{:S(2)}) collective-permute-start(bf16[160,1024]{1,0:T(8,128)(2,1)S(1)} %get-tuple-element.92.refs_1_.refs_0_), channel_id=1, source_target_pairs={{0,2},{1,3},{2,0},{3,1},{4,6},{5,7},{6,4},{7,5},{8,10},{9,11},{10,... | collective-permute-start | bytes 983048 | tf_op jit(solution)/shard_map/ppermute | solution.py:350
  99.2 3.1 %collective-permute-start.22 = (bf16[640,1024]{1,0:T(8,128)(2,1)S(1)}, bf16[640,1024]{1,0:T(8,128)(2,1)S(1)}, u32[]{:S(2)}, u32[]{:S(2)}) collective-permute-start(bf16[640,1024]{1,0:T(8,128)(2,1)S(1)} %shard_map.161.refs_0_), channel_id=1, source_target_pairs={{0,1},{1,0},{2,3},{3,2},{4,5},{5,4},{6,7},{7,6},{8,9},{9,8},{10,11... | collective-permute-start | bytes 3932168 | tf_op jit(solution)/shard_map/ppermute | solution.py:350

commit v4 on v3

--- a/solution.py
+++ b/solution.py
@@ -13,6 +13,9 @@
 PACKED = 48
 BLOCK = 256
 ROOM = 28
+TOP_SHARE = 0.625
+LOW_SHARE = 0.5
+LOW_MIDS = 2
 BF = jnp.bfloat16
 F32 = jnp.float32
 VMEM = pl.BlockSpec(memory_space=pltpu.VMEM)
@@ -72,24 +75,26 @@
 
 
 def activate(v):
+    v = v.astype(BF)
     s = 0.5 + 0.5 * jnp.tanh(0.5 * v)
     act = v * s
-    return act.astype(BF), (s + act * (1.0 - s)).astype(BF)
-
-
-def step_body(
-    depth, near, far, owner, warm_in, brine_in, desired_in, stepped, pack, warm, brine, desired, sems
-):
-    lon, lat, levels = warm.shape
-    cols = lon * lat
+    return act, s + act * (1.0 - s)
+
+
+def stage_body(*refs):
+    count = len(refs) // 2
     copies = [
-        pltpu.make_async_copy(source, ref, sems.at[i])
-        for i, (source, ref) in enumerate(
-            ((warm_in, warm), (brine_in, brine), (desired_in, desired))
-        )
+        pltpu.make_async_copy(refs[i], refs[count + i], refs[-1].at[i]) for i in range(count)
     ]
     for copy in copies:
         copy.start()
+    for copy in copies:
+        copy.wait()
+
+
+def step_body(depth, near, far, owner, warm, brine, desired, stepped, pack):
+    lon, lat, levels = warm.shape
+    cols = lon * lat
     odd = bit_of(1) == 1
     before = jnp.where(odd, near[...], far[...])
     after = jnp.where(odd, far[...], near[...])
@@ -103,8 +108,6 @@
     wet_n = jnp.where(row < lat - 1, pltpu.roll(wet, lat - 1, 1), 0.0)
     wet_s = jnp.where(row > 0, pltpu.roll(wet, 1, 1), 0.0)
     lane = lax.broadcasted_iota(jnp.int32, (cols, levels), 1)
-    for copy in copies:
-        copy.wait()
     target = desired[...].reshape(cols, levels).astype(F32)
     for i, ref in enumerate((warm, brine)):
         q = ref[...]
@@ -307,19 +310,28 @@
         send[...] = total[at]
 
 
-def pair_body(keep, *refs):
-    got, out = refs[:-1], refs[-1]
-    base = 0
-    for ref in got:
-        at = slice(base, base + ref.shape[0])
-        out[at] = keep[at] + ref[...]
+def rows_of(refs):
+    base, places = 0, []
+    for ref in refs:
+        places.append(slice(base, base + ref.shape[0]))
         base += ref.shape[0]
-
-
-def unpair_body(x, got, a, b):
-    rows = a.shape[0]
-    a[...] = x[:rows] + got[:rows]
-    b[...] = x[rows:] + got[rows:]
+    return places
+
+
+def pair_body(count, keep, *refs):
+    got, outs, total = refs[:count], refs[count:-1], refs[-1]
+    for ref, at in zip(got, rows_of(got)):
+        total[at] = keep[at] + ref[...]
+    for ref, at in zip(outs, rows_of(outs)):
+        ref[...] = total[at]
+
+
+def unpair_body(count, *refs):
+    own, got, (a, b, total) = refs[:count], refs[count : 2 * count], refs[2 * count :]
+    for x, ref, at in zip(own, got, rows_of(own)):
+        total[at] = x[...] + ref[...]
+    for ref, at in zip((a, b), rows_of((a, b))):
+        ref[...] = total[at]
 
 
 def join_body(a, got_a, b, got_b, a_out, b_out):
@@ -331,16 +343,18 @@
 
 
 def whole_body(a, got_a, b, got_b, out):
-    rows = a.shape[0] // 2
+    rows = a.shape[0] // 2, b.shape[0] // 2
     y, z = bit_of(2), bit_of(4)
 
     def at(z, y, low):
-        return pl.ds(pl.multiple_of((z * 2 + y) * 2 * rows + low * rows, 16), rows)
+        base = (z * 2 + y) * (rows[0] + rows[1]) + low * rows[0]
+        return pl.ds(pl.multiple_of(base, 16), rows[low])
 
     for i in range(2):
-        own = slice(i * rows, (i + 1) * rows)
+        own = slice(i * rows[0], (i + 1) * rows[0])
         out[at(i, y, 0)] = a[own]
         out[at(i, 1 - y, 0)] = got_a[own]
+        own = slice(i * rows[1], (i + 1) * rows[1])
         out[at(z, i, 1)] = b[own]
         out[at(1 - z, i, 1)] = got_b[own]
 
@@ -355,9 +369,11 @@
 
 
 class Sum:
-    def __init__(self, mine, others, sends):
+    def __init__(self, mine, others, sends, mids, share):
         self.mine, self.got = mine, [swap(other, 1) for other in others]
-        self.rows, self.sends = mine.shape[0], sends
+        self.rows, self.sends, self.mids = mine.shape[0], sends, mids
+        self.a = int(share * self.rows / 32) * 16
+        self.b = self.rows // 2 - self.a
 
     def step(self, body, rows, args, after, carry=(), scratch=()):
         outs = [bf(r, self.mine) for r in rows]
@@ -378,21 +394,38 @@
         return keep, *carry
 
     def pair(self, after, carry=()):
-        (m,), carry = self.step(pair_body, [self.rows // 2], self.parts, after, carry)
-        token, stride = m, 8
+        half = self.rows // 2
+        m, carry = self.step(
+            functools.partial(pair_body, len(self.parts) - 1),
+            [half // self.mids] * self.mids,
+            self.parts,
+            after,
+            carry,
+            [pltpu.VMEM((half, self.mine.shape[1]), BF)],
+        )
+        token, stride = m[0], 8
         while 2 * stride < lax.axis_size("tiles"):
-            m = m + swap(m, stride)
+            m = [x + swap(x, stride) for x in m]
             stride *= 2
-        self.parts = m, swap(m, stride)
+        self.parts = (*m, *[swap(x, stride) for x in m])
         return token, *carry
 
     def unpair(self, after, carry=()):
-        (a, b), carry = self.step(unpair_body, [self.rows // 4] * 2, self.parts, after, carry)
+        (a, b), carry = self.step(
+            functools.partial(unpair_body, self.mids),
+            [self.a, self.b],
+            self.parts,
+            after,
+            carry,
+            [pltpu.VMEM((self.rows // 2, self.mine.shape[1]), BF)],
+        )
         self.parts = a, swap(a, 4), b, swap(b, 2)
         return a, *carry
 
     def join(self, after, carry=()):
-        (a, b), carry = self.step(join_body, [self.rows // 2] * 2, self.parts, after, carry)
+        (a, b), carry = self.step(
+            join_body, [2 * self.a, 2 * self.b], self.parts, after, carry
+        )
         self.parts = a, swap(a, 2), b, swap(b, 4)
         return a, *carry
 
@@ -436,11 +469,12 @@
     )
 
 
-def finish_body(n, x, got, held, out, lead_out, readout_out, own_out, wide, rest, sems):
+def finish_body(
+    n, x, got, held, out, lead_out, readout_out, own_out, wide, rest, lead, turned, sems
+):
     hid = out.shape[1]
-    levels = lead_out.shape[0] // 2
+    levels = lead.shape[0] // 2
     bit = bit_of(1)
-    copies = place_rows(got, 1 - bit, 0, out, wide, sems)
     quarter, part = hid // 8, rest.shape[0] // 8
     for ref, b in ((x, bit), (got, 1 - bit)):
         for i in range(4):
@@ -449,12 +483,17 @@
             rest[at] = ref[base : base + part].astype(F32)
     a = KEPT + n
     zeros = jnp.zeros((levels - KEPT, hid), F32)
-    lead_out[: KEPT - 2] = rest[: KEPT - 2]
-    lead_out[KEPT - 2 : levels] = jnp.zeros((levels - KEPT + 2, hid), F32)
-    lead_out[levels : levels + KEPT] = rest[a : a + KEPT]
-    lead_out[levels + KEPT :] = zeros
+    lead[: KEPT - 2] = rest[: KEPT - 2]
+    lead[KEPT - 2 : levels] = jnp.zeros((levels - KEPT + 2, hid), F32)
+    lead[levels : levels + KEPT] = rest[a : a + KEPT]
+    lead[levels + KEPT :] = zeros
+    copies = [pltpu.make_async_copy(lead, lead_out, sems.at[4])]
+    copies[0].start()
+    copies += place_rows(got, 1 - bit, 0, out, wide, sems)
+    turned[...] = jnp.concatenate([rest[a + KEPT : a + 2 * KEPT], zeros], 0).T
+    copies.append(pltpu.make_async_copy(turned, readout_out, sems.at[5]))
+    copies[-1].start()
     own_out[...] = rest[pl.ds(KEPT + lax.axis_index("tiles"), 1)]
-    readout_out[...] = jnp.concatenate([rest[a + KEPT : a + 2 * KEPT], zeros], 0).T
     for copy in copies:
         copy.wait()
 
@@ -498,18 +537,18 @@
         pltpu.with_memory_space_constraint(a, pltpu.HBM)
         for a in (warmth, brine, desired, leading, interior, readout)
     ]
+    warmth, brine, desired = call(
+        stage_body,
+        [pltpu.VMEM(a.shape, a.dtype) for a in (warmth, brine, desired)],
+        (warmth, brine, desired),
+        specs=[HBM] * 3,
+        scratch=[pltpu.SemaphoreType.DMA((3,))],
+    )
     stepped, pack = call(
         step_body,
         (Shape((2,) + wide, F32), Shape((cols, 2 * levels), BF)),
         (depth, near, far, owner, warmth, brine, desired),
         bias,
-        specs=[VMEM] * 4 + [HBM] * 3,
-        scratch=[
-            pltpu.VMEM(wide, F32),
-            pltpu.VMEM(wide, F32),
-            pltpu.VMEM(wide, BF),
-            pltpu.SemaphoreType.DMA((3,)),
-        ],
     )
     pack_p = swap(pack, 4)
     act = Shape((cols, hid), BF)
@@ -542,7 +581,7 @@
         scratch=[pltpu.VMEM((hid, hid), BF), sem],
         room=ROOM,
     )
-    top = Sum(mine, [other], 1)
+    top = Sum(mine, [other], 1, 1, TOP_SHARE)
     (token,) = top.split(delta1)
     rows = rest_rows(n)
     part = Shape((hid // 4 + rows // 4, hid), BF)
@@ -574,7 +613,7 @@
         ],
         room=ROOM,
     )
-    low = Sum(mine, others, 2)
+    low = Sum(mine, others, 2, LOW_MIDS, LOW_SHARE)
     (token,) = top.pair(mine)
     (token,) = low.split(token)
     (token,) = top.unpair(token)
@@ -598,11 +637,13 @@
         ),
         (y, swap(y, 1), held),
         specs=[VMEM, VMEM, HBM],
-        out_specs=(HBM, VMEM, VMEM, VMEM),
+        out_specs=(HBM, HBM, HBM, VMEM),
         scratch=[
             pltpu.VMEM((hid // 2, hid), F32),
             pltpu.VMEM((rows, hid), F32),
-            pltpu.SemaphoreType.DMA((4,)),
+            pltpu.VMEM((2 * levels, hid), F32),
+            pltpu.VMEM((hid, levels), F32),
+            pltpu.SemaphoreType.DMA((6,)),
         ],
         aliases={2: 0},
     )

time: 106 us -> 102 us (0.962)
  starting transfers between devices: 26.3 us -> 24.4 us
  Pallas kernels: 34.3 us -> 33.2 us
    ppermute x22 -> x23, starting transfers between devices: 14.5 us -> 12.6 us  [swap(): return lax.ppermute(x, 'tiles', [(t, t ^ stride) for t in range(n)])]
    ppermute x1, waiting for transfers between devices: 1.14 us -> 0.04 us  [local(): far = lax.ppermute(jnp.where(odd, last, first), 'tiles', pairs)]
    pallas_call x19 -> x20, Pallas kernels: 34.3 us -> 33.2 us  [call(): pl.pallas_call(body, out_shape=outs + tuple((Shape(a.shape, a.dtype) for...]
    ppermute x22 -> x23, waiting for transfers between devices: 38.5 us -> 39.1 us  [swap(): return lax.ppermute(x, 'tiles', [(t, t ^ stride) for t in range(n)])]
  transfers between devices with their start and end apart: 24 -> 25, of which waited for: 12 -> 17; matrix products, arithmetic and copies ran while one was open for 2% -> 2% of each run, Pallas kernels for 21% -> 22%
where the time goes in v4:
time: 102 us
  waiting for transfers between devices  39.2 us (38%)
  Pallas kernels  33.2 us (33%)
  starting transfers between devices  24.4 us (24%)
  local copies, waits for them, and re-layouts  2.49 us (2%)
  other arithmetic  1.43 us (1%)
  between operations  1.03 us (1%)
    ppermute x23, waiting for transfers between devices, swap(): return lax.ppermute(x, 'tiles', [(t, t ^ stride) for t in range(n)])  39.1 us
    pallas_call x20, Pallas kernels, call(): pl.pallas_call(body, out_shape=outs + tuple((Shape(a.shape, a.dtype) for...  33.2 us
    ppermute x23, starting transfers between devices, swap(): return lax.ppermute(x, 'tiles', [(t, t ^ stride) for t in range(n)])  12.6 us
    all_to_all x1, starting transfers between devices, local(): lax.all_to_all(jnp.broadcast_to(intercepts.reshape(1, hid // 128, 128), (...  7.39 us
    ppermute x1, starting transfers between devices, local(): far = lax.ppermute(jnp.where(odd, last, first), 'tiles', pairs)  4.43 us
  transfers between devices with their start and end apart: 25, of which 17 were waited for; matrix products, arithmetic and copies ran while one was open for 2% of the time, Pallas kernels for 22%

profile of v4, /device:TPU:0, one launch (start us, length us, event | category | flops | bytes accessed | tf_op | source)
XLA Modules:
  0.0 101.7 jit_solution(8829632528984443580)
XLA Ops:
  0.6 1.3 %broadcast_in_dim.24 = f32[16,8,128]{2,1,0:T(8,128)} broadcast(f32[8,128]{1,0:T(8,128)} %bitcast.13), dimensions={1,2} | broadcast | bytes 69632 | tf_op jit(solution)/shard_map/broadcast_in_dim | solution.py:530
  2.0 7.4 %all-to-all-start = ((f32[16,8,128]{2,1,0:T(8,128)}), f32[16,8,128]{2,1,0:T(8,128)S(1)}, u32[]{:S(2)}, u32[]{:S(2)}) async-start(f32[16,8,128]{2,1,0:T(8,128)} %broadcast_in_dim.24), calls=%async_computation | async-start | bytes 131072 | tf_op jit(solution)/shard_map/all_to_all | solution.py:529
  11.0 4.4 %collective-permute-start.1 = (f32[3,1,32,128]{3,2,1,0:T(8,128)S(1)}, f32[3,1,32,128]{3,2,1,0:T(8,128)S(1)}, u32[]{:S(2)}, u32[]{:S(2)}) collective-permute-start(f32[3,1,32,128]{3,2,1,0:T(8,128)S(1)} %get-tuple-element.118), channel_id=1, source_target_pairs={{0,15},{1,2},{2,1},{3,4},{4,3},{5,6},{6,5},{7,8},{8,7},{9,10},{10,... | collective-permute-start | bytes 147464 | tf_op jit(solution)/shard_map/ppermute | solution.py:528
  15.5 1.1 %shard_map.145 = (f32[16,32,128]{2,1,0:T(8,128)S(1)}, f32[16,32,128]{2,1,0:T(8,128)S(1)}, bf16[16,32,128]{2,1,0:T(8,128)(2,1)S(1)}) custom-call(f32[16,32,128]{2,1,0:T(8,128)} %refs_0_.3, f32[16,32,128]{2,1,0:T(8,128)} %refs_1_.1, bf16[16,32,128]{2,1,0:T(8,128)(2,1)} %refs_2_.3), custom_call_target="tpu_custom_call" | custom-call | flops 1 | bytes 1 | tf_op jit(solution)/shard_map/pallas_call | solution.py:65
  17.6 1.3 %shard_map.146 = (f32[2,16,32,128]{3,2,1,0:T(8,128)}, bf16[512,256]{1,0:T(8,128)(2,1)S(1)}) custom-call(f32[16,32,128]{2,1,0:T(8,128)S(1)} %broadcast_in_dim.10.refs_0_, f32[3,1,32,128]{3,2,1,0:T(8,128)S(1)} %collective-permute-done.refs_1_, f32[3,1,32,128]{3,2,1,0:T(8,128)S(1)} %collective-permute-done.1.refs_2_, ...), custom_call_target="tpu_custom_call" | custom-call | flops 1 | bytes 1 | tf_op jit(solution)/shard_map/pallas_call | solution.py:65
  19.0 6.1 %shard_map.147 = (bf16[16,32,128]{2,1,0:T(8,128)(2,1)}, bf16[256,1024]{1,0:T(8,128)(2,1)S(1)}, bf16[512,1024]{1,0:T(8,128)(2,1)S(1)}, bf16[512,1024]{1,0:T(8,128...) custom-call(bf16[512,256]{1,0:T(8,128)(2,1)S(1)} %get-tuple-element., ...), custom_call_target="tpu_custom_call" | custom-call | flops 1 | bytes 1 | tf_op jit(solution)/shard_map/pallas_call | solution.py:65
  25.2 2.4 %collective-permute-done.2.refs_0_ = bf16[512,256]{1,0:T(8,128)(2,1)S(1)} collective-permute-done((bf16[512,256]{1,0:T(8,128)(2,1)S(1)}, bf16[512,256]{1,0:T(8,128)(2,1)S(1)}, u32[]{:S(2)}, u32[]{:S(2)}) %collective-permute-start.2) | collective-permute-done | bytes 262176 | tf_op jit(solution)/shard_map/ppermute | solution.py:364
  27.5 6.5 %shard_map.148 = (bf16[512,1024]{1,0:T(8,128)(2,1)S(1)}, bf16[512,1024]{1,0:T(8,128)(2,1)S(1)}, bf16[512,1024]{1,0:T(8,128)(2,1)S(1)}, bf16[512,1024]{1,0:T(8,12...) custom-call(bf16[512,256]{1,0:T(8,128)(2,1)S(1)} %collective-permute, ...), custom_call_target="tpu_custom_call" | custom-call | flops 1 | bytes 1 | tf_op jit(solution)/shard_map/pallas_call | solution.py:65
  34.1 3.0 %shard_map.149 = (bf16[256,1024]{1,0:T(8,128)(2,1)S(1)}, bf16[512,1024]{1,0:T(8,128)(2,1)S(1)}) custom-call(bf16[2,1024,1024]{2,1,0:T(8,128)(2,1)} %refs_0_.5, bf16[512,1024]{1,0:T(8,128)(2,1)S(1)} %get-tuple-element.69.refs_4_.refs_1_, bf16[512,1024]{1,0:T(8,128)(2,1)S(1)} %get-tuple-element.70.refs_5_.refs_2_, ...), custom_call_target="tpu_custom_call" | custom-call | flops 1 | bytes 1 | tf_op jit(solution)/shard_map/pallas_call | solution.py:65
  37.3 7.2 %shard_map.151 = (bf16[320,1024]{1,0:T(8,128)(2,1)S(1)}, bf16[80,1024]{1,0:T(8,128)(2,1)S(1)}, bf16[80,1024]{1,0:T(8,128)(2,1)S(1)}, bf16[80,1024]{1,0:T(8,128)(2,1)S(1)}, bf16[80,1024]{1,0:T(8,128)(2,1)S(1)}) custom-call(bf16[2,1024,1024]{2,1,0:T(8,128)(2,1)} %refs_0_.5, bf16[512,256]{1,0:T(8,128)(2,1)S(1)} %get-tuple-element.66.refs_1_, ...), custom_call_target="tpu_custom_call" | custom-call | flops 1 | bytes 1 | tf_op jit(solution)/shard_map/pallas_call | solution.py:65
  44.4 1.5 %collective-permute-done.8.refs_1_ = bf16[128,1024]{1,0:T(8,128)(2,1)S(1)} collective-permute-done((bf16[128,1024]{1,0:T(8,128)(2,1)S(1)}, bf16[128,1024]{1,0:T(8,128)(2,1)S(1)}, u32[]{:S(2)}, u32[]{:S(2)}) %collective-permute-start.8) | collective-permute-done | bytes 262176 | tf_op jit(solution)/shard_map/ppermute | solution.py:364
  46.0 1.6 %collective-permute-start.11 = (bf16[128,1024]{1,0:T(8,128)(2,1)S(1)}, bf16[128,1024]{1,0:T(8,128)(2,1)S(1)}, u32[]{:S(2)}, u32[]{:S(2)}) collective-permute-start(bf16[128,1024]{1,0:T(8,128)(2,1)S(1)} %shard_map.152.refs_5_.refs_0_), channel_id=1, source_target_pairs={{0,8},{1,9},{2,10},{3,11},{4,12},{5,13},{6,14},{7,15},{8,0},{9,1},... | collective-permute-start | bytes 786440 | tf_op jit(solution)/shard_map/ppermute | solution.py:364
  49.8 1.1 %collective-permute-start.9 = (bf16[80,1024]{1,0:T(8,128)(2,1)S(1)}, bf16[80,1024]{1,0:T(8,128)(2,1)S(1)}, u32[]{:S(2)}, u32[]{:S(2)}) collective-permute-start(bf16[80,1024]{1,0:T(8,128)(2,1)S(1)} %get-tuple-element.92), channel_id=1, source_target_pairs={{0,2},{1,3},{2,0},{3,1},{4,6},{5,7},{6,4},{7,5},{8,10},{9,11},{10,... | collective-permute-start | bytes 491528 | tf_op jit(solution)/shard_map/ppermute | solution.py:364
  51.0 1.0 collective-permute-start.10
  51.9 8.3 %collective-permute-done.11.refs_1_ = bf16[128,1024]{1,0:T(8,128)(2,1)S(1)} collective-permute-done((bf16[128,1024]{1,0:T(8,128)(2,1)S(1)}, bf16[128,1024]{1,0:T(8,128)(2,1)S(1)}, u32[]{:S(2)}, u32[]{:S(2)}) %collective-permute-start.11) | collective-permute-done | bytes 262176 | tf_op jit(solution)/shard_map/ppermute | solution.py:364
  60.3 1.1 %collective-permute-start.15 = (bf16[48,1024]{1,0:T(8,128)(2,1)S(1)}, bf16[48,1024]{1,0:T(8,128)(2,1)S(1)}, u32[]{:S(2)}, u32[]{:S(2)}) collective-permute-start(bf16[48,1024]{1,0:T(8,128)(2,1)S(1)} %get-tuple-element.97.refs_2_), channel_id=1, source_target_pairs={{0,2},{1,3},{2,0},{3,1},{4,6},{5,7},{6,4},{7,5},{8,10},{9,11},{10,... | collective-permute-start | bytes 294920 | tf_op jit(solution)/shard_map/ppermute | solution.py:364
  61.4 1.6 %collective-permute-start.13 = (bf16[80,1024]{1,0:T(8,128)(2,1)S(1)}, bf16[80,1024]{1,0:T(8,128)(2,1)S(1)}, u32[]{:S(2)}, u32[]{:S(2)}) collective-permute-start(bf16[80,1024]{1,0:T(8,128)(2,1)S(1)} %get-tuple-element.96.refs_1_), channel_id=1, source_target_pairs={{0,8},{1,9},{2,10},{3,11},{4,12},{5,13},{6,14},{7,15},{8,0},{9,1},... | collective-permute-start | bytes 491528 | tf_op jit(solution)/shard_map/ppermute | solution.py:364
  63.1 1.4 %collective-permute-start.12 = (bf16[80,1024]{1,0:T(8,128)(2,1)S(1)}, bf16[80,1024]{1,0:T(8,128)(2,1)S(1)}, u32[]{:S(2)}, u32[]{:S(2)}) collective-permute-start(bf16[80,1024]{1,0:T(8,128)(2,1)S(1)} %get-tuple-element.95.refs_4_.refs_0_), channel_id=1, source_target_pairs={{0,8},{1,9},{2,10},{3,11},{4,12},{5,13},{6,14},{7,15},{8,0},{9,1},... | collective-permute-start | bytes 491528 | tf_op jit(solution)/shard_map/ppermute | solution.py:364
  65.1 2.5 %collective-permute-done.14.refs_1_ = bf16[80,1024]{1,0:T(8,128)(2,1)S(1)} collective-permute-done((bf16[80,1024]{1,0:T(8,128)(2,1)S(1)}, bf16[80,1024]{1,0:T(8,128)(2,1)S(1)}, u32[]{:S(2)}, u32[]{:S(2)}) %collective-permute-start.14) | collective-permute-done | bytes 163872 | tf_op jit(solution)/shard_map/ppermute | solution.py:364
  67.7 1.1 %collective-permute-start.18 = (bf16[160,1024]{1,0:T(8,128)(2,1)S(1)}, bf16[160,1024]{1,0:T(8,128)(2,1)S(1)}, u32[]{:S(2)}, u32[]{:S(2)}) collective-permute-start(bf16[160,1024]{1,0:T(8,128)(2,1)S(1)} %get-tuple-element.98.refs_4_.refs_0_), channel_id=1, source_target_pairs={{0,2},{1,3},{2,0},{3,1},{4,6},{5,7},{6,4},{7,5},{8,10},{9,11},{10,... | collective-permute-start | bytes 983048 | tf_op jit(solution)/shard_map/ppermute | solution.py:364
  68.8 7.9 %collective-permute-done.13.refs_3_ = bf16[80,1024]{1,0:T(8,128)(2,1)S(1)} collective-permute-done((bf16[80,1024]{1,0:T(8,128)(2,1)S(1)}, bf16[80,1024]{1,0:T(8,128)(2,1)S(1)}, u32[]{:S(2)}, u32[]{:S(2)}) %collective-permute-start.13) | collective-permute-done | bytes 163872 | tf_op jit(solution)/shard_map/ppermute | solution.py:364
  76.6 2.3 %collective-permute-done.12.refs_2_ = bf16[80,1024]{1,0:T(8,128)(2,1)S(1)} collective-permute-done((bf16[80,1024]{1,0:T(8,128)(2,1)S(1)}, bf16[80,1024]{1,0:T(8,128)(2,1)S(1)}, u32[]{:S(2)}, u32[]{:S(2)}) %collective-permute-start.12) | collective-permute-done | bytes 163872 | tf_op jit(solution)/shard_map/ppermute | solution.py:364
  79.0 1.1 %collective-permute-start.17 = (bf16[80,1024]{1,0:T(8,128)(2,1)S(1)}, bf16[80,1024]{1,0:T(8,128)(2,1)S(1)}, u32[]{:S(2)}, u32[]{:S(2)}) collective-permute-start(bf16[80,1024]{1,0:T(8,128)(2,1)S(1)} %get-tuple-element.100.refs_2_), channel_id=1, source_target_pairs={{0,2},{1,3},{2,0},{3,1},{4,6},{5,7},{6,4},{7,5},{8,10},{9,11},{10,... | collective-permute-start | bytes 491528 | tf_op jit(solution)/shard_map/ppermute | solution.py:364
  80.4 4.0 %collective-permute-done.17.refs_3_ = bf16[80,1024]{1,0:T(8,128)(2,1)S(1)} collective-permute-done((bf16[80,1024]{1,0:T(8,128)(2,1)S(1)}, bf16[80,1024]{1,0:T(8,128)(2,1)S(1)}, u32[]{:S(2)}, u32[]{:S(2)}) %collective-permute-start.17) | collective-permute-done | bytes 163872 | tf_op jit(solution)/shard_map/ppermute | solution.py:364
  84.4 1.0 collective-permute-done.16.refs_1_
  85.6 1.1 %collective-permute-start.20 = (bf16[160,1024]{1,0:T(8,128)(2,1)S(1)}, bf16[160,1024]{1,0:T(8,128)(2,1)S(1)}, u32[]{:S(2)}, u32[]{:S(2)}) collective-permute-start(bf16[160,1024]{1,0:T(8,128)(2,1)S(1)} %get-tuple-element.102.refs_1_.refs_0_), channel_id=1, source_target_pairs={{0,2},{1,3},{2,0},{3,1},{4,6},{5,7},{6,4},{7,5},{8,10},{9,11},{10,... | collective-permute-start | bytes 983048 | tf_op jit(solution)/shard_map/ppermute | solution.py:364
  86.7 1.4 %shard_map.160 = (f32[2,1024,1024]{2,1,0:T(8,128)}, f32[8,128]{1,0:T(8,128)S(1)}) custom-call(bf16[512,1024]{1,0:T(8,128)(2,1)S(1)} %get-tuple-element.104.refs_0_, bf16[160,1024]{1,0:T(8,128)(2,1)S(1)} %get-tuple-element.102.refs_1_.refs_0_), custom_call_target="tpu_custom_call" | custom-call | flops 1 | bytes 1 | tf_op jit(solution)/shard_map/pallas_call | solution.py:65
  88.2 1.4 %shard_map.161 = (f32[2,1024,1024]{2,1,0:T(8,128)}, f32[8,128]{1,0:T(8,128)S(1)}) custom-call(bf16[512,1024]{1,0:T(8,128)(2,1)S(1)} %collective-permute-done.22.refs_0_, f32[2,1024,1024]{2,1,0:T(8,128)} %get-tuple-element.105.refs_1_, f32[8,128]{1,0:T(8,128)S(1)} %get-tuple-element.106.refs_2_), custom_call_target="tpu_custom_call", output_to_operand_aliasing={{0}: (1, {})} | custom-call | flops 1 | bytes 1 | tf_op jit(solution)/shard_map/pallas_call | solution.py:65
  89.6 6.1 %collective-permute-done.21.refs_3_ = bf16[160,1024]{1,0:T(8,128)(2,1)S(1)} collective-permute-done((bf16[160,1024]{1,0:T(8,128)(2,1)S(1)}, bf16[160,1024]{1,0:T(8,128)(2,1)S(1)}, u32[]{:S(2)}, u32[]{:S(2)}) %collective-permute-start.21) | collective-permute-done | bytes 327712 | tf_op jit(solution)/shard_map/ppermute | solution.py:364
  95.8 2.0 %shard_map.163 = (f32[2,1024,1024]{2,1,0:T(8,128)}, f32[8,128]{1,0:T(8,128)}) custom-call(bf16[640,1024]{1,0:T(8,128)(2,1)S(1)} %shard_map.162.refs_0_, f32[2,1024,1024]{2,1,0:T(8,128)} %get-tuple-element.108.refs_1_), custom_call_target="tpu_custom_call", output_to_operand_aliasing={{0}: (1, {})} | custom-call | flops 1 | bytes 1 | tf_op jit(solution)/shard_map/pallas_call | solution.py:65
  97.8 1.0 %collective-permute-done.23.refs_1_ = bf16[640,1024]{1,0:T(8,128)(2,1)S(1)} collective-permute-done((bf16[640,1024]{1,0:T(8,128)(2,1)S(1)}, bf16[640,1024]{1,0:T(8,128)(2,1)S(1)}, u32[]{:S(2)}, u32[]{:S(2)}) %collective-permute-start.23) | collective-permute-done | bytes 1310752 | tf_op jit(solution)/shard_map/ppermute | solution.py:364
  98.9 2.7 %shard_map.164 = (f32[2,1024,1024]{2,1,0:T(8,128)}, f32[256,1024]{1,0:T(8,128)}, f32[1024,128]{1,0:T(8,128)}, f32[1,1024]{1,0:T(1,128)}) custom-call(bf16[640,1024]{1,0:T(8,128)(2,1)S(1)} %shard_map.162.refs_0_, bf16[640,1024]{1,0:T(8,128)(2,1)S(1)} %collective-permute-done.23.refs_1_, ...), custom_call_target="tpu_custom_call", output_to_operand_aliasing={{0}: (2, {})} | custom-call | flops 1 | bytes 1 | tf_op jit(solution)/shard_map/pallas_call | solution.py:65
  (48 shorter events, 7.0 us)
Async XLA Ops:
  2.0 15.3 %all-to-all-start = ((f32[16,8,128]{2,1,0:T(8,128)}), f32[16,8,128]{2,1,0:T(8,128)S(1)}, u32[]{:S(2)}, u32[]{:S(2)}) async-start(f32[16,8,128]{2,1,0:T(8,128)} %broadcast_in_dim.24), calls=%async_computation | async-start | bytes 131072 | tf_op jit(solution)/shard_map/all_to_all | solution.py:529
  11.0 6.3 %collective-permute-start.1 = (f32[3,1,32,128]{3,2,1,0:T(8,128)S(1)}, f32[3,1,32,128]{3,2,1,0:T(8,128)S(1)}, u32[]{:S(2)}, u32[]{:S(2)}) collective-permute-start(f32[3,1,32,128]{3,2,1,0:T(8,128)S(1)} %get-tuple-element.118), channel_id=1, source_target_pairs={{0,15},{1,2},{2,1},{3,4},{4,3},{5,6},{6,5},{7,8},{8,7},{9,10},{10,... | collective-permute-start | bytes 147464 | tf_op jit(solution)/shard_map/ppermute | solution.py:528
  15.4 1.8 %collective-permute-start = (f32[3,1,32,128]{3,2,1,0:T(8,128)S(1)}, f32[3,1,32,128]{3,2,1,0:T(8,128)S(1)}, u32[]{:S(2)}, u32[]{:S(2)}) collective-permute-start(f32[3,1,32,128]{3,2,1,0:T(8,128)S(1)} %get-tuple-element.119), channel_id=1, source_target_pairs={{0,1},{1,0},{2,3},{3,2},{4,5},{5,4},{6,7},{7,6},{8,9},{9,8},{10,11... | collective-permute-start | bytes 147464 | tf_op jit(solution)/shard_map/ppermute | solution.py:364
  18.9 8.7 %collective-permute-start.2 = (bf16[512,256]{1,0:T(8,128)(2,1)S(1)}, bf16[512,256]{1,0:T(8,128)(2,1)S(1)}, u32[]{:S(2)}, u32[]{:S(2)}) collective-permute-start(bf16[512,256]{1,0:T(8,128)(2,1)S(1)} %get-tuple-element.64.refs_0_), channel_id=1, source_target_pairs={{0,4},{1,5},{2,6},{3,7},{4,0},{5,1},{6,2},{7,3},{8,12},{9,13},{10,... | collective-permute-start | bytes 786440 | tf_op jit(solution)/shard_map/ppermute | solution.py:364
  34.0 3.1 %collective-permute-start.3 = (bf16[256,1024]{1,0:T(8,128)(2,1)S(1)}, bf16[256,1024]{1,0:T(8,128)(2,1)S(1)}, u32[]{:S(2)}, u32[]{:S(2)}) collective-permute-start(bf16[256,1024]{1,0:T(8,128)(2,1)S(1)} %get-tuple-element.83), channel_id=1, source_target_pairs={{0,1},{1,0},{2,3},{3,2},{4,5},{5,4},{6,7},{7,6},{8,9},{9,8},{10,11... | collective-permute-start | bytes 1572872 | tf_op jit(solution)/shard_map/ppermute | solution.py:364
  37.2 8.8 %collective-permute-start.8 = (bf16[128,1024]{1,0:T(8,128)(2,1)S(1)}, bf16[128,1024]{1,0:T(8,128)(2,1)S(1)}, u32[]{:S(2)}, u32[]{:S(2)}) collective-permute-start(bf16[128,1024]{1,0:T(8,128)(2,1)S(1)} %get-tuple-element.90), channel_id=1, source_target_pairs={{0,2},{1,3},{2,0},{3,1},{4,6},{5,7},{6,4},{7,5},{8,10},{9,11},{10,... | collective-permute-start | bytes 786440 | tf_op jit(solution)/shard_map/ppermute | solution.py:364
  46.0 14.2 %collective-permute-start.11 = (bf16[128,1024]{1,0:T(8,128)(2,1)S(1)}, bf16[128,1024]{1,0:T(8,128)(2,1)S(1)}, u32[]{:S(2)}, u32[]{:S(2)}) collective-permute-start(bf16[128,1024]{1,0:T(8,128)(2,1)S(1)} %shard_map.152.refs_5_.refs_0_), channel_id=1, source_target_pairs={{0,8},{1,9},{2,10},{3,11},{4,12},{5,13},{6,14},{7,15},{8,0},{9,1},... | collective-permute-start | bytes 786440 | tf_op jit(solution)/shard_map/ppermute | solution.py:364
  47.6 1.4 %collective-permute-start.4 = (bf16[80,1024]{1,0:T(8,128)(2,1)S(1)}, bf16[80,1024]{1,0:T(8,128)(2,1)S(1)}, u32[]{:S(2)}, u32[]{:S(2)}) collective-permute-start(bf16[80,1024]{1,0:T(8,128)(2,1)S(1)} %get-tuple-element.86), channel_id=1, source_target_pairs={{0,1},{1,0},{2,3},{3,2},{4,5},{5,4},{6,7},{7,6},{8,9},{9,8},{10,11... | collective-permute-start | bytes 491528 | tf_op jit(solution)/shard_map/ppermute | solution.py:364
  47.6 1.6 %collective-permute-start.5 = (bf16[80,1024]{1,0:T(8,128)(2,1)S(1)}, bf16[80,1024]{1,0:T(8,128)(2,1)S(1)}, u32[]{:S(2)}, u32[]{:S(2)}) collective-permute-start(bf16[80,1024]{1,0:T(8,128)(2,1)S(1)} %get-tuple-element.87), channel_id=1, source_target_pairs={{0,1},{1,0},{2,3},{3,2},{4,5},{5,4},{6,7},{7,6},{8,9},{9,8},{10,11... | collective-permute-start | bytes 491528 | tf_op jit(solution)/shard_map/ppermute | solution.py:364
  48.1 1.4 %collective-permute-start.6 = (bf16[80,1024]{1,0:T(8,128)(2,1)S(1)}, bf16[80,1024]{1,0:T(8,128)(2,1)S(1)}, u32[]{:S(2)}, u32[]{:S(2)}) collective-permute-start(bf16[80,1024]{1,0:T(8,128)(2,1)S(1)} %get-tuple-element.88), channel_id=1, source_target_pairs={{0,1},{1,0},{2,3},{3,2},{4,5},{5,4},{6,7},{7,6},{8,9},{9,8},{10,11... | collective-permute-start | bytes 491528 | tf_op jit(solution)/shard_map/ppermute | solution.py:364
  48.1 1.6 %collective-permute-start.7 = (bf16[80,1024]{1,0:T(8,128)(2,1)S(1)}, bf16[80,1024]{1,0:T(8,128)(2,1)S(1)}, u32[]{:S(2)}, u32[]{:S(2)}) collective-permute-start(bf16[80,1024]{1,0:T(8,128)(2,1)S(1)} %get-tuple-element.89), channel_id=1, source_target_pairs={{0,1},{1,0},{2,3},{3,2},{4,5},{5,4},{6,7},{7,6},{8,9},{9,8},{10,11... | collective-permute-start | bytes 491528 | tf_op jit(solution)/shard_map/ppermute | solution.py:364
  49.8 11.6 %collective-permute-start.9 = (bf16[80,1024]{1,0:T(8,128)(2,1)S(1)}, bf16[80,1024]{1,0:T(8,128)(2,1)S(1)}, u32[]{:S(2)}, u32[]{:S(2)}) collective-permute-start(bf16[80,1024]{1,0:T(8,128)(2,1)S(1)} %get-tuple-element.92), channel_id=1, source_target_pairs={{0,2},{1,3},{2,0},{3,1},{4,6},{5,7},{6,4},{7,5},{8,10},{9,11},{10,... | collective-permute-start | bytes 491528 | tf_op jit(solution)/shard_map/ppermute | solution.py:364
  51.0 10.4 %collective-permute-start.10 = (bf16[80,1024]{1,0:T(8,128)(2,1)S(1)}, bf16[80,1024]{1,0:T(8,128)(2,1)S(1)}, u32[]{:S(2)}, u32[]{:S(2)}) collective-permute-start(bf16[80,1024]{1,0:T(8,128)(2,1)S(1)} %get-tuple-element.93), channel_id=1, source_target_pairs={{0,2},{1,3},{2,0},{3,1},{4,6},{5,7},{6,4},{7,5},{8,10},{9,11},{10,... | collective-permute-start | bytes 491528 | tf_op jit(solution)/shard_map/ppermute | solution.py:364
  60.3 7.3 %collective-permute-start.14 = (bf16[80,1024]{1,0:T(8,128)(2,1)S(1)}, bf16[80,1024]{1,0:T(8,128)(2,1)S(1)}, u32[]{:S(2)}, u32[]{:S(2)}) collective-permute-start(bf16[80,1024]{1,0:T(8,128)(2,1)S(1)} %get-tuple-element.94.refs_3_.refs_0_), channel_id=1, source_target_pairs={{0,4},{1,5},{2,6},{3,7},{4,0},{5,1},{6,2},{7,3},{8,12},{9,13},{10,... | collective-permute-start | bytes 491528 | tf_op jit(solution)/shard_map/ppermute | solution.py:364
  60.3 4.8 %collective-permute-start.15 = (bf16[48,1024]{1,0:T(8,128)(2,1)S(1)}, bf16[48,1024]{1,0:T(8,128)(2,1)S(1)}, u32[]{:S(2)}, u32[]{:S(2)}) collective-permute-start(bf16[48,1024]{1,0:T(8,128)(2,1)S(1)} %get-tuple-element.97.refs_2_), channel_id=1, source_target_pairs={{0,2},{1,3},{2,0},{3,1},{4,6},{5,7},{6,4},{7,5},{8,10},{9,11},{10,... | collective-permute-start | bytes 294920 | tf_op jit(solution)/shard_map/ppermute | solution.py:364
  61.4 15.2 %collective-permute-start.13 = (bf16[80,1024]{1,0:T(8,128)(2,1)S(1)}, bf16[80,1024]{1,0:T(8,128)(2,1)S(1)}, u32[]{:S(2)}, u32[]{:S(2)}) collective-permute-start(bf16[80,1024]{1,0:T(8,128)(2,1)S(1)} %get-tuple-element.96.refs_1_), channel_id=1, source_target_pairs={{0,8},{1,9},{2,10},{3,11},{4,12},{5,13},{6,14},{7,15},{8,0},{9,1},... | collective-permute-start | bytes 491528 | tf_op jit(solution)/shard_map/ppermute | solution.py:364
  63.1 15.9 %collective-permute-start.12 = (bf16[80,1024]{1,0:T(8,128)(2,1)S(1)}, bf16[80,1024]{1,0:T(8,128)(2,1)S(1)}, u32[]{:S(2)}, u32[]{:S(2)}) collective-permute-start(bf16[80,1024]{1,0:T(8,128)(2,1)S(1)} %get-tuple-element.95.refs_4_.refs_0_), channel_id=1, source_target_pairs={{0,8},{1,9},{2,10},{3,11},{4,12},{5,13},{6,14},{7,15},{8,0},{9,1},... | collective-permute-start | bytes 491528 | tf_op jit(solution)/shard_map/ppermute | solution.py:364
  67.7 12.7 %collective-permute-start.18 = (bf16[160,1024]{1,0:T(8,128)(2,1)S(1)}, bf16[160,1024]{1,0:T(8,128)(2,1)S(1)}, u32[]{:S(2)}, u32[]{:S(2)}) collective-permute-start(bf16[160,1024]{1,0:T(8,128)(2,1)S(1)} %get-tuple-element.98.refs_4_.refs_0_), channel_id=1, source_target_pairs={{0,2},{1,3},{2,0},{3,1},{4,6},{5,7},{6,4},{7,5},{8,10},{9,11},{10,... | collective-permute-start | bytes 983048 | tf_op jit(solution)/shard_map/ppermute | solution.py:364
  68.8 11.6 %collective-permute-start.19 = (bf16[96,1024]{1,0:T(8,128)(2,1)S(1)}, bf16[96,1024]{1,0:T(8,128)(2,1)S(1)}, u32[]{:S(2)}, u32[]{:S(2)}) collective-permute-start(bf16[96,1024]{1,0:T(8,128)(2,1)S(1)} %get-tuple-element.101.refs_2_), channel_id=1, source_target_pairs={{0,4},{1,5},{2,6},{3,7},{4,0},{5,1},{6,2},{7,3},{8,12},{9,13},{10,... | collective-permute-start | bytes 589832 | tf_op jit(solution)/shard_map/ppermute | solution.py:364
  79.0 5.4 %collective-permute-start.17 = (bf16[80,1024]{1,0:T(8,128)(2,1)S(1)}, bf16[80,1024]{1,0:T(8,128)(2,1)S(1)}, u32[]{:S(2)}, u32[]{:S(2)}) collective-permute-start(bf16[80,1024]{1,0:T(8,128)(2,1)S(1)} %get-tuple-element.100.refs_2_), channel_id=1, source_target_pairs={{0,2},{1,3},{2,0},{3,1},{4,6},{5,7},{6,4},{7,5},{8,10},{9,11},{10,... | collective-permute-start | bytes 491528 | tf_op jit(solution)/shard_map/ppermute | solution.py:364
  80.1 5.3 %collective-permute-start.16 = (bf16[80,1024]{1,0:T(8,128)(2,1)S(1)}, bf16[80,1024]{1,0:T(8,128)(2,1)S(1)}, u32[]{:S(2)}, u32[]{:S(2)}) collective-permute-start(bf16[80,1024]{1,0:T(8,128)(2,1)S(1)} %get-tuple-element.99.refs_4_.refs_0_), channel_id=1, source_target_pairs={{0,4},{1,5},{2,6},{3,7},{4,0},{5,1},{6,2},{7,3},{8,12},{9,13},{10,... | collective-permute-start | bytes 491528 | tf_op jit(solution)/shard_map/ppermute | solution.py:364
  85.5 2.7 %collective-permute-start.22 = (bf16[512,1024]{1,0:T(8,128)(2,1)S(1)}, bf16[512,1024]{1,0:T(8,128)(2,1)S(1)}, u32[]{:S(2)}, u32[]{:S(2)}) collective-permute-start(bf16[512,1024]{1,0:T(8,128)(2,1)S(1)} %get-tuple-element.104.refs_0_), channel_id=1, source_target_pairs={{0,1},{1,0},{2,3},{3,2},{4,5},{5,4},{6,7},{7,6},{8,9},{9,8},{10,11... | collective-permute-start | bytes 3145736 | tf_op jit(solution)/shard_map/ppermute | solution.py:364
  85.5 10.1 %collective-permute-start.21 = (bf16[160,1024]{1,0:T(8,128)(2,1)S(1)}, bf16[160,1024]{1,0:T(8,128)(2,1)S(1)}, u32[]{:S(2)}, u32[]{:S(2)}) collective-permute-start(bf16[160,1024]{1,0:T(8,128)(2,1)S(1)} %get-tuple-element.103.refs_2_), channel_id=1, source_target_pairs={{0,4},{1,5},{2,6},{3,7},{4,0},{5,1},{6,2},{7,3},{8,12},{9,13},{10,... | collective-permute-start | bytes 983048 | tf_op jit(solution)/shard_map/ppermute | solution.py:364
  85.6 10.1 %collective-permute-start.20 = (bf16[160,1024]{1,0:T(8,128)(2,1)S(1)}, bf16[160,1024]{1,0:T(8,128)(2,1)S(1)}, u32[]{:S(2)}, u32[]{:S(2)}) collective-permute-start(bf16[160,1024]{1,0:T(8,128)(2,1)S(1)} %get-tuple-element.102.refs_1_.refs_0_), channel_id=1, source_target_pairs={{0,2},{1,3},{2,0},{3,1},{4,6},{5,7},{6,4},{7,5},{8,10},{9,11},{10,... | collective-permute-start | bytes 983048 | tf_op jit(solution)/shard_map/ppermute | solution.py:364
  95.8 3.1 %collective-permute-start.23 = (bf16[640,1024]{1,0:T(8,128)(2,1)S(1)}, bf16[640,1024]{1,0:T(8,128)(2,1)S(1)}, u32[]{:S(2)}, u32[]{:S(2)}) collective-permute-start(bf16[640,1024]{1,0:T(8,128)(2,1)S(1)} %shard_map.162.refs_0_), channel_id=1, source_target_pairs={{0,1},{1,0},{2,3},{3,2},{4,5},{5,4},{6,7},{7,6},{8,9},{9,8},{10,11... | collective-permute-start | bytes 3932168 | tf_op jit(solution)/shard_map/ppermute | solution.py:364

commit v5 on v4

--- a/solution.py
+++ b/solution.py
@@ -15,6 +15,7 @@
 ROOM = 28
 TOP_SHARE = 0.625
 LOW_SHARE = 0.5
+LOW_SENDS = 2
 LOW_MIDS = 2
 BF = jnp.bfloat16
 F32 = jnp.float32
@@ -75,9 +76,9 @@
 
 
 def activate(v):
-    v = v.astype(BF)
     s = 0.5 + 0.5 * jnp.tanh(0.5 * v)
-    act = v * s
+    act = (v * s).astype(BF)
+    s = s.astype(BF)
     return act, s + act * (1.0 - s)
 
 
@@ -483,16 +484,16 @@
             rest[at] = ref[base : base + part].astype(F32)
     a = KEPT + n
     zeros = jnp.zeros((levels - KEPT, hid), F32)
+    turned[...] = jnp.concatenate([rest[a + KEPT : a + 2 * KEPT], zeros], 0).T
+    copies = [pltpu.make_async_copy(turned, readout_out, sems.at[5])]
+    copies[0].start()
     lead[: KEPT - 2] = rest[: KEPT - 2]
     lead[KEPT - 2 : levels] = jnp.zeros((levels - KEPT + 2, hid), F32)
     lead[levels : levels + KEPT] = rest[a : a + KEPT]
     lead[levels + KEPT :] = zeros
-    copies = [pltpu.make_async_copy(lead, lead_out, sems.at[4])]
-    copies[0].start()
+    copies.append(pltpu.make_async_copy(lead, lead_out, sems.at[4]))
+    copies[-1].start()
     copies += place_rows(got, 1 - bit, 0, out, wide, sems)
-    turned[...] = jnp.concatenate([rest[a + KEPT : a + 2 * KEPT], zeros], 0).T
-    copies.append(pltpu.make_async_copy(turned, readout_out, sems.at[5]))
-    copies[-1].start()
     own_out[...] = rest[pl.ds(KEPT + lax.axis_index("tiles"), 1)]
     for copy in copies:
         copy.wait()
@@ -613,7 +614,7 @@
         ],
         room=ROOM,
     )
-    low = Sum(mine, others, 2, LOW_MIDS, LOW_SHARE)
+    low = Sum(mine, others, LOW_SENDS, LOW_MIDS, LOW_SHARE)
     (token,) = top.pair(mine)
     (token,) = low.split(token)
     (token,) = top.unpair(token)

time: 102 us -> 103 us (level)
  no operation moved by 1% of the time
where the time goes in v5:
time: 103 us; the launch traced here: 102 us
  waiting for transfers between devices  38.3 us (37%)
  Pallas kernels  34 us (33%)
  starting transfers between devices  24.9 us (24%)
  local copies, waits for them, and re-layouts  2.49 us (2%)
  other arithmetic  1.43 us (1%)
  between operations  1.03 us (1%)
    ppermute x23, waiting for transfers between devices, swap(): return lax.ppermute(x, 'tiles', [(t, t ^ stride) for t in range(n)])  38.2 us
    pallas_call x20, Pallas kernels, call(): pl.pallas_call(body, out_shape=outs + tuple((Shape(a.shape, a.dtype) for...  34 us
    ppermute x23, starting transfers between devices, swap(): return lax.ppermute(x, 'tiles', [(t, t ^ stride) for t in range(n)])  13.1 us
    all_to_all x1, starting transfers between devices, local(): lax.all_to_all(jnp.broadcast_to(intercepts.reshape(1, hid // 128, 128), (...  7.39 us
    ppermute x1, starting transfers between devices, local(): far = lax.ppermute(jnp.where(odd, last, first), 'tiles', pairs)  4.43 us
  transfers between devices with their start and end apart: 25, of which 17 were waited for; matrix products, arithmetic and copies ran while one was open for 2% of the time, Pallas kernels for 22%

profile of v5, /device:TPU:0, one launch (start us, length us, event | category | flops | bytes accessed | tf_op | source)
XLA Modules:
  0.0 102.1 jit_solution(7325622008907624423)
XLA Ops:
  0.6 1.3 %broadcast_in_dim.24 = f32[16,8,128]{2,1,0:T(8,128)} broadcast(f32[8,128]{1,0:T(8,128)} %bitcast.13), dimensions={1,2} | broadcast | bytes 69632 | tf_op jit(solution)/shard_map/broadcast_in_dim | solution.py:531
  2.0 7.4 %all-to-all-start = ((f32[16,8,128]{2,1,0:T(8,128)}), f32[16,8,128]{2,1,0:T(8,128)S(1)}, u32[]{:S(2)}, u32[]{:S(2)}) async-start(f32[16,8,128]{2,1,0:T(8,128)} %broadcast_in_dim.24), calls=%async_computation | async-start | bytes 131072 | tf_op jit(solution)/shard_map/all_to_all | solution.py:530
  11.0 4.4 %collective-permute-start.1 = (f32[3,1,32,128]{3,2,1,0:T(8,128)S(1)}, f32[3,1,32,128]{3,2,1,0:T(8,128)S(1)}, u32[]{:S(2)}, u32[]{:S(2)}) collective-permute-start(f32[3,1,32,128]{3,2,1,0:T(8,128)S(1)} %get-tuple-element.118), channel_id=1, source_target_pairs={{0,15},{1,2},{2,1},{3,4},{4,3},{5,6},{6,5},{7,8},{8,7},{9,10},{10,... | collective-permute-start | bytes 147464 | tf_op jit(solution)/shard_map/ppermute | solution.py:529
  15.5 1.1 %shard_map.145 = (f32[16,32,128]{2,1,0:T(8,128)S(1)}, f32[16,32,128]{2,1,0:T(8,128)S(1)}, bf16[16,32,128]{2,1,0:T(8,128)(2,1)S(1)}) custom-call(f32[16,32,128]{2,1,0:T(8,128)} %refs_0_.3, f32[16,32,128]{2,1,0:T(8,128)} %refs_1_.1, bf16[16,32,128]{2,1,0:T(8,128)(2,1)} %refs_2_.3), custom_call_target="tpu_custom_call" | custom-call | flops 1 | bytes 1 | tf_op jit(solution)/shard_map/pallas_call | solution.py:66
  17.6 1.3 %shard_map.146 = (f32[2,16,32,128]{3,2,1,0:T(8,128)}, bf16[512,256]{1,0:T(8,128)(2,1)S(1)}) custom-call(f32[16,32,128]{2,1,0:T(8,128)S(1)} %broadcast_in_dim.10.refs_0_, f32[3,1,32,128]{3,2,1,0:T(8,128)S(1)} %collective-permute-done.refs_1_, f32[3,1,32,128]{3,2,1,0:T(8,128)S(1)} %collective-permute-done.1.refs_2_, ...), custom_call_target="tpu_custom_call" | custom-call | flops 1 | bytes 1 | tf_op jit(solution)/shard_map/pallas_call | solution.py:66
  19.0 6.6 %shard_map.147 = (bf16[16,32,128]{2,1,0:T(8,128)(2,1)}, bf16[256,1024]{1,0:T(8,128)(2,1)S(1)}, bf16[512,1024]{1,0:T(8,128)(2,1)S(1)}, bf16[512,1024]{1,0:T(8,128...) custom-call(bf16[512,256]{1,0:T(8,128)(2,1)S(1)} %get-tuple-element., ...), custom_call_target="tpu_custom_call" | custom-call | flops 1 | bytes 1 | tf_op jit(solution)/shard_map/pallas_call | solution.py:66
  25.6 1.9 %collective-permute-done.2.refs_0_ = bf16[512,256]{1,0:T(8,128)(2,1)S(1)} collective-permute-done((bf16[512,256]{1,0:T(8,128)(2,1)S(1)}, bf16[512,256]{1,0:T(8,128)(2,1)S(1)}, u32[]{:S(2)}, u32[]{:S(2)}) %collective-permute-start.2) | collective-permute-done | bytes 262176 | tf_op jit(solution)/shard_map/ppermute | solution.py:365
  27.5 6.8 %shard_map.148 = (bf16[512,1024]{1,0:T(8,128)(2,1)S(1)}, bf16[512,1024]{1,0:T(8,128)(2,1)S(1)}, bf16[512,1024]{1,0:T(8,128)(2,1)S(1)}, bf16[512,1024]{1,0:T(8,12...) custom-call(bf16[512,256]{1,0:T(8,128)(2,1)S(1)} %collective-permute, ...), custom_call_target="tpu_custom_call" | custom-call | flops 1 | bytes 1 | tf_op jit(solution)/shard_map/pallas_call | solution.py:66
  34.4 3.0 %shard_map.149 = (bf16[256,1024]{1,0:T(8,128)(2,1)S(1)}, bf16[512,1024]{1,0:T(8,128)(2,1)S(1)}) custom-call(bf16[2,1024,1024]{2,1,0:T(8,128)(2,1)} %refs_0_.5, bf16[512,1024]{1,0:T(8,128)(2,1)S(1)} %get-tuple-element.69.refs_4_.refs_1_, bf16[512,1024]{1,0:T(8,128)(2,1)S(1)} %get-tuple-element.70.refs_5_.refs_2_, ...), custom_call_target="tpu_custom_call" | custom-call | flops 1 | bytes 1 | tf_op jit(solution)/shard_map/pallas_call | solution.py:66
  37.6 7.2 %shard_map.151 = (bf16[320,1024]{1,0:T(8,128)(2,1)S(1)}, bf16[80,1024]{1,0:T(8,128)(2,1)S(1)}, bf16[80,1024]{1,0:T(8,128)(2,1)S(1)}, bf16[80,1024]{1,0:T(8,128)(2,1)S(1)}, bf16[80,1024]{1,0:T(8,128)(2,1)S(1)}) custom-call(bf16[2,1024,1024]{2,1,0:T(8,128)(2,1)} %refs_0_.5, bf16[512,256]{1,0:T(8,128)(2,1)S(1)} %get-tuple-element.66.refs_1_, ...), custom_call_target="tpu_custom_call" | custom-call | flops 1 | bytes 1 | tf_op jit(solution)/shard_map/pallas_call | solution.py:66
  44.7 1.5 %collective-permute-done.8.refs_1_ = bf16[128,1024]{1,0:T(8,128)(2,1)S(1)} collective-permute-done((bf16[128,1024]{1,0:T(8,128)(2,1)S(1)}, bf16[128,1024]{1,0:T(8,128)(2,1)S(1)}, u32[]{:S(2)}, u32[]{:S(2)}) %collective-permute-start.8) | collective-permute-done | bytes 262176 | tf_op jit(solution)/shard_map/ppermute | solution.py:365
  46.3 2.0 %collective-permute-start.11 = (bf16[128,1024]{1,0:T(8,128)(2,1)S(1)}, bf16[128,1024]{1,0:T(8,128)(2,1)S(1)}, u32[]{:S(2)}, u32[]{:S(2)}) collective-permute-start(bf16[128,1024]{1,0:T(8,128)(2,1)S(1)} %shard_map.152.refs_5_.refs_0_), channel_id=1, source_target_pairs={{0,8},{1,9},{2,10},{3,11},{4,12},{5,13},{6,14},{7,15},{8,0},{9,1},... | collective-permute-start | bytes 786440 | tf_op jit(solution)/shard_map/ppermute | solution.py:365
  50.6 1.1 %collective-permute-start.9 = (bf16[80,1024]{1,0:T(8,128)(2,1)S(1)}, bf16[80,1024]{1,0:T(8,128)(2,1)S(1)}, u32[]{:S(2)}, u32[]{:S(2)}) collective-permute-start(bf16[80,1024]{1,0:T(8,128)(2,1)S(1)} %get-tuple-element.92), channel_id=1, source_target_pairs={{0,2},{1,3},{2,0},{3,1},{4,6},{5,7},{6,4},{7,5},{8,10},{9,11},{10,... | collective-permute-start | bytes 491528 | tf_op jit(solution)/shard_map/ppermute | solution.py:365
  51.7 1.0 collective-permute-start.10
  52.7 7.8 %collective-permute-done.11.refs_1_ = bf16[128,1024]{1,0:T(8,128)(2,1)S(1)} collective-permute-done((bf16[128,1024]{1,0:T(8,128)(2,1)S(1)}, bf16[128,1024]{1,0:T(8,128)(2,1)S(1)}, u32[]{:S(2)}, u32[]{:S(2)}) %collective-permute-start.11) | collective-permute-done | bytes 262176 | tf_op jit(solution)/shard_map/ppermute | solution.py:365
  60.6 1.1 %collective-permute-start.15 = (bf16[48,1024]{1,0:T(8,128)(2,1)S(1)}, bf16[48,1024]{1,0:T(8,128)(2,1)S(1)}, u32[]{:S(2)}, u32[]{:S(2)}) collective-permute-start(bf16[48,1024]{1,0:T(8,128)(2,1)S(1)} %get-tuple-element.97.refs_2_), channel_id=1, source_target_pairs={{0,2},{1,3},{2,0},{3,1},{4,6},{5,7},{6,4},{7,5},{8,10},{9,11},{10,... | collective-permute-start | bytes 294920 | tf_op jit(solution)/shard_map/ppermute | solution.py:365
  61.7 2.0 %collective-permute-start.13 = (bf16[80,1024]{1,0:T(8,128)(2,1)S(1)}, bf16[80,1024]{1,0:T(8,128)(2,1)S(1)}, u32[]{:S(2)}, u32[]{:S(2)}) collective-permute-start(bf16[80,1024]{1,0:T(8,128)(2,1)S(1)} %get-tuple-element.96.refs_1_), channel_id=1, source_target_pairs={{0,8},{1,9},{2,10},{3,11},{4,12},{5,13},{6,14},{7,15},{8,0},{9,1},... | collective-permute-start | bytes 491528 | tf_op jit(solution)/shard_map/ppermute | solution.py:365
  63.8 0.9 collective-permute-start.12
  65.4 2.5 %collective-permute-done.14.refs_1_ = bf16[80,1024]{1,0:T(8,128)(2,1)S(1)} collective-permute-done((bf16[80,1024]{1,0:T(8,128)(2,1)S(1)}, bf16[80,1024]{1,0:T(8,128)(2,1)S(1)}, u32[]{:S(2)}, u32[]{:S(2)}) %collective-permute-start.14) | collective-permute-done | bytes 163872 | tf_op jit(solution)/shard_map/ppermute | solution.py:365
  67.9 1.1 %collective-permute-start.18 = (bf16[160,1024]{1,0:T(8,128)(2,1)S(1)}, bf16[160,1024]{1,0:T(8,128)(2,1)S(1)}, u32[]{:S(2)}, u32[]{:S(2)}) collective-permute-start(bf16[160,1024]{1,0:T(8,128)(2,1)S(1)} %get-tuple-element.98.refs_4_.refs_0_), channel_id=1, source_target_pairs={{0,2},{1,3},{2,0},{3,1},{4,6},{5,7},{6,4},{7,5},{8,10},{9,11},{10,... | collective-permute-start | bytes 983048 | tf_op jit(solution)/shard_map/ppermute | solution.py:365
  69.0 7.9 %collective-permute-done.13.refs_3_ = bf16[80,1024]{1,0:T(8,128)(2,1)S(1)} collective-permute-done((bf16[80,1024]{1,0:T(8,128)(2,1)S(1)}, bf16[80,1024]{1,0:T(8,128)(2,1)S(1)}, u32[]{:S(2)}, u32[]{:S(2)}) %collective-permute-start.13) | collective-permute-done | bytes 163872 | tf_op jit(solution)/shard_map/ppermute | solution.py:365
  76.9 2.3 %collective-permute-done.12.refs_2_ = bf16[80,1024]{1,0:T(8,128)(2,1)S(1)} collective-permute-done((bf16[80,1024]{1,0:T(8,128)(2,1)S(1)}, bf16[80,1024]{1,0:T(8,128)(2,1)S(1)}, u32[]{:S(2)}, u32[]{:S(2)}) %collective-permute-start.12) | collective-permute-done | bytes 163872 | tf_op jit(solution)/shard_map/ppermute | solution.py:365
  79.3 1.1 %collective-permute-start.17 = (bf16[80,1024]{1,0:T(8,128)(2,1)S(1)}, bf16[80,1024]{1,0:T(8,128)(2,1)S(1)}, u32[]{:S(2)}, u32[]{:S(2)}) collective-permute-start(bf16[80,1024]{1,0:T(8,128)(2,1)S(1)} %get-tuple-element.100.refs_2_), channel_id=1, source_target_pairs={{0,2},{1,3},{2,0},{3,1},{4,6},{5,7},{6,4},{7,5},{8,10},{9,11},{10,... | collective-permute-start | bytes 491528 | tf_op jit(solution)/shard_map/ppermute | solution.py:365
  80.7 4.0 %collective-permute-done.17.refs_3_ = bf16[80,1024]{1,0:T(8,128)(2,1)S(1)} collective-permute-done((bf16[80,1024]{1,0:T(8,128)(2,1)S(1)}, bf16[80,1024]{1,0:T(8,128)(2,1)S(1)}, u32[]{:S(2)}, u32[]{:S(2)}) %collective-permute-start.17) | collective-permute-done | bytes 163872 | tf_op jit(solution)/shard_map/ppermute | solution.py:365
  84.7 1.0 collective-permute-done.16.refs_1_
  85.9 1.1 %collective-permute-start.20 = (bf16[160,1024]{1,0:T(8,128)(2,1)S(1)}, bf16[160,1024]{1,0:T(8,128)(2,1)S(1)}, u32[]{:S(2)}, u32[]{:S(2)}) collective-permute-start(bf16[160,1024]{1,0:T(8,128)(2,1)S(1)} %get-tuple-element.102.refs_1_.refs_0_), channel_id=1, source_target_pairs={{0,2},{1,3},{2,0},{3,1},{4,6},{5,7},{6,4},{7,5},{8,10},{9,11},{10,... | collective-permute-start | bytes 983048 | tf_op jit(solution)/shard_map/ppermute | solution.py:365
  87.0 1.4 %shard_map.160 = (f32[2,1024,1024]{2,1,0:T(8,128)}, f32[8,128]{1,0:T(8,128)S(1)}) custom-call(bf16[512,1024]{1,0:T(8,128)(2,1)S(1)} %get-tuple-element.104.refs_0_, bf16[160,1024]{1,0:T(8,128)(2,1)S(1)} %get-tuple-element.102.refs_1_.refs_0_), custom_call_target="tpu_custom_call" | custom-call | flops 1 | bytes 1 | tf_op jit(solution)/shard_map/pallas_call | solution.py:66
  88.5 1.4 %shard_map.161 = (f32[2,1024,1024]{2,1,0:T(8,128)}, f32[8,128]{1,0:T(8,128)S(1)}) custom-call(bf16[512,1024]{1,0:T(8,128)(2,1)S(1)} %collective-permute-done.22.refs_0_, f32[2,1024,1024]{2,1,0:T(8,128)} %get-tuple-element.105.refs_1_, f32[8,128]{1,0:T(8,128)S(1)} %get-tuple-element.106.refs_2_), custom_call_target="tpu_custom_call", output_to_operand_aliasing={{0}: (1, {})} | custom-call | flops 1 | bytes 1 | tf_op jit(solution)/shard_map/pallas_call | solution.py:66
  89.8 6.1 %collective-permute-done.21.refs_3_ = bf16[160,1024]{1,0:T(8,128)(2,1)S(1)} collective-permute-done((bf16[160,1024]{1,0:T(8,128)(2,1)S(1)}, bf16[160,1024]{1,0:T(8,128)(2,1)S(1)}, u32[]{:S(2)}, u32[]{:S(2)}) %collective-permute-start.21) | collective-permute-done | bytes 327712 | tf_op jit(solution)/shard_map/ppermute | solution.py:365
  96.1 2.0 %shard_map.163 = (f32[2,1024,1024]{2,1,0:T(8,128)}, f32[8,128]{1,0:T(8,128)}) custom-call(bf16[640,1024]{1,0:T(8,128)(2,1)S(1)} %shard_map.162.refs_0_, f32[2,1024,1024]{2,1,0:T(8,128)} %get-tuple-element.108.refs_1_), custom_call_target="tpu_custom_call", output_to_operand_aliasing={{0}: (1, {})} | custom-call | flops 1 | bytes 1 | tf_op jit(solution)/shard_map/pallas_call | solution.py:66
  98.1 1.0 %collective-permute-done.23.refs_1_ = bf16[640,1024]{1,0:T(8,128)(2,1)S(1)} collective-permute-done((bf16[640,1024]{1,0:T(8,128)(2,1)S(1)}, bf16[640,1024]{1,0:T(8,128)(2,1)S(1)}, u32[]{:S(2)}, u32[]{:S(2)}) %collective-permute-start.23) | collective-permute-done | bytes 1310752 | tf_op jit(solution)/shard_map/ppermute | solution.py:365
  99.2 2.8 %shard_map.164 = (f32[2,1024,1024]{2,1,0:T(8,128)}, f32[256,1024]{1,0:T(8,128)}, f32[1024,128]{1,0:T(8,128)}, f32[1,1024]{1,0:T(1,128)}) custom-call(bf16[640,1024]{1,0:T(8,128)(2,1)S(1)} %shard_map.162.refs_0_, bf16[640,1024]{1,0:T(8,128)(2,1)S(1)} %collective-permute-done.23.refs_1_, ...), custom_call_target="tpu_custom_call", output_to_operand_aliasing={{0}: (2, {})} | custom-call | flops 1 | bytes 1 | tf_op jit(solution)/shard_map/pallas_call | solution.py:66
  (48 shorter events, 7.1 us)
Async XLA Ops:
  2.0 15.3 %all-to-all-start = ((f32[16,8,128]{2,1,0:T(8,128)}), f32[16,8,128]{2,1,0:T(8,128)S(1)}, u32[]{:S(2)}, u32[]{:S(2)}) async-start(f32[16,8,128]{2,1,0:T(8,128)} %broadcast_in_dim.24), calls=%async_computation | async-start | bytes 131072 | tf_op jit(solution)/shard_map/all_to_all | solution.py:530
  11.0 6.3 %collective-permute-start.1 = (f32[3,1,32,128]{3,2,1,0:T(8,128)S(1)}, f32[3,1,32,128]{3,2,1,0:T(8,128)S(1)}, u32[]{:S(2)}, u32[]{:S(2)}) collective-permute-start(f32[3,1,32,128]{3,2,1,0:T(8,128)S(1)} %get-tuple-element.118), channel_id=1, source_target_pairs={{0,15},{1,2},{2,1},{3,4},{4,3},{5,6},{6,5},{7,8},{8,7},{9,10},{10,... | collective-permute-start | bytes 147464 | tf_op jit(solution)/shard_map/ppermute | solution.py:529
  15.4 1.8 %collective-permute-start = (f32[3,1,32,128]{3,2,1,0:T(8,128)S(1)}, f32[3,1,32,128]{3,2,1,0:T(8,128)S(1)}, u32[]{:S(2)}, u32[]{:S(2)}) collective-permute-start(f32[3,1,32,128]{3,2,1,0:T(8,128)S(1)} %get-tuple-element.119), channel_id=1, source_target_pairs={{0,1},{1,0},{2,3},{3,2},{4,5},{5,4},{6,7},{7,6},{8,9},{9,8},{10,11... | collective-permute-start | bytes 147464 | tf_op jit(solution)/shard_map/ppermute | solution.py:365
  18.9 8.7 %collective-permute-start.2 = (bf16[512,256]{1,0:T(8,128)(2,1)S(1)}, bf16[512,256]{1,0:T(8,128)(2,1)S(1)}, u32[]{:S(2)}, u32[]{:S(2)}) collective-permute-start(bf16[512,256]{1,0:T(8,128)(2,1)S(1)} %get-tuple-element.64.refs_0_), channel_id=1, source_target_pairs={{0,4},{1,5},{2,6},{3,7},{4,0},{5,1},{6,2},{7,3},{8,12},{9,13},{10,... | collective-permute-start | bytes 786440 | tf_op jit(solution)/shard_map/ppermute | solution.py:365
  34.3 3.1 %collective-permute-start.3 = (bf16[256,1024]{1,0:T(8,128)(2,1)S(1)}, bf16[256,1024]{1,0:T(8,128)(2,1)S(1)}, u32[]{:S(2)}, u32[]{:S(2)}) collective-permute-start(bf16[256,1024]{1,0:T(8,128)(2,1)S(1)} %get-tuple-element.83), channel_id=1, source_target_pairs={{0,1},{1,0},{2,3},{3,2},{4,5},{5,4},{6,7},{7,6},{8,9},{9,8},{10,11... | collective-permute-start | bytes 1572872 | tf_op jit(solution)/shard_map/ppermute | solution.py:365
  37.5 8.8 %collective-permute-start.8 = (bf16[128,1024]{1,0:T(8,128)(2,1)S(1)}, bf16[128,1024]{1,0:T(8,128)(2,1)S(1)}, u32[]{:S(2)}, u32[]{:S(2)}) collective-permute-start(bf16[128,1024]{1,0:T(8,128)(2,1)S(1)} %get-tuple-element.90), channel_id=1, source_target_pairs={{0,2},{1,3},{2,0},{3,1},{4,6},{5,7},{6,4},{7,5},{8,10},{9,11},{10,... | collective-permute-start | bytes 786440 | tf_op jit(solution)/shard_map/ppermute | solution.py:365
  46.3 14.2 %collective-permute-start.11 = (bf16[128,1024]{1,0:T(8,128)(2,1)S(1)}, bf16[128,1024]{1,0:T(8,128)(2,1)S(1)}, u32[]{:S(2)}, u32[]{:S(2)}) collective-permute-start(bf16[128,1024]{1,0:T(8,128)(2,1)S(1)} %shard_map.152.refs_5_.refs_0_), channel_id=1, source_target_pairs={{0,8},{1,9},{2,10},{3,11},{4,12},{5,13},{6,14},{7,15},{8,0},{9,1},... | collective-permute-start | bytes 786440 | tf_op jit(solution)/shard_map/ppermute | solution.py:365
  48.3 1.4 %collective-permute-start.4 = (bf16[80,1024]{1,0:T(8,128)(2,1)S(1)}, bf16[80,1024]{1,0:T(8,128)(2,1)S(1)}, u32[]{:S(2)}, u32[]{:S(2)}) collective-permute-start(bf16[80,1024]{1,0:T(8,128)(2,1)S(1)} %get-tuple-element.86), channel_id=1, source_target_pairs={{0,1},{1,0},{2,3},{3,2},{4,5},{5,4},{6,7},{7,6},{8,9},{9,8},{10,11... | collective-permute-start | bytes 491528 | tf_op jit(solution)/shard_map/ppermute | solution.py:365
  48.3 1.6 %collective-permute-start.5 = (bf16[80,1024]{1,0:T(8,128)(2,1)S(1)}, bf16[80,1024]{1,0:T(8,128)(2,1)S(1)}, u32[]{:S(2)}, u32[]{:S(2)}) collective-permute-start(bf16[80,1024]{1,0:T(8,128)(2,1)S(1)} %get-tuple-element.87), channel_id=1, source_target_pairs={{0,1},{1,0},{2,3},{3,2},{4,5},{5,4},{6,7},{7,6},{8,9},{9,8},{10,11... | collective-permute-start | bytes 491528 | tf_op jit(solution)/shard_map/ppermute | solution.py:365
  48.8 1.4 %collective-permute-start.6 = (bf16[80,1024]{1,0:T(8,128)(2,1)S(1)}, bf16[80,1024]{1,0:T(8,128)(2,1)S(1)}, u32[]{:S(2)}, u32[]{:S(2)}) collective-permute-start(bf16[80,1024]{1,0:T(8,128)(2,1)S(1)} %get-tuple-element.88), channel_id=1, source_target_pairs={{0,1},{1,0},{2,3},{3,2},{4,5},{5,4},{6,7},{7,6},{8,9},{9,8},{10,11... | collective-permute-start | bytes 491528 | tf_op jit(solution)/shard_map/ppermute | solution.py:365
  48.8 1.6 %collective-permute-start.7 = (bf16[80,1024]{1,0:T(8,128)(2,1)S(1)}, bf16[80,1024]{1,0:T(8,128)(2,1)S(1)}, u32[]{:S(2)}, u32[]{:S(2)}) collective-permute-start(bf16[80,1024]{1,0:T(8,128)(2,1)S(1)} %get-tuple-element.89), channel_id=1, source_target_pairs={{0,1},{1,0},{2,3},{3,2},{4,5},{5,4},{6,7},{7,6},{8,9},{9,8},{10,11... | collective-permute-start | bytes 491528 | tf_op jit(solution)/shard_map/ppermute | solution.py:365
  50.6 11.1 %collective-permute-start.9 = (bf16[80,1024]{1,0:T(8,128)(2,1)S(1)}, bf16[80,1024]{1,0:T(8,128)(2,1)S(1)}, u32[]{:S(2)}, u32[]{:S(2)}) collective-permute-start(bf16[80,1024]{1,0:T(8,128)(2,1)S(1)} %get-tuple-element.92), channel_id=1, source_target_pairs={{0,2},{1,3},{2,0},{3,1},{4,6},{5,7},{6,4},{7,5},{8,10},{9,11},{10,... | collective-permute-start | bytes 491528 | tf_op jit(solution)/shard_map/ppermute | solution.py:365
  51.7 10.0 %collective-permute-start.10 = (bf16[80,1024]{1,0:T(8,128)(2,1)S(1)}, bf16[80,1024]{1,0:T(8,128)(2,1)S(1)}, u32[]{:S(2)}, u32[]{:S(2)}) collective-permute-start(bf16[80,1024]{1,0:T(8,128)(2,1)S(1)} %get-tuple-element.93), channel_id=1, source_target_pairs={{0,2},{1,3},{2,0},{3,1},{4,6},{5,7},{6,4},{7,5},{8,10},{9,11},{10,... | collective-permute-start | bytes 491528 | tf_op jit(solution)/shard_map/ppermute | solution.py:365
  60.5 7.3 %collective-permute-start.14 = (bf16[80,1024]{1,0:T(8,128)(2,1)S(1)}, bf16[80,1024]{1,0:T(8,128)(2,1)S(1)}, u32[]{:S(2)}, u32[]{:S(2)}) collective-permute-start(bf16[80,1024]{1,0:T(8,128)(2,1)S(1)} %get-tuple-element.94.refs_3_.refs_0_), channel_id=1, source_target_pairs={{0,4},{1,5},{2,6},{3,7},{4,0},{5,1},{6,2},{7,3},{8,12},{9,13},{10,... | collective-permute-start | bytes 491528 | tf_op jit(solution)/shard_map/ppermute | solution.py:365
  60.6 4.8 %collective-permute-start.15 = (bf16[48,1024]{1,0:T(8,128)(2,1)S(1)}, bf16[48,1024]{1,0:T(8,128)(2,1)S(1)}, u32[]{:S(2)}, u32[]{:S(2)}) collective-permute-start(bf16[48,1024]{1,0:T(8,128)(2,1)S(1)} %get-tuple-element.97.refs_2_), channel_id=1, source_target_pairs={{0,2},{1,3},{2,0},{3,1},{4,6},{5,7},{6,4},{7,5},{8,10},{9,11},{10,... | collective-permute-start | bytes 294920 | tf_op jit(solution)/shard_map/ppermute | solution.py:365
  61.7 15.2 %collective-permute-start.13 = (bf16[80,1024]{1,0:T(8,128)(2,1)S(1)}, bf16[80,1024]{1,0:T(8,128)(2,1)S(1)}, u32[]{:S(2)}, u32[]{:S(2)}) collective-permute-start(bf16[80,1024]{1,0:T(8,128)(2,1)S(1)} %get-tuple-element.96.refs_1_), channel_id=1, source_target_pairs={{0,8},{1,9},{2,10},{3,11},{4,12},{5,13},{6,14},{7,15},{8,0},{9,1},... | collective-permute-start | bytes 491528 | tf_op jit(solution)/shard_map/ppermute | solution.py:365
  63.8 15.5 %collective-permute-start.12 = (bf16[80,1024]{1,0:T(8,128)(2,1)S(1)}, bf16[80,1024]{1,0:T(8,128)(2,1)S(1)}, u32[]{:S(2)}, u32[]{:S(2)}) collective-permute-start(bf16[80,1024]{1,0:T(8,128)(2,1)S(1)} %get-tuple-element.95.refs_4_.refs_0_), channel_id=1, source_target_pairs={{0,8},{1,9},{2,10},{3,11},{4,12},{5,13},{6,14},{7,15},{8,0},{9,1},... | collective-permute-start | bytes 491528 | tf_op jit(solution)/shard_map/ppermute | solution.py:365
  67.9 12.7 %collective-permute-start.18 = (bf16[160,1024]{1,0:T(8,128)(2,1)S(1)}, bf16[160,1024]{1,0:T(8,128)(2,1)S(1)}, u32[]{:S(2)}, u32[]{:S(2)}) collective-permute-start(bf16[160,1024]{1,0:T(8,128)(2,1)S(1)} %get-tuple-element.98.refs_4_.refs_0_), channel_id=1, source_target_pairs={{0,2},{1,3},{2,0},{3,1},{4,6},{5,7},{6,4},{7,5},{8,10},{9,11},{10,... | collective-permute-start | bytes 983048 | tf_op jit(solution)/shard_map/ppermute | solution.py:365
  69.0 11.6 %collective-permute-start.19 = (bf16[96,1024]{1,0:T(8,128)(2,1)S(1)}, bf16[96,1024]{1,0:T(8,128)(2,1)S(1)}, u32[]{:S(2)}, u32[]{:S(2)}) collective-permute-start(bf16[96,1024]{1,0:T(8,128)(2,1)S(1)} %get-tuple-element.101.refs_2_), channel_id=1, source_target_pairs={{0,4},{1,5},{2,6},{3,7},{4,0},{5,1},{6,2},{7,3},{8,12},{9,13},{10,... | collective-permute-start | bytes 589832 | tf_op jit(solution)/shard_map/ppermute | solution.py:365
  79.3 5.4 %collective-permute-start.17 = (bf16[80,1024]{1,0:T(8,128)(2,1)S(1)}, bf16[80,1024]{1,0:T(8,128)(2,1)S(1)}, u32[]{:S(2)}, u32[]{:S(2)}) collective-permute-start(bf16[80,1024]{1,0:T(8,128)(2,1)S(1)} %get-tuple-element.100.refs_2_), channel_id=1, source_target_pairs={{0,2},{1,3},{2,0},{3,1},{4,6},{5,7},{6,4},{7,5},{8,10},{9,11},{10,... | collective-permute-start | bytes 491528 | tf_op jit(solution)/shard_map/ppermute | solution.py:365
  80.3 5.3 %collective-permute-start.16 = (bf16[80,1024]{1,0:T(8,128)(2,1)S(1)}, bf16[80,1024]{1,0:T(8,128)(2,1)S(1)}, u32[]{:S(2)}, u32[]{:S(2)}) collective-permute-start(bf16[80,1024]{1,0:T(8,128)(2,1)S(1)} %get-tuple-element.99.refs_4_.refs_0_), channel_id=1, source_target_pairs={{0,4},{1,5},{2,6},{3,7},{4,0},{5,1},{6,2},{7,3},{8,12},{9,13},{10,... | collective-permute-start | bytes 491528 | tf_op jit(solution)/shard_map/ppermute | solution.py:365
  85.7 2.7 %collective-permute-start.22 = (bf16[512,1024]{1,0:T(8,128)(2,1)S(1)}, bf16[512,1024]{1,0:T(8,128)(2,1)S(1)}, u32[]{:S(2)}, u32[]{:S(2)}) collective-permute-start(bf16[512,1024]{1,0:T(8,128)(2,1)S(1)} %get-tuple-element.104.refs_0_), channel_id=1, source_target_pairs={{0,1},{1,0},{2,3},{3,2},{4,5},{5,4},{6,7},{7,6},{8,9},{9,8},{10,11... | collective-permute-start | bytes 3145736 | tf_op jit(solution)/shard_map/ppermute | solution.py:365
  85.8 10.1 %collective-permute-start.21 = (bf16[160,1024]{1,0:T(8,128)(2,1)S(1)}, bf16[160,1024]{1,0:T(8,128)(2,1)S(1)}, u32[]{:S(2)}, u32[]{:S(2)}) collective-permute-start(bf16[160,1024]{1,0:T(8,128)(2,1)S(1)} %get-tuple-element.103.refs_2_), channel_id=1, source_target_pairs={{0,4},{1,5},{2,6},{3,7},{4,0},{5,1},{6,2},{7,3},{8,12},{9,13},{10,... | collective-permute-start | bytes 983048 | tf_op jit(solution)/shard_map/ppermute | solution.py:365
  85.9 10.1 %collective-permute-start.20 = (bf16[160,1024]{1,0:T(8,128)(2,1)S(1)}, bf16[160,1024]{1,0:T(8,128)(2,1)S(1)}, u32[]{:S(2)}, u32[]{:S(2)}) collective-permute-start(bf16[160,1024]{1,0:T(8,128)(2,1)S(1)} %get-tuple-element.102.refs_1_.refs_0_), channel_id=1, source_target_pairs={{0,2},{1,3},{2,0},{3,1},{4,6},{5,7},{6,4},{7,5},{8,10},{9,11},{10,... | collective-permute-start | bytes 983048 | tf_op jit(solution)/shard_map/ppermute | solution.py:365
  96.1 3.1 %collective-permute-start.23 = (bf16[640,1024]{1,0:T(8,128)(2,1)S(1)}, bf16[640,1024]{1,0:T(8,128)(2,1)S(1)}, u32[]{:S(2)}, u32[]{:S(2)}) collective-permute-start(bf16[640,1024]{1,0:T(8,128)(2,1)S(1)} %shard_map.162.refs_0_), channel_id=1, source_target_pairs={{0,1},{1,0},{2,3},{3,2},{4,5},{5,4},{6,7},{7,6},{8,9},{9,8},{10,11... | collective-permute-start | bytes 3932168 | tf_op jit(solution)/shard_map/ppermute | solution.py:365

commit v6 on v5

--- a/solution.py
+++ b/solution.py
@@ -135,8 +135,8 @@
     return total.astype(BF)
 
 
-def back_through(delta, weights, slope, out):
-    for j in range(0, out.shape[1], BLOCK):
+def back_through(delta, weights, slope, out, start=0, stop=None):
+    for j in range(start, stop or out.shape[1], BLOCK):
         back = times_transposed(delta, weights[j : j + BLOCK])
         out[:, j : j + BLOCK] = (back * slope[:, j : j + BLOCK].astype(F32)).astype(BF)
 
@@ -220,16 +220,15 @@
     other[...] = weight_grad(((act1, delta2), (outs[1], outs[4])), at)
 
 
-def middle_body(
-    interior, act1, delta2, act1_p, delta2_p, slope1, mine, delta1, w_int, sems
-):
-    copy = pltpu.make_async_copy(interior.at[1], w_int, sems.at[0])
+def middle_body(interior, act1, delta2, act1_p, delta2_p, slope1, mine, low, w_int, sems):
+    units = low.shape[1]
+    copy = pltpu.make_async_copy(interior.at[1, pl.ds(0, units)], w_int, sems.at[0])
     copy.start()
     rows = mine.shape[0]
     at = pl.ds(pl.multiple_of(bit_of(1) * 2 * rows + bit_of(4) * rows, rows), rows)
     mine[...] = weight_grad(((act1, delta2), (act1_p, delta2_p)), at)
     copy.wait()
-    back_through(delta2[...], w_int, slope1, delta1)
+    back_through(delta2[...], w_int, slope1, low)
 
 
 def first_body(
@@ -238,7 +237,9 @@
     feat,
     act0,
     slope0,
-    delta1,
+    slope1,
+    delta2,
+    low,
     rest_in,
     feat_p,
     act0_p,
@@ -251,6 +252,7 @@
     other_1,
     other_2,
     other_3,
+    delta1,
     delta1_p,
     delta0,
     delta0_p,
@@ -267,7 +269,10 @@
     ]
     for copy in reversed(copies):
         copy.start()
+    units = low.shape[1]
+    delta1[:, :units] = low[...]
     copies[1].wait()
+    back_through(delta2[...], w_int.at[1], slope1, delta1, units)
     back_through(delta2_p[...], w_int.at[1], slope1_p, delta1_p)
     copies[0].wait()
     back_through(delta1[...], w_int.at[0], slope0, delta0)
@@ -574,16 +579,16 @@
         scratch=scratch,
         room=ROOM,
     )
-    mine, delta1 = call(
+    mine, begun = call(
         middle_body,
-        (half, act),
+        (half, Shape((cols, hid // 2), BF)),
         (interior, act1, delta2, act1_p, delta2_p, slope1),
         specs=[HBM] + [VMEM] * 5,
-        scratch=[pltpu.VMEM((hid, hid), BF), sem],
+        scratch=[pltpu.VMEM((hid // 2, hid), BF), sem],
         room=ROOM,
     )
     top = Sum(mine, [other], 1, 1, TOP_SHARE)
-    (token,) = top.split(delta1)
+    (token,) = top.split(begun)
     rows = rest_rows(n)
     part = Shape((hid // 4 + rows // 4, hid), BF)
     mine, *others = call(
@@ -594,7 +599,9 @@
             feat,
             act0,
             slope0,
-            delta1,
+            slope1,
+            delta2,
+            begun,
             rest,
             feat_p,
             act0_p,
@@ -604,9 +611,9 @@
             rest_p,
         ),
         token,
-        specs=[HBM] + [VMEM] * 11,
+        specs=[HBM] + [VMEM] * 13,
         scratch=[
-            *[one] * 3,
+            *[one] * 4,
             pltpu.VMEM((rows, hid), BF),
             pltpu.VMEM(part.shape, BF),
             pltpu.VMEM(interior.shape, BF),

time: 103 us -> 102 us (level)
  waiting for transfers between devices: 38.3 us -> 36.7 us
  starting transfers between devices: 24.9 us -> 26 us
    ppermute x23, waiting for transfers between devices: 38.2 us -> 36.7 us  [swap(): return lax.ppermute(x, 'tiles', [(t, t ^ stride) for t in range(n)])]
    ppermute x23, starting transfers between devices: 13.1 us -> 14.2 us  [swap(): return lax.ppermute(x, 'tiles', [(t, t ^ stride) for t in range(n)])]
  transfers between devices with their start and end apart: 25 -> 25, of which waited for: 17 -> 16; matrix products, arithmetic and copies ran while one was open for 2% -> 2% of each run, Pallas kernels for 22% -> 22%
where the time goes in v6:
time: 102 us; the launch traced here: 101 us
  waiting for transfers between devices  36.7 us (36%)
  Pallas kernels  33.6 us (33%)
  starting transfers between devices  26 us (25%)
  local copies, waits for them, and re-layouts  2.49 us (2%)
  other arithmetic  1.43 us (1%)
  between operations  1.04 us (1%)
    ppermute x23, waiting for transfers between devices, swap(): return lax.ppermute(x, 'tiles', [(t, t ^ stride) for t in range(n)])  36.7 us
    pallas_call x20, Pallas kernels, call(): pl.pallas_call(body, out_shape=outs + tuple((Shape(a.shape, a.dtype) for...  33.6 us
    ppermute x23, starting transfers between devices, swap(): return lax.ppermute(x, 'tiles', [(t, t ^ stride) for t in range(n)])  14.2 us
    all_to_all x1, starting transfers between devices, local(): lax.all_to_all(jnp.broadcast_to(intercepts.reshape(1, hid // 128, 128), (...  7.39 us
    ppermute x1, starting transfers between devices, local(): far = lax.ppermute(jnp.where(odd, last, first), 'tiles', pairs)  4.43 us
  transfers between devices with their start and end apart: 25, of which 16 were waited for; matrix products, arithmetic and copies ran while one was open for 2% of the time, Pallas kernels for 22%

profile of v6, /device:TPU:0, one launch (start us, length us, event | category | flops | bytes accessed | tf_op | source)
XLA Modules:
  0.0 101.4 jit_solution(1076524513038976559)
XLA Ops:
  0.6 1.3 %broadcast_in_dim.24 = f32[16,8,128]{2,1,0:T(8,128)} broadcast(f32[8,128]{1,0:T(8,128)} %bitcast.13), dimensions={1,2} | broadcast | bytes 69632 | tf_op jit(solution)/shard_map/broadcast_in_dim | solution.py:536
  2.0 7.4 %all-to-all-start = ((f32[16,8,128]{2,1,0:T(8,128)}), f32[16,8,128]{2,1,0:T(8,128)S(1)}, u32[]{:S(2)}, u32[]{:S(2)}) async-start(f32[16,8,128]{2,1,0:T(8,128)} %broadcast_in_dim.24), calls=%async_computation | async-start | bytes 131072 | tf_op jit(solution)/shard_map/all_to_all | solution.py:535
  9.4 0.7 select_convert_fusion
  10.1 0.8 slice_bitcast_fusion.2
  11.0 4.4 %collective-permute-start.1 = (f32[3,1,32,128]{3,2,1,0:T(8,128)S(1)}, f32[3,1,32,128]{3,2,1,0:T(8,128)S(1)}, u32[]{:S(2)}, u32[]{:S(2)}) collective-permute-start(f32[3,1,32,128]{3,2,1,0:T(8,128)S(1)} %get-tuple-element.118), channel_id=1, source_target_pairs={{0,15},{1,2},{2,1},{3,4},{4,3},{5,6},{6,5},{7,8},{8,7},{9,10},{10,... | collective-permute-start | bytes 147464 | tf_op jit(solution)/shard_map/ppermute | solution.py:534
  15.5 1.1 %shard_map.145 = (f32[16,32,128]{2,1,0:T(8,128)S(1)}, f32[16,32,128]{2,1,0:T(8,128)S(1)}, bf16[16,32,128]{2,1,0:T(8,128)(2,1)S(1)}) custom-call(f32[16,32,128]{2,1,0:T(8,128)} %refs_0_.3, f32[16,32,128]{2,1,0:T(8,128)} %refs_1_.1, bf16[16,32,128]{2,1,0:T(8,128)(2,1)} %refs_2_.3), custom_call_target="tpu_custom_call" | custom-call | flops 1 | bytes 1 | tf_op jit(solution)/shard_map/pallas_call | solution.py:66
  17.6 1.3 %shard_map.146 = (f32[2,16,32,128]{3,2,1,0:T(8,128)}, bf16[512,256]{1,0:T(8,128)(2,1)S(1)}) custom-call(f32[16,32,128]{2,1,0:T(8,128)S(1)} %broadcast_in_dim.10.refs_0_, f32[3,1,32,128]{3,2,1,0:T(8,128)S(1)} %collective-permute-done.refs_1_, f32[3,1,32,128]{3,2,1,0:T(8,128)S(1)} %collective-permute-done.1.refs_2_, ...), custom_call_target="tpu_custom_call" | custom-call | flops 1 | bytes 1 | tf_op jit(solution)/shard_map/pallas_call | solution.py:66
  19.0 6.6 %shard_map.147 = (bf16[16,32,128]{2,1,0:T(8,128)(2,1)}, bf16[256,1024]{1,0:T(8,128)(2,1)S(1)}, bf16[512,1024]{1,0:T(8,128)(2,1)S(1)}, bf16[512,1024]{1,0:T(8,128...) custom-call(bf16[512,256]{1,0:T(8,128)(2,1)S(1)} %get-tuple-element., ...), custom_call_target="tpu_custom_call" | custom-call | flops 1 | bytes 1 | tf_op jit(solution)/shard_map/pallas_call | solution.py:66
  25.6 1.9 %collective-permute-done.2.refs_0_ = bf16[512,256]{1,0:T(8,128)(2,1)S(1)} collective-permute-done((bf16[512,256]{1,0:T(8,128)(2,1)S(1)}, bf16[512,256]{1,0:T(8,128)(2,1)S(1)}, u32[]{:S(2)}, u32[]{:S(2)}) %collective-permute-start.2) | collective-permute-done | bytes 262176 | tf_op jit(solution)/shard_map/ppermute | solution.py:370
  27.5 6.8 %shard_map.148 = (bf16[512,1024]{1,0:T(8,128)(2,1)S(1)}, bf16[512,1024]{1,0:T(8,128)(2,1)S(1)}, bf16[512,1024]{1,0:T(8,128)(2,1)S(1)}, bf16[512,1024]{1,0:T(8,12...) custom-call(bf16[512,256]{1,0:T(8,128)(2,1)S(1)} %collective-permute, ...), custom_call_target="tpu_custom_call" | custom-call | flops 1 | bytes 1 | tf_op jit(solution)/shard_map/pallas_call | solution.py:66
  34.4 2.1 %shard_map.149 = (bf16[256,1024]{1,0:T(8,128)(2,1)S(1)}, bf16[512,512]{1,0:T(8,128)(2,1)S(1)}) custom-call(bf16[2,1024,1024]{2,1,0:T(8,128)(2,1)} %refs_0_.5, bf16[512,1024]{1,0:T(8,128)(2,1)S(1)} %get-tuple-element.71.refs_4_.refs_1_, bf16[512,1024]{1,0:T(8,128)(2,1)S(1)} %get-tuple-element.70.refs_5_.refs_2_, ...), custom_call_target="tpu_custom_call" | custom-call | flops 1 | bytes 1 | tf_op jit(solution)/shard_map/pallas_call | solution.py:66
  36.6 7.7 %shard_map.151 = (bf16[320,1024]{1,0:T(8,128)(2,1)S(1)}, bf16[80,1024]{1,0:T(8,128)(2,1)S(1)}, bf16[80,1024]{1,0:T(8,128)(2,1)S(1)}, bf16[80,1024]{1,0:T(8,128)(2,1)S(1)}, bf16[80,1024]{1,0:T(8,128)(2,1)S(1)}) custom-call(bf16[2,1024,1024]{2,1,0:T(8,128)(2,1)} %refs_0_.5, bf16[512,256]{1,0:T(8,128)(2,1)S(1)} %get-tuple-element.66.refs_1_, ...), custom_call_target="tpu_custom_call" | custom-call | flops 1 | bytes 1 | tf_op jit(solution)/shard_map/pallas_call | solution.py:66
  44.4 1.0 collective-permute-done.8.refs_1_
  45.4 2.6 %collective-permute-start.11 = (bf16[128,1024]{1,0:T(8,128)(2,1)S(1)}, bf16[128,1024]{1,0:T(8,128)(2,1)S(1)}, u32[]{:S(2)}, u32[]{:S(2)}) collective-permute-start(bf16[128,1024]{1,0:T(8,128)(2,1)S(1)} %shard_map.152.refs_5_.refs_0_), channel_id=1, source_target_pairs={{0,8},{1,9},{2,10},{3,11},{4,12},{5,13},{6,14},{7,15},{8,0},{9,1},... | collective-permute-start | bytes 786440 | tf_op jit(solution)/shard_map/ppermute | solution.py:370
  50.8 1.5 %collective-permute-start.10 = (bf16[80,1024]{1,0:T(8,128)(2,1)S(1)}, bf16[80,1024]{1,0:T(8,128)(2,1)S(1)}, u32[]{:S(2)}, u32[]{:S(2)}) collective-permute-start(bf16[80,1024]{1,0:T(8,128)(2,1)S(1)} %get-tuple-element.93), channel_id=1, source_target_pairs={{0,2},{1,3},{2,0},{3,1},{4,6},{5,7},{6,4},{7,5},{8,10},{9,11},{10,... | collective-permute-start | bytes 491528 | tf_op jit(solution)/shard_map/ppermute | solution.py:370
  52.3 7.6 %collective-permute-done.11.refs_1_ = bf16[128,1024]{1,0:T(8,128)(2,1)S(1)} collective-permute-done((bf16[128,1024]{1,0:T(8,128)(2,1)S(1)}, bf16[128,1024]{1,0:T(8,128)(2,1)S(1)}, u32[]{:S(2)}, u32[]{:S(2)}) %collective-permute-start.11) | collective-permute-done | bytes 262176 | tf_op jit(solution)/shard_map/ppermute | solution.py:370
  60.0 1.3 %collective-permute-start.15 = (bf16[48,1024]{1,0:T(8,128)(2,1)S(1)}, bf16[48,1024]{1,0:T(8,128)(2,1)S(1)}, u32[]{:S(2)}, u32[]{:S(2)}) collective-permute-start(bf16[48,1024]{1,0:T(8,128)(2,1)S(1)} %get-tuple-element.97.refs_2_), channel_id=1, source_target_pairs={{0,2},{1,3},{2,0},{3,1},{4,6},{5,7},{6,4},{7,5},{8,10},{9,11},{10,... | collective-permute-start | bytes 294920 | tf_op jit(solution)/shard_map/ppermute | solution.py:370
  61.4 1.9 %collective-permute-start.13 = (bf16[80,1024]{1,0:T(8,128)(2,1)S(1)}, bf16[80,1024]{1,0:T(8,128)(2,1)S(1)}, u32[]{:S(2)}, u32[]{:S(2)}) collective-permute-start(bf16[80,1024]{1,0:T(8,128)(2,1)S(1)} %get-tuple-element.96.refs_1_), channel_id=1, source_target_pairs={{0,8},{1,9},{2,10},{3,11},{4,12},{5,13},{6,14},{7,15},{8,0},{9,1},... | collective-permute-start | bytes 491528 | tf_op jit(solution)/shard_map/ppermute | solution.py:370
  63.2 1.1 %collective-permute-start.12 = (bf16[80,1024]{1,0:T(8,128)(2,1)S(1)}, bf16[80,1024]{1,0:T(8,128)(2,1)S(1)}, u32[]{:S(2)}, u32[]{:S(2)}) collective-permute-start(bf16[80,1024]{1,0:T(8,128)(2,1)S(1)} %get-tuple-element.95.refs_4_.refs_0_), channel_id=1, source_target_pairs={{0,8},{1,9},{2,10},{3,11},{4,12},{5,13},{6,14},{7,15},{8,0},{9,1},... | collective-permute-start | bytes 491528 | tf_op jit(solution)/shard_map/ppermute | solution.py:370
  64.7 2.5 %collective-permute-done.14.refs_1_ = bf16[80,1024]{1,0:T(8,128)(2,1)S(1)} collective-permute-done((bf16[80,1024]{1,0:T(8,128)(2,1)S(1)}, bf16[80,1024]{1,0:T(8,128)(2,1)S(1)}, u32[]{:S(2)}, u32[]{:S(2)}) %collective-permute-start.14) | collective-permute-done | bytes 163872 | tf_op jit(solution)/shard_map/ppermute | solution.py:370
  67.2 1.4 %collective-permute-start.18 = (bf16[160,1024]{1,0:T(8,128)(2,1)S(1)}, bf16[160,1024]{1,0:T(8,128)(2,1)S(1)}, u32[]{:S(2)}, u32[]{:S(2)}) collective-permute-start(bf16[160,1024]{1,0:T(8,128)(2,1)S(1)} %get-tuple-element.98.refs_4_.refs_0_), channel_id=1, source_target_pairs={{0,2},{1,3},{2,0},{3,1},{4,6},{5,7},{6,4},{7,5},{8,10},{9,11},{10,... | collective-permute-start | bytes 983048 | tf_op jit(solution)/shard_map/ppermute | solution.py:370
  68.7 7.9 %collective-permute-done.13.refs_3_ = bf16[80,1024]{1,0:T(8,128)(2,1)S(1)} collective-permute-done((bf16[80,1024]{1,0:T(8,128)(2,1)S(1)}, bf16[80,1024]{1,0:T(8,128)(2,1)S(1)}, u32[]{:S(2)}, u32[]{:S(2)}) %collective-permute-start.13) | collective-permute-done | bytes 163872 | tf_op jit(solution)/shard_map/ppermute | solution.py:370
  76.5 2.3 %collective-permute-done.12.refs_2_ = bf16[80,1024]{1,0:T(8,128)(2,1)S(1)} collective-permute-done((bf16[80,1024]{1,0:T(8,128)(2,1)S(1)}, bf16[80,1024]{1,0:T(8,128)(2,1)S(1)}, u32[]{:S(2)}, u32[]{:S(2)}) %collective-permute-start.12) | collective-permute-done | bytes 163872 | tf_op jit(solution)/shard_map/ppermute | solution.py:370
  78.9 0.7 collective-permute-start.17
  80.4 4.0 %collective-permute-done.17.refs_3_ = bf16[80,1024]{1,0:T(8,128)(2,1)S(1)} collective-permute-done((bf16[80,1024]{1,0:T(8,128)(2,1)S(1)}, bf16[80,1024]{1,0:T(8,128)(2,1)S(1)}, u32[]{:S(2)}, u32[]{:S(2)}) %collective-permute-start.17) | collective-permute-done | bytes 163872 | tf_op jit(solution)/shard_map/ppermute | solution.py:370
  85.2 1.4 %collective-permute-start.20 = (bf16[160,1024]{1,0:T(8,128)(2,1)S(1)}, bf16[160,1024]{1,0:T(8,128)(2,1)S(1)}, u32[]{:S(2)}, u32[]{:S(2)}) collective-permute-start(bf16[160,1024]{1,0:T(8,128)(2,1)S(1)} %get-tuple-element.102.refs_1_.refs_0_), channel_id=1, source_target_pairs={{0,2},{1,3},{2,0},{3,1},{4,6},{5,7},{6,4},{7,5},{8,10},{9,11},{10,... | collective-permute-start | bytes 983048 | tf_op jit(solution)/shard_map/ppermute | solution.py:370
  86.6 1.4 %shard_map.160 = (f32[2,1024,1024]{2,1,0:T(8,128)}, f32[8,128]{1,0:T(8,128)S(1)}) custom-call(bf16[512,1024]{1,0:T(8,128)(2,1)S(1)} %get-tuple-element.104.refs_0_, bf16[160,1024]{1,0:T(8,128)(2,1)S(1)} %get-tuple-element.102.refs_1_.refs_0_), custom_call_target="tpu_custom_call" | custom-call | flops 1 | bytes 1 | tf_op jit(solution)/shard_map/pallas_call | solution.py:66
  88.0 1.4 %shard_map.161 = (f32[2,1024,1024]{2,1,0:T(8,128)}, f32[8,128]{1,0:T(8,128)S(1)}) custom-call(bf16[512,1024]{1,0:T(8,128)(2,1)S(1)} %collective-permute-done.22.refs_0_, f32[2,1024,1024]{2,1,0:T(8,128)} %get-tuple-element.105.refs_1_, f32[8,128]{1,0:T(8,128)S(1)} %get-tuple-element.106.refs_2_), custom_call_target="tpu_custom_call", output_to_operand_aliasing={{0}: (1, {})} | custom-call | flops 1 | bytes 1 | tf_op jit(solution)/shard_map/pallas_call | solution.py:66
  89.4 5.8 %collective-permute-done.21.refs_3_ = bf16[160,1024]{1,0:T(8,128)(2,1)S(1)} collective-permute-done((bf16[160,1024]{1,0:T(8,128)(2,1)S(1)}, bf16[160,1024]{1,0:T(8,128)(2,1)S(1)}, u32[]{:S(2)}, u32[]{:S(2)}) %collective-permute-start.21) | collective-permute-done | bytes 327712 | tf_op jit(solution)/shard_map/ppermute | solution.py:370
  95.4 2.0 %shard_map.163 = (f32[2,1024,1024]{2,1,0:T(8,128)}, f32[8,128]{1,0:T(8,128)}) custom-call(bf16[640,1024]{1,0:T(8,128)(2,1)S(1)} %shard_map.162.refs_0_, f32[2,1024,1024]{2,1,0:T(8,128)} %get-tuple-element.108.refs_1_), custom_call_target="tpu_custom_call", output_to_operand_aliasing={{0}: (1, {})} | custom-call | flops 1 | bytes 1 | tf_op jit(solution)/shard_map/pallas_call | solution.py:66
  97.4 1.0 %collective-permute-done.23.refs_1_ = bf16[640,1024]{1,0:T(8,128)(2,1)S(1)} collective-permute-done((bf16[640,1024]{1,0:T(8,128)(2,1)S(1)}, bf16[640,1024]{1,0:T(8,128)(2,1)S(1)}, u32[]{:S(2)}, u32[]{:S(2)}) %collective-permute-start.23) | collective-permute-done | bytes 1310752 | tf_op jit(solution)/shard_map/ppermute | solution.py:370
  98.5 2.8 %shard_map.164 = (f32[2,1024,1024]{2,1,0:T(8,128)}, f32[256,1024]{1,0:T(8,128)}, f32[1024,128]{1,0:T(8,128)}, f32[1,1024]{1,0:T(1,128)}) custom-call(bf16[640,1024]{1,0:T(8,128)(2,1)S(1)} %shard_map.162.refs_0_, bf16[640,1024]{1,0:T(8,128)(2,1)S(1)} %collective-permute-done.23.refs_1_, ...), custom_call_target="tpu_custom_call", output_to_operand_aliasing={{0}: (2, {})} | custom-call | flops 1 | bytes 1 | tf_op jit(solution)/shard_map/pallas_call | solution.py:66
  (48 shorter events, 6.7 us)
Async XLA Ops:
  2.0 15.3 %all-to-all-start = ((f32[16,8,128]{2,1,0:T(8,128)}), f32[16,8,128]{2,1,0:T(8,128)S(1)}, u32[]{:S(2)}, u32[]{:S(2)}) async-start(f32[16,8,128]{2,1,0:T(8,128)} %broadcast_in_dim.24), calls=%async_computation | async-start | bytes 131072 | tf_op jit(solution)/shard_map/all_to_all | solution.py:535
  11.0 6.3 %collective-permute-start.1 = (f32[3,1,32,128]{3,2,1,0:T(8,128)S(1)}, f32[3,1,32,128]{3,2,1,0:T(8,128)S(1)}, u32[]{:S(2)}, u32[]{:S(2)}) collective-permute-start(f32[3,1,32,128]{3,2,1,0:T(8,128)S(1)} %get-tuple-element.118), channel_id=1, source_target_pairs={{0,15},{1,2},{2,1},{3,4},{4,3},{5,6},{6,5},{7,8},{8,7},{9,10},{10,... | collective-permute-start | bytes 147464 | tf_op jit(solution)/shard_map/ppermute | solution.py:534
  15.4 1.8 %collective-permute-start = (f32[3,1,32,128]{3,2,1,0:T(8,128)S(1)}, f32[3,1,32,128]{3,2,1,0:T(8,128)S(1)}, u32[]{:S(2)}, u32[]{:S(2)}) collective-permute-start(f32[3,1,32,128]{3,2,1,0:T(8,128)S(1)} %get-tuple-element.119), channel_id=1, source_target_pairs={{0,1},{1,0},{2,3},{3,2},{4,5},{5,4},{6,7},{7,6},{8,9},{9,8},{10,11... | collective-permute-start | bytes 147464 | tf_op jit(solution)/shard_map/ppermute | solution.py:370
  18.9 8.7 %collective-permute-start.2 = (bf16[512,256]{1,0:T(8,128)(2,1)S(1)}, bf16[512,256]{1,0:T(8,128)(2,1)S(1)}, u32[]{:S(2)}, u32[]{:S(2)}) collective-permute-start(bf16[512,256]{1,0:T(8,128)(2,1)S(1)} %get-tuple-element.64.refs_0_), channel_id=1, source_target_pairs={{0,4},{1,5},{2,6},{3,7},{4,0},{5,1},{6,2},{7,3},{8,12},{9,13},{10,... | collective-permute-start | bytes 786440 | tf_op jit(solution)/shard_map/ppermute | solution.py:370
  34.3 2.2 %collective-permute-start.3 = (bf16[256,1024]{1,0:T(8,128)(2,1)S(1)}, bf16[256,1024]{1,0:T(8,128)(2,1)S(1)}, u32[]{:S(2)}, u32[]{:S(2)}) collective-permute-start(bf16[256,1024]{1,0:T(8,128)(2,1)S(1)} %get-tuple-element.83), channel_id=1, source_target_pairs={{0,1},{1,0},{2,3},{3,2},{4,5},{5,4},{6,7},{7,6},{8,9},{9,8},{10,11... | collective-permute-start | bytes 1572872 | tf_op jit(solution)/shard_map/ppermute | solution.py:370
  36.6 8.8 %collective-permute-start.8 = (bf16[128,1024]{1,0:T(8,128)(2,1)S(1)}, bf16[128,1024]{1,0:T(8,128)(2,1)S(1)}, u32[]{:S(2)}, u32[]{:S(2)}) collective-permute-start(bf16[128,1024]{1,0:T(8,128)(2,1)S(1)} %get-tuple-element.90), channel_id=1, source_target_pairs={{0,2},{1,3},{2,0},{3,1},{4,6},{5,7},{6,4},{7,5},{8,10},{9,11},{10,... | collective-permute-start | bytes 786440 | tf_op jit(solution)/shard_map/ppermute | solution.py:370
  45.4 14.5 %collective-permute-start.11 = (bf16[128,1024]{1,0:T(8,128)(2,1)S(1)}, bf16[128,1024]{1,0:T(8,128)(2,1)S(1)}, u32[]{:S(2)}, u32[]{:S(2)}) collective-permute-start(bf16[128,1024]{1,0:T(8,128)(2,1)S(1)} %shard_map.152.refs_5_.refs_0_), channel_id=1, source_target_pairs={{0,8},{1,9},{2,10},{3,11},{4,12},{5,13},{6,14},{7,15},{8,0},{9,1},... | collective-permute-start | bytes 786440 | tf_op jit(solution)/shard_map/ppermute | solution.py:370
  48.0 1.4 %collective-permute-start.4 = (bf16[80,1024]{1,0:T(8,128)(2,1)S(1)}, bf16[80,1024]{1,0:T(8,128)(2,1)S(1)}, u32[]{:S(2)}, u32[]{:S(2)}) collective-permute-start(bf16[80,1024]{1,0:T(8,128)(2,1)S(1)} %get-tuple-element.86), channel_id=1, source_target_pairs={{0,1},{1,0},{2,3},{3,2},{4,5},{5,4},{6,7},{7,6},{8,9},{9,8},{10,11... | collective-permute-start | bytes 491528 | tf_op jit(solution)/shard_map/ppermute | solution.py:370
  48.0 1.6 %collective-permute-start.5 = (bf16[80,1024]{1,0:T(8,128)(2,1)S(1)}, bf16[80,1024]{1,0:T(8,128)(2,1)S(1)}, u32[]{:S(2)}, u32[]{:S(2)}) collective-permute-start(bf16[80,1024]{1,0:T(8,128)(2,1)S(1)} %get-tuple-element.87), channel_id=1, source_target_pairs={{0,1},{1,0},{2,3},{3,2},{4,5},{5,4},{6,7},{7,6},{8,9},{9,8},{10,11... | collective-permute-start | bytes 491528 | tf_op jit(solution)/shard_map/ppermute | solution.py:370
  48.5 1.4 %collective-permute-start.6 = (bf16[80,1024]{1,0:T(8,128)(2,1)S(1)}, bf16[80,1024]{1,0:T(8,128)(2,1)S(1)}, u32[]{:S(2)}, u32[]{:S(2)}) collective-permute-start(bf16[80,1024]{1,0:T(8,128)(2,1)S(1)} %get-tuple-element.88), channel_id=1, source_target_pairs={{0,1},{1,0},{2,3},{3,2},{4,5},{5,4},{6,7},{7,6},{8,9},{9,8},{10,11... | collective-permute-start | bytes 491528 | tf_op jit(solution)/shard_map/ppermute | solution.py:370
  48.5 1.6 %collective-permute-start.7 = (bf16[80,1024]{1,0:T(8,128)(2,1)S(1)}, bf16[80,1024]{1,0:T(8,128)(2,1)S(1)}, u32[]{:S(2)}, u32[]{:S(2)}) collective-permute-start(bf16[80,1024]{1,0:T(8,128)(2,1)S(1)} %get-tuple-element.89), channel_id=1, source_target_pairs={{0,1},{1,0},{2,3},{3,2},{4,5},{5,4},{6,7},{7,6},{8,9},{9,8},{10,11... | collective-permute-start | bytes 491528 | tf_op jit(solution)/shard_map/ppermute | solution.py:370
  50.2 11.1 %collective-permute-start.9 = (bf16[80,1024]{1,0:T(8,128)(2,1)S(1)}, bf16[80,1024]{1,0:T(8,128)(2,1)S(1)}, u32[]{:S(2)}, u32[]{:S(2)}) collective-permute-start(bf16[80,1024]{1,0:T(8,128)(2,1)S(1)} %get-tuple-element.92), channel_id=1, source_target_pairs={{0,2},{1,3},{2,0},{3,1},{4,6},{5,7},{6,4},{7,5},{8,10},{9,11},{10,... | collective-permute-start | bytes 491528 | tf_op jit(solution)/shard_map/ppermute | solution.py:370
  50.8 10.5 %collective-permute-start.10 = (bf16[80,1024]{1,0:T(8,128)(2,1)S(1)}, bf16[80,1024]{1,0:T(8,128)(2,1)S(1)}, u32[]{:S(2)}, u32[]{:S(2)}) collective-permute-start(bf16[80,1024]{1,0:T(8,128)(2,1)S(1)} %get-tuple-element.93), channel_id=1, source_target_pairs={{0,2},{1,3},{2,0},{3,1},{4,6},{5,7},{6,4},{7,5},{8,10},{9,11},{10,... | collective-permute-start | bytes 491528 | tf_op jit(solution)/shard_map/ppermute | solution.py:370
  59.9 7.3 %collective-permute-start.14 = (bf16[80,1024]{1,0:T(8,128)(2,1)S(1)}, bf16[80,1024]{1,0:T(8,128)(2,1)S(1)}, u32[]{:S(2)}, u32[]{:S(2)}) collective-permute-start(bf16[80,1024]{1,0:T(8,128)(2,1)S(1)} %get-tuple-element.94.refs_3_.refs_0_), channel_id=1, source_target_pairs={{0,4},{1,5},{2,6},{3,7},{4,0},{5,1},{6,2},{7,3},{8,12},{9,13},{10,... | collective-permute-start | bytes 491528 | tf_op jit(solution)/shard_map/ppermute | solution.py:370
  60.0 4.7 %collective-permute-start.15 = (bf16[48,1024]{1,0:T(8,128)(2,1)S(1)}, bf16[48,1024]{1,0:T(8,128)(2,1)S(1)}, u32[]{:S(2)}, u32[]{:S(2)}) collective-permute-start(bf16[48,1024]{1,0:T(8,128)(2,1)S(1)} %get-tuple-element.97.refs_2_), channel_id=1, source_target_pairs={{0,2},{1,3},{2,0},{3,1},{4,6},{5,7},{6,4},{7,5},{8,10},{9,11},{10,... | collective-permute-start | bytes 294920 | tf_op jit(solution)/shard_map/ppermute | solution.py:370
  61.4 15.2 %collective-permute-start.13 = (bf16[80,1024]{1,0:T(8,128)(2,1)S(1)}, bf16[80,1024]{1,0:T(8,128)(2,1)S(1)}, u32[]{:S(2)}, u32[]{:S(2)}) collective-permute-start(bf16[80,1024]{1,0:T(8,128)(2,1)S(1)} %get-tuple-element.96.refs_1_), channel_id=1, source_target_pairs={{0,8},{1,9},{2,10},{3,11},{4,12},{5,13},{6,14},{7,15},{8,0},{9,1},... | collective-permute-start | bytes 491528 | tf_op jit(solution)/shard_map/ppermute | solution.py:370
  63.2 15.6 %collective-permute-start.12 = (bf16[80,1024]{1,0:T(8,128)(2,1)S(1)}, bf16[80,1024]{1,0:T(8,128)(2,1)S(1)}, u32[]{:S(2)}, u32[]{:S(2)}) collective-permute-start(bf16[80,1024]{1,0:T(8,128)(2,1)S(1)} %get-tuple-element.95.refs_4_.refs_0_), channel_id=1, source_target_pairs={{0,8},{1,9},{2,10},{3,11},{4,12},{5,13},{6,14},{7,15},{8,0},{9,1},... | collective-permute-start | bytes 491528 | tf_op jit(solution)/shard_map/ppermute | solution.py:370
  67.2 13.0 %collective-permute-start.18 = (bf16[160,1024]{1,0:T(8,128)(2,1)S(1)}, bf16[160,1024]{1,0:T(8,128)(2,1)S(1)}, u32[]{:S(2)}, u32[]{:S(2)}) collective-permute-start(bf16[160,1024]{1,0:T(8,128)(2,1)S(1)} %get-tuple-element.98.refs_4_.refs_0_), channel_id=1, source_target_pairs={{0,2},{1,3},{2,0},{3,1},{4,6},{5,7},{6,4},{7,5},{8,10},{9,11},{10,... | collective-permute-start | bytes 983048 | tf_op jit(solution)/shard_map/ppermute | solution.py:370
  68.7 11.6 %collective-permute-start.19 = (bf16[96,1024]{1,0:T(8,128)(2,1)S(1)}, bf16[96,1024]{1,0:T(8,128)(2,1)S(1)}, u32[]{:S(2)}, u32[]{:S(2)}) collective-permute-start(bf16[96,1024]{1,0:T(8,128)(2,1)S(1)} %get-tuple-element.101.refs_2_), channel_id=1, source_target_pairs={{0,4},{1,5},{2,6},{3,7},{4,0},{5,1},{6,2},{7,3},{8,12},{9,13},{10,... | collective-permute-start | bytes 589832 | tf_op jit(solution)/shard_map/ppermute | solution.py:370
  78.9 5.4 %collective-permute-start.17 = (bf16[80,1024]{1,0:T(8,128)(2,1)S(1)}, bf16[80,1024]{1,0:T(8,128)(2,1)S(1)}, u32[]{:S(2)}, u32[]{:S(2)}) collective-permute-start(bf16[80,1024]{1,0:T(8,128)(2,1)S(1)} %get-tuple-element.100.refs_2_), channel_id=1, source_target_pairs={{0,2},{1,3},{2,0},{3,1},{4,6},{5,7},{6,4},{7,5},{8,10},{9,11},{10,... | collective-permute-start | bytes 491528 | tf_op jit(solution)/shard_map/ppermute | solution.py:370
  79.7 5.3 %collective-permute-start.16 = (bf16[80,1024]{1,0:T(8,128)(2,1)S(1)}, bf16[80,1024]{1,0:T(8,128)(2,1)S(1)}, u32[]{:S(2)}, u32[]{:S(2)}) collective-permute-start(bf16[80,1024]{1,0:T(8,128)(2,1)S(1)} %get-tuple-element.99.refs_4_.refs_0_), channel_id=1, source_target_pairs={{0,4},{1,5},{2,6},{3,7},{4,0},{5,1},{6,2},{7,3},{8,12},{9,13},{10,... | collective-permute-start | bytes 491528 | tf_op jit(solution)/shard_map/ppermute | solution.py:370
  85.0 3.0 %collective-permute-start.22 = (bf16[512,1024]{1,0:T(8,128)(2,1)S(1)}, bf16[512,1024]{1,0:T(8,128)(2,1)S(1)}, u32[]{:S(2)}, u32[]{:S(2)}) collective-permute-start(bf16[512,1024]{1,0:T(8,128)(2,1)S(1)} %get-tuple-element.104.refs_0_), channel_id=1, source_target_pairs={{0,1},{1,0},{2,3},{3,2},{4,5},{5,4},{6,7},{7,6},{8,9},{9,8},{10,11... | collective-permute-start | bytes 3145736 | tf_op jit(solution)/shard_map/ppermute | solution.py:370
  85.1 10.1 %collective-permute-start.21 = (bf16[160,1024]{1,0:T(8,128)(2,1)S(1)}, bf16[160,1024]{1,0:T(8,128)(2,1)S(1)}, u32[]{:S(2)}, u32[]{:S(2)}) collective-permute-start(bf16[160,1024]{1,0:T(8,128)(2,1)S(1)} %get-tuple-element.103.refs_2_), channel_id=1, source_target_pairs={{0,4},{1,5},{2,6},{3,7},{4,0},{5,1},{6,2},{7,3},{8,12},{9,13},{10,... | collective-permute-start | bytes 983048 | tf_op jit(solution)/shard_map/ppermute | solution.py:370
  85.2 10.1 %collective-permute-start.20 = (bf16[160,1024]{1,0:T(8,128)(2,1)S(1)}, bf16[160,1024]{1,0:T(8,128)(2,1)S(1)}, u32[]{:S(2)}, u32[]{:S(2)}) collective-permute-start(bf16[160,1024]{1,0:T(8,128)(2,1)S(1)} %get-tuple-element.102.refs_1_.refs_0_), channel_id=1, source_target_pairs={{0,2},{1,3},{2,0},{3,1},{4,6},{5,7},{6,4},{7,5},{8,10},{9,11},{10,... | collective-permute-start | bytes 983048 | tf_op jit(solution)/shard_map/ppermute | solution.py:370
  95.4 3.1 %collective-permute-start.23 = (bf16[640,1024]{1,0:T(8,128)(2,1)S(1)}, bf16[640,1024]{1,0:T(8,128)(2,1)S(1)}, u32[]{:S(2)}, u32[]{:S(2)}) collective-permute-start(bf16[640,1024]{1,0:T(8,128)(2,1)S(1)} %shard_map.162.refs_0_), channel_id=1, source_target_pairs={{0,1},{1,0},{2,3},{3,2},{4,5},{5,4},{6,7},{7,6},{8,9},{9,8},{10,11... | collective-permute-start | bytes 3932168 | tf_op jit(solution)/shard_map/ppermute | solution.py:370

commit v7 on v6

--- a/solution.py
+++ b/solution.py
@@ -93,7 +93,7 @@
         copy.wait()
 
 
-def step_body(depth, near, far, owner, warm, brine, desired, stepped, pack):
+def step_body(planes, near, far, warm, brine, desired, stepped, pack):
     lon, lat, levels = warm.shape
     cols = lon * lat
     odd = bit_of(1) == 1
@@ -101,7 +101,7 @@
     after = jnp.where(odd, far[...], near[...])
     level = lax.broadcasted_iota(jnp.int32, (lon, lat, levels), 2).astype(F32)
     row = lax.broadcasted_iota(jnp.int32, (lon, lat, levels), 1)
-    wet = (level < depth[...]).astype(F32)
+    wet = (level < planes[0]).astype(F32)
     wet_b = (level[:1] < before[2]).astype(F32)
     wet_a = (level[:1] < after[2]).astype(F32)
     wet_e = jnp.concatenate([wet[1:], wet_a], 0)
@@ -120,8 +120,8 @@
         stepped[i] = out
         group = (out * wet).reshape(cols, levels)
         if i == 0:
-            group = jnp.where(lane == KEPT - 2, owner[...].reshape(cols, levels), group)
-            group = jnp.where(lane == KEPT - 1, depth[...].reshape(cols, levels), group)
+            group = jnp.where(lane == KEPT - 2, planes[1].reshape(cols, levels), group)
+            group = jnp.where(lane == KEPT - 1, planes[0].reshape(cols, levels), group)
         beside = pltpu.roll(target, (KEPT - i * PACKED) % levels, 1)
         group = jnp.where(lane >= KEPT, beside, group)
         pack[:, i * levels : (i + 1) * levels] = group.astype(BF)
@@ -523,9 +523,9 @@
     scale = 1.0 / math.sqrt(cols * n)
 
     wide = (lon, lat, levels)
-    depth = jnp.where(flags > 0, tally, 0).astype(F32)
-    depth = jnp.broadcast_to(depth[:, :, None], wide)
-    owner = jnp.broadcast_to(assigned[:, :, None].astype(F32), wide)
+    numbers = jnp.stack([jnp.where(flags > 0, tally, 0), assigned]).astype(F32)
+    planes = jnp.broadcast_to(numbers[..., None], (2,) + wide)
+    depth = planes[0]
     odd = bit_of(1) == 1
     first = jnp.stack([warmth[:1], brine[:1], depth[:1]])
     last = jnp.stack([warmth[-1:], brine[-1:], depth[-1:]])
@@ -553,7 +553,7 @@
     stepped, pack = call(
         step_body,
         (Shape((2,) + wide, F32), Shape((cols, 2 * levels), BF)),
-        (depth, near, far, owner, warmth, brine, desired),
+        (planes, near, far, warmth, brine, desired),
         bias,
     )
     pack_p = swap(pack, 4)

time: 102 us -> 102 us (level)
  no operation moved by 1% of the time
where the time goes in v7:
time: 102 us; the launch traced here: 101 us
  waiting for transfers between devices  36.9 us (36%)
  Pallas kernels  33.6 us (33%)
  starting transfers between devices  26 us (25%)
  local copies, waits for them, and re-layouts  2.43 us (2%)
  other arithmetic  1.44 us (1%)
  between operations  1.03 us (1%)
    ppermute x23, waiting for transfers between devices, swap(): return lax.ppermute(x, 'tiles', [(t, t ^ stride) for t in range(n)])  36.9 us
    pallas_call x20, Pallas kernels, call(): pl.pallas_call(body, out_shape=outs + tuple((Shape(a.shape, a.dtype) for...  33.6 us
    ppermute x23, starting transfers between devices, swap(): return lax.ppermute(x, 'tiles', [(t, t ^ stride) for t in range(n)])  14.1 us
    all_to_all x1, starting transfers between devices, local(): lax.all_to_all(jnp.broadcast_to(intercepts.reshape(1, hid // 128, 128), (...  7.39 us
    ppermute x1, starting transfers between devices, local(): far = lax.ppermute(jnp.where(odd, last, first), 'tiles', pairs)  4.43 us
  transfers between devices with their start and end apart: 25, of which 16 were waited for; matrix products, arithmetic and copies ran while one was open for 2% of the time, Pallas kernels for 22%

profile of v7, /device:TPU:0, one launch (start us, length us, event | category | flops | bytes accessed | tf_op | source)
XLA Modules:
  0.0 101.4 jit_solution(1676620836745058680)
XLA Ops:
  0.6 1.3 %broadcast_in_dim.23 = f32[16,8,128]{2,1,0:T(8,128)} broadcast(f32[8,128]{1,0:T(8,128)} %bitcast.21), dimensions={1,2} | broadcast | bytes 69632 | tf_op jit(solution)/shard_map/broadcast_in_dim | solution.py:536
  2.0 7.4 %all-to-all-start = ((f32[16,8,128]{2,1,0:T(8,128)}), f32[16,8,128]{2,1,0:T(8,128)S(1)}, u32[]{:S(2)}, u32[]{:S(2)}) async-start(f32[16,8,128]{2,1,0:T(8,128)} %broadcast_in_dim.23), calls=%async_computation | async-start | bytes 131072 | tf_op jit(solution)/shard_map/all_to_all | solution.py:535
  9.4 0.7 fusion.2
  10.1 0.8 slice_bitcast_fusion.2
  11.0 4.4 %collective-permute-start.1 = (f32[3,1,32,128]{3,2,1,0:T(8,128)S(1)}, f32[3,1,32,128]{3,2,1,0:T(8,128)S(1)}, u32[]{:S(2)}, u32[]{:S(2)}) collective-permute-start(f32[3,1,32,128]{3,2,1,0:T(8,128)S(1)} %get-tuple-element.118), channel_id=1, source_target_pairs={{0,15},{1,2},{2,1},{3,4},{4,3},{5,6},{6,5},{7,8},{8,7},{9,10},{10,... | collective-permute-start | bytes 147464 | tf_op jit(solution)/shard_map/ppermute | solution.py:534
  16.2 1.1 %shard_map.145 = (f32[16,32,128]{2,1,0:T(8,128)S(1)}, f32[16,32,128]{2,1,0:T(8,128)S(1)}, bf16[16,32,128]{2,1,0:T(8,128)(2,1)S(1)}) custom-call(f32[16,32,128]{2,1,0:T(8,128)} %refs_0_.3, f32[16,32,128]{2,1,0:T(8,128)} %refs_1_.1, bf16[16,32,128]{2,1,0:T(8,128)(2,1)} %refs_2_.3), custom_call_target="tpu_custom_call" | custom-call | flops 1 | bytes 1 | tf_op jit(solution)/shard_map/pallas_call | solution.py:66
  17.5 1.3 %shard_map.146 = (f32[2,16,32,128]{3,2,1,0:T(8,128)}, bf16[512,256]{1,0:T(8,128)(2,1)S(1)}) custom-call(f32[2,16,32,128]{3,2,1,0:T(8,128)S(1)} %broadcast_in_dim.19.refs_0_, f32[3,1,32,128]{3,2,1,0:T(8,128)S(1)} %collective-permute-done.refs_1_, f32[3,1,32,128]{3,2,1,0:T(8,128)S(1)} %collective-permute-done.1.refs_2_, ...), custom_call_target="tpu_custom_call" | custom-call | flops 1 | bytes 1 | tf_op jit(solution)/shard_map/pallas_call | solution.py:66
  19.0 6.6 %shard_map.147 = (bf16[16,32,128]{2,1,0:T(8,128)(2,1)}, bf16[256,1024]{1,0:T(8,128)(2,1)S(1)}, bf16[512,1024]{1,0:T(8,128)(2,1)S(1)}, bf16[512,1024]{1,0:T(8,128...) custom-call(bf16[512,256]{1,0:T(8,128)(2,1)S(1)} %get-tuple-element., ...), custom_call_target="tpu_custom_call" | custom-call | flops 1 | bytes 1 | tf_op jit(solution)/shard_map/pallas_call | solution.py:66
  25.6 2.0 %collective-permute-done.2.refs_0_ = bf16[512,256]{1,0:T(8,128)(2,1)S(1)} collective-permute-done((bf16[512,256]{1,0:T(8,128)(2,1)S(1)}, bf16[512,256]{1,0:T(8,128)(2,1)S(1)}, u32[]{:S(2)}, u32[]{:S(2)}) %collective-permute-start.2) | collective-permute-done | bytes 262176 | tf_op jit(solution)/shard_map/ppermute | solution.py:370
  27.5 6.8 %shard_map.148 = (bf16[512,1024]{1,0:T(8,128)(2,1)S(1)}, bf16[512,1024]{1,0:T(8,128)(2,1)S(1)}, bf16[512,1024]{1,0:T(8,128)(2,1)S(1)}, bf16[512,1024]{1,0:T(8,12...) custom-call(bf16[512,256]{1,0:T(8,128)(2,1)S(1)} %collective-permute, ...), custom_call_target="tpu_custom_call" | custom-call | flops 1 | bytes 1 | tf_op jit(solution)/shard_map/pallas_call | solution.py:66
  34.3 2.1 %shard_map.149 = (bf16[256,1024]{1,0:T(8,128)(2,1)S(1)}, bf16[512,512]{1,0:T(8,128)(2,1)S(1)}) custom-call(bf16[2,1024,1024]{2,1,0:T(8,128)(2,1)} %refs_0_.5, bf16[512,1024]{1,0:T(8,128)(2,1)S(1)} %get-tuple-element.71.refs_4_.refs_1_, bf16[512,1024]{1,0:T(8,128)(2,1)S(1)} %get-tuple-element.70.refs_5_.refs_2_, ...), custom_call_target="tpu_custom_call" | custom-call | flops 1 | bytes 1 | tf_op jit(solution)/shard_map/pallas_call | solution.py:66
  36.6 7.7 %shard_map.151 = (bf16[320,1024]{1,0:T(8,128)(2,1)S(1)}, bf16[80,1024]{1,0:T(8,128)(2,1)S(1)}, bf16[80,1024]{1,0:T(8,128)(2,1)S(1)}, bf16[80,1024]{1,0:T(8,128)(2,1)S(1)}, bf16[80,1024]{1,0:T(8,128)(2,1)S(1)}) custom-call(bf16[2,1024,1024]{2,1,0:T(8,128)(2,1)} %refs_0_.5, bf16[512,256]{1,0:T(8,128)(2,1)S(1)} %get-tuple-element.66.refs_1_, ...), custom_call_target="tpu_custom_call" | custom-call | flops 1 | bytes 1 | tf_op jit(solution)/shard_map/pallas_call | solution.py:66
  44.3 1.0 collective-permute-done.8.refs_1_
  45.3 2.6 %collective-permute-start.11 = (bf16[128,1024]{1,0:T(8,128)(2,1)S(1)}, bf16[128,1024]{1,0:T(8,128)(2,1)S(1)}, u32[]{:S(2)}, u32[]{:S(2)}) collective-permute-start(bf16[128,1024]{1,0:T(8,128)(2,1)S(1)} %shard_map.152.refs_5_.refs_0_), channel_id=1, source_target_pairs={{0,8},{1,9},{2,10},{3,11},{4,12},{5,13},{6,14},{7,15},{8,0},{9,1},... | collective-permute-start | bytes 786440 | tf_op jit(solution)/shard_map/ppermute | solution.py:370
  50.7 1.5 %collective-permute-start.10 = (bf16[80,1024]{1,0:T(8,128)(2,1)S(1)}, bf16[80,1024]{1,0:T(8,128)(2,1)S(1)}, u32[]{:S(2)}, u32[]{:S(2)}) collective-permute-start(bf16[80,1024]{1,0:T(8,128)(2,1)S(1)} %get-tuple-element.93), channel_id=1, source_target_pairs={{0,2},{1,3},{2,0},{3,1},{4,6},{5,7},{6,4},{7,5},{8,10},{9,11},{10,... | collective-permute-start | bytes 491528 | tf_op jit(solution)/shard_map/ppermute | solution.py:370
  52.3 7.6 %collective-permute-done.11.refs_1_ = bf16[128,1024]{1,0:T(8,128)(2,1)S(1)} collective-permute-done((bf16[128,1024]{1,0:T(8,128)(2,1)S(1)}, bf16[128,1024]{1,0:T(8,128)(2,1)S(1)}, u32[]{:S(2)}, u32[]{:S(2)}) %collective-permute-start.11) | collective-permute-done | bytes 262176 | tf_op jit(solution)/shard_map/ppermute | solution.py:370
  60.0 1.3 %collective-permute-start.15 = (bf16[48,1024]{1,0:T(8,128)(2,1)S(1)}, bf16[48,1024]{1,0:T(8,128)(2,1)S(1)}, u32[]{:S(2)}, u32[]{:S(2)}) collective-permute-start(bf16[48,1024]{1,0:T(8,128)(2,1)S(1)} %get-tuple-element.97.refs_2_), channel_id=1, source_target_pairs={{0,2},{1,3},{2,0},{3,1},{4,6},{5,7},{6,4},{7,5},{8,10},{9,11},{10,... | collective-permute-start | bytes 294920 | tf_op jit(solution)/shard_map/ppermute | solution.py:370
  61.3 1.9 %collective-permute-start.13 = (bf16[80,1024]{1,0:T(8,128)(2,1)S(1)}, bf16[80,1024]{1,0:T(8,128)(2,1)S(1)}, u32[]{:S(2)}, u32[]{:S(2)}) collective-permute-start(bf16[80,1024]{1,0:T(8,128)(2,1)S(1)} %get-tuple-element.96.refs_1_), channel_id=1, source_target_pairs={{0,8},{1,9},{2,10},{3,11},{4,12},{5,13},{6,14},{7,15},{8,0},{9,1},... | collective-permute-start | bytes 491528 | tf_op jit(solution)/shard_map/ppermute | solution.py:370
  63.2 1.1 %collective-permute-start.12 = (bf16[80,1024]{1,0:T(8,128)(2,1)S(1)}, bf16[80,1024]{1,0:T(8,128)(2,1)S(1)}, u32[]{:S(2)}, u32[]{:S(2)}) collective-permute-start(bf16[80,1024]{1,0:T(8,128)(2,1)S(1)} %get-tuple-element.95.refs_4_.refs_0_), channel_id=1, source_target_pairs={{0,8},{1,9},{2,10},{3,11},{4,12},{5,13},{6,14},{7,15},{8,0},{9,1},... | collective-permute-start | bytes 491528 | tf_op jit(solution)/shard_map/ppermute | solution.py:370
  64.7 2.5 %collective-permute-done.14.refs_1_ = bf16[80,1024]{1,0:T(8,128)(2,1)S(1)} collective-permute-done((bf16[80,1024]{1,0:T(8,128)(2,1)S(1)}, bf16[80,1024]{1,0:T(8,128)(2,1)S(1)}, u32[]{:S(2)}, u32[]{:S(2)}) %collective-permute-start.14) | collective-permute-done | bytes 163872 | tf_op jit(solution)/shard_map/ppermute | solution.py:370
  67.2 1.4 %collective-permute-start.18 = (bf16[160,1024]{1,0:T(8,128)(2,1)S(1)}, bf16[160,1024]{1,0:T(8,128)(2,1)S(1)}, u32[]{:S(2)}, u32[]{:S(2)}) collective-permute-start(bf16[160,1024]{1,0:T(8,128)(2,1)S(1)} %get-tuple-element.98.refs_4_.refs_0_), channel_id=1, source_target_pairs={{0,2},{1,3},{2,0},{3,1},{4,6},{5,7},{6,4},{7,5},{8,10},{9,11},{10,... | collective-permute-start | bytes 983048 | tf_op jit(solution)/shard_map/ppermute | solution.py:370
  68.6 7.9 %collective-permute-done.13.refs_3_ = bf16[80,1024]{1,0:T(8,128)(2,1)S(1)} collective-permute-done((bf16[80,1024]{1,0:T(8,128)(2,1)S(1)}, bf16[80,1024]{1,0:T(8,128)(2,1)S(1)}, u32[]{:S(2)}, u32[]{:S(2)}) %collective-permute-start.13) | collective-permute-done | bytes 163872 | tf_op jit(solution)/shard_map/ppermute | solution.py:370
  76.5 2.3 %collective-permute-done.12.refs_2_ = bf16[80,1024]{1,0:T(8,128)(2,1)S(1)} collective-permute-done((bf16[80,1024]{1,0:T(8,128)(2,1)S(1)}, bf16[80,1024]{1,0:T(8,128)(2,1)S(1)}, u32[]{:S(2)}, u32[]{:S(2)}) %collective-permute-start.12) | collective-permute-done | bytes 163872 | tf_op jit(solution)/shard_map/ppermute | solution.py:370
  78.9 0.8 collective-permute-start.17
  80.3 4.0 %collective-permute-done.17.refs_3_ = bf16[80,1024]{1,0:T(8,128)(2,1)S(1)} collective-permute-done((bf16[80,1024]{1,0:T(8,128)(2,1)S(1)}, bf16[80,1024]{1,0:T(8,128)(2,1)S(1)}, u32[]{:S(2)}, u32[]{:S(2)}) %collective-permute-start.17) | collective-permute-done | bytes 163872 | tf_op jit(solution)/shard_map/ppermute | solution.py:370
  85.2 1.4 %collective-permute-start.20 = (bf16[160,1024]{1,0:T(8,128)(2,1)S(1)}, bf16[160,1024]{1,0:T(8,128)(2,1)S(1)}, u32[]{:S(2)}, u32[]{:S(2)}) collective-permute-start(bf16[160,1024]{1,0:T(8,128)(2,1)S(1)} %get-tuple-element.102.refs_1_.refs_0_), channel_id=1, source_target_pairs={{0,2},{1,3},{2,0},{3,1},{4,6},{5,7},{6,4},{7,5},{8,10},{9,11},{10,... | collective-permute-start | bytes 983048 | tf_op jit(solution)/shard_map/ppermute | solution.py:370
  86.6 1.4 %shard_map.160 = (f32[2,1024,1024]{2,1,0:T(8,128)}, f32[8,128]{1,0:T(8,128)S(1)}) custom-call(bf16[512,1024]{1,0:T(8,128)(2,1)S(1)} %get-tuple-element.104.refs_0_, bf16[160,1024]{1,0:T(8,128)(2,1)S(1)} %get-tuple-element.102.refs_1_.refs_0_), custom_call_target="tpu_custom_call" | custom-call | flops 1 | bytes 1 | tf_op jit(solution)/shard_map/pallas_call | solution.py:66
  88.0 1.4 %shard_map.161 = (f32[2,1024,1024]{2,1,0:T(8,128)}, f32[8,128]{1,0:T(8,128)S(1)}) custom-call(bf16[512,1024]{1,0:T(8,128)(2,1)S(1)} %collective-permute-done.22.refs_0_, f32[2,1024,1024]{2,1,0:T(8,128)} %get-tuple-element.105.refs_1_, f32[8,128]{1,0:T(8,128)S(1)} %get-tuple-element.106.refs_2_), custom_call_target="tpu_custom_call", output_to_operand_aliasing={{0}: (1, {})} | custom-call | flops 1 | bytes 1 | tf_op jit(solution)/shard_map/pallas_call | solution.py:66
  89.4 5.9 %collective-permute-done.21.refs_3_ = bf16[160,1024]{1,0:T(8,128)(2,1)S(1)} collective-permute-done((bf16[160,1024]{1,0:T(8,128)(2,1)S(1)}, bf16[160,1024]{1,0:T(8,128)(2,1)S(1)}, u32[]{:S(2)}, u32[]{:S(2)}) %collective-permute-start.21) | collective-permute-done | bytes 327712 | tf_op jit(solution)/shard_map/ppermute | solution.py:370
  95.4 2.0 %shard_map.163 = (f32[2,1024,1024]{2,1,0:T(8,128)}, f32[8,128]{1,0:T(8,128)}) custom-call(bf16[640,1024]{1,0:T(8,128)(2,1)S(1)} %shard_map.162.refs_0_, f32[2,1024,1024]{2,1,0:T(8,128)} %get-tuple-element.108.refs_1_), custom_call_target="tpu_custom_call", output_to_operand_aliasing={{0}: (1, {})} | custom-call | flops 1 | bytes 1 | tf_op jit(solution)/shard_map/pallas_call | solution.py:66
  97.4 1.0 %collective-permute-done.23.refs_1_ = bf16[640,1024]{1,0:T(8,128)(2,1)S(1)} collective-permute-done((bf16[640,1024]{1,0:T(8,128)(2,1)S(1)}, bf16[640,1024]{1,0:T(8,128)(2,1)S(1)}, u32[]{:S(2)}, u32[]{:S(2)}) %collective-permute-start.23) | collective-permute-done | bytes 1310752 | tf_op jit(solution)/shard_map/ppermute | solution.py:370
  98.5 2.8 %shard_map.164 = (f32[2,1024,1024]{2,1,0:T(8,128)}, f32[256,1024]{1,0:T(8,128)}, f32[1024,128]{1,0:T(8,128)}, f32[1,1024]{1,0:T(1,128)}) custom-call(bf16[640,1024]{1,0:T(8,128)(2,1)S(1)} %shard_map.162.refs_0_, bf16[640,1024]{1,0:T(8,128)(2,1)S(1)} %collective-permute-done.23.refs_1_, ...), custom_call_target="tpu_custom_call", output_to_operand_aliasing={{0}: (2, {})} | custom-call | flops 1 | bytes 1 | tf_op jit(solution)/shard_map/pallas_call | solution.py:66
  (47 shorter events, 6.7 us)
Async XLA Ops:
  2.0 15.4 %all-to-all-start = ((f32[16,8,128]{2,1,0:T(8,128)}), f32[16,8,128]{2,1,0:T(8,128)S(1)}, u32[]{:S(2)}, u32[]{:S(2)}) async-start(f32[16,8,128]{2,1,0:T(8,128)} %broadcast_in_dim.23), calls=%async_computation | async-start | bytes 131072 | tf_op jit(solution)/shard_map/all_to_all | solution.py:535
  11.0 6.3 %collective-permute-start.1 = (f32[3,1,32,128]{3,2,1,0:T(8,128)S(1)}, f32[3,1,32,128]{3,2,1,0:T(8,128)S(1)}, u32[]{:S(2)}, u32[]{:S(2)}) collective-permute-start(f32[3,1,32,128]{3,2,1,0:T(8,128)S(1)} %get-tuple-element.118), channel_id=1, source_target_pairs={{0,15},{1,2},{2,1},{3,4},{4,3},{5,6},{6,5},{7,8},{8,7},{9,10},{10,... | collective-permute-start | bytes 147464 | tf_op jit(solution)/shard_map/ppermute | solution.py:534
  15.5 1.8 %collective-permute-start = (f32[3,1,32,128]{3,2,1,0:T(8,128)S(1)}, f32[3,1,32,128]{3,2,1,0:T(8,128)S(1)}, u32[]{:S(2)}, u32[]{:S(2)}) collective-permute-start(f32[3,1,32,128]{3,2,1,0:T(8,128)S(1)} %get-tuple-element.119), channel_id=1, source_target_pairs={{0,1},{1,0},{2,3},{3,2},{4,5},{5,4},{6,7},{7,6},{8,9},{9,8},{10,11... | collective-permute-start | bytes 147464 | tf_op jit(solution)/shard_map/ppermute | solution.py:370
  18.8 8.7 %collective-permute-start.2 = (bf16[512,256]{1,0:T(8,128)(2,1)S(1)}, bf16[512,256]{1,0:T(8,128)(2,1)S(1)}, u32[]{:S(2)}, u32[]{:S(2)}) collective-permute-start(bf16[512,256]{1,0:T(8,128)(2,1)S(1)} %get-tuple-element.64.refs_0_), channel_id=1, source_target_pairs={{0,4},{1,5},{2,6},{3,7},{4,0},{5,1},{6,2},{7,3},{8,12},{9,13},{10,... | collective-permute-start | bytes 786440 | tf_op jit(solution)/shard_map/ppermute | solution.py:370
  34.3 2.2 %collective-permute-start.3 = (bf16[256,1024]{1,0:T(8,128)(2,1)S(1)}, bf16[256,1024]{1,0:T(8,128)(2,1)S(1)}, u32[]{:S(2)}, u32[]{:S(2)}) collective-permute-start(bf16[256,1024]{1,0:T(8,128)(2,1)S(1)} %get-tuple-element.83), channel_id=1, source_target_pairs={{0,1},{1,0},{2,3},{3,2},{4,5},{5,4},{6,7},{7,6},{8,9},{9,8},{10,11... | collective-permute-start | bytes 1572872 | tf_op jit(solution)/shard_map/ppermute | solution.py:370
  36.5 8.8 %collective-permute-start.8 = (bf16[128,1024]{1,0:T(8,128)(2,1)S(1)}, bf16[128,1024]{1,0:T(8,128)(2,1)S(1)}, u32[]{:S(2)}, u32[]{:S(2)}) collective-permute-start(bf16[128,1024]{1,0:T(8,128)(2,1)S(1)} %get-tuple-element.90), channel_id=1, source_target_pairs={{0,2},{1,3},{2,0},{3,1},{4,6},{5,7},{6,4},{7,5},{8,10},{9,11},{10,... | collective-permute-start | bytes 786440 | tf_op jit(solution)/shard_map/ppermute | solution.py:370
  45.3 14.5 %collective-permute-start.11 = (bf16[128,1024]{1,0:T(8,128)(2,1)S(1)}, bf16[128,1024]{1,0:T(8,128)(2,1)S(1)}, u32[]{:S(2)}, u32[]{:S(2)}) collective-permute-start(bf16[128,1024]{1,0:T(8,128)(2,1)S(1)} %shard_map.152.refs_5_.refs_0_), channel_id=1, source_target_pairs={{0,8},{1,9},{2,10},{3,11},{4,12},{5,13},{6,14},{7,15},{8,0},{9,1},... | collective-permute-start | bytes 786440 | tf_op jit(solution)/shard_map/ppermute | solution.py:370
  47.9 1.4 %collective-permute-start.4 = (bf16[80,1024]{1,0:T(8,128)(2,1)S(1)}, bf16[80,1024]{1,0:T(8,128)(2,1)S(1)}, u32[]{:S(2)}, u32[]{:S(2)}) collective-permute-start(bf16[80,1024]{1,0:T(8,128)(2,1)S(1)} %get-tuple-element.86), channel_id=1, source_target_pairs={{0,1},{1,0},{2,3},{3,2},{4,5},{5,4},{6,7},{7,6},{8,9},{9,8},{10,11... | collective-permute-start | bytes 491528 | tf_op jit(solution)/shard_map/ppermute | solution.py:370
  47.9 1.6 %collective-permute-start.5 = (bf16[80,1024]{1,0:T(8,128)(2,1)S(1)}, bf16[80,1024]{1,0:T(8,128)(2,1)S(1)}, u32[]{:S(2)}, u32[]{:S(2)}) collective-permute-start(bf16[80,1024]{1,0:T(8,128)(2,1)S(1)} %get-tuple-element.87), channel_id=1, source_target_pairs={{0,1},{1,0},{2,3},{3,2},{4,5},{5,4},{6,7},{7,6},{8,9},{9,8},{10,11... | collective-permute-start | bytes 491528 | tf_op jit(solution)/shard_map/ppermute | solution.py:370
  48.4 1.4 %collective-permute-start.6 = (bf16[80,1024]{1,0:T(8,128)(2,1)S(1)}, bf16[80,1024]{1,0:T(8,128)(2,1)S(1)}, u32[]{:S(2)}, u32[]{:S(2)}) collective-permute-start(bf16[80,1024]{1,0:T(8,128)(2,1)S(1)} %get-tuple-element.88), channel_id=1, source_target_pairs={{0,1},{1,0},{2,3},{3,2},{4,5},{5,4},{6,7},{7,6},{8,9},{9,8},{10,11... | collective-permute-start | bytes 491528 | tf_op jit(solution)/shard_map/ppermute | solution.py:370
  48.4 1.6 %collective-permute-start.7 = (bf16[80,1024]{1,0:T(8,128)(2,1)S(1)}, bf16[80,1024]{1,0:T(8,128)(2,1)S(1)}, u32[]{:S(2)}, u32[]{:S(2)}) collective-permute-start(bf16[80,1024]{1,0:T(8,128)(2,1)S(1)} %get-tuple-element.89), channel_id=1, source_target_pairs={{0,1},{1,0},{2,3},{3,2},{4,5},{5,4},{6,7},{7,6},{8,9},{9,8},{10,11... | collective-permute-start | bytes 491528 | tf_op jit(solution)/shard_map/ppermute | solution.py:370
  50.2 11.1 %collective-permute-start.9 = (bf16[80,1024]{1,0:T(8,128)(2,1)S(1)}, bf16[80,1024]{1,0:T(8,128)(2,1)S(1)}, u32[]{:S(2)}, u32[]{:S(2)}) collective-permute-start(bf16[80,1024]{1,0:T(8,128)(2,1)S(1)} %get-tuple-element.92), channel_id=1, source_target_pairs={{0,2},{1,3},{2,0},{3,1},{4,6},{5,7},{6,4},{7,5},{8,10},{9,11},{10,... | collective-permute-start | bytes 491528 | tf_op jit(solution)/shard_map/ppermute | solution.py:370
  50.7 10.6 %collective-permute-start.10 = (bf16[80,1024]{1,0:T(8,128)(2,1)S(1)}, bf16[80,1024]{1,0:T(8,128)(2,1)S(1)}, u32[]{:S(2)}, u32[]{:S(2)}) collective-permute-start(bf16[80,1024]{1,0:T(8,128)(2,1)S(1)} %get-tuple-element.93), channel_id=1, source_target_pairs={{0,2},{1,3},{2,0},{3,1},{4,6},{5,7},{6,4},{7,5},{8,10},{9,11},{10,... | collective-permute-start | bytes 491528 | tf_op jit(solution)/shard_map/ppermute | solution.py:370
  59.9 7.3 %collective-permute-start.14 = (bf16[80,1024]{1,0:T(8,128)(2,1)S(1)}, bf16[80,1024]{1,0:T(8,128)(2,1)S(1)}, u32[]{:S(2)}, u32[]{:S(2)}) collective-permute-start(bf16[80,1024]{1,0:T(8,128)(2,1)S(1)} %get-tuple-element.94.refs_3_.refs_0_), channel_id=1, source_target_pairs={{0,4},{1,5},{2,6},{3,7},{4,0},{5,1},{6,2},{7,3},{8,12},{9,13},{10,... | collective-permute-start | bytes 491528 | tf_op jit(solution)/shard_map/ppermute | solution.py:370
  60.0 4.7 %collective-permute-start.15 = (bf16[48,1024]{1,0:T(8,128)(2,1)S(1)}, bf16[48,1024]{1,0:T(8,128)(2,1)S(1)}, u32[]{:S(2)}, u32[]{:S(2)}) collective-permute-start(bf16[48,1024]{1,0:T(8,128)(2,1)S(1)} %get-tuple-element.97.refs_2_), channel_id=1, source_target_pairs={{0,2},{1,3},{2,0},{3,1},{4,6},{5,7},{6,4},{7,5},{8,10},{9,11},{10,... | collective-permute-start | bytes 294920 | tf_op jit(solution)/shard_map/ppermute | solution.py:370
  61.3 15.2 %collective-permute-start.13 = (bf16[80,1024]{1,0:T(8,128)(2,1)S(1)}, bf16[80,1024]{1,0:T(8,128)(2,1)S(1)}, u32[]{:S(2)}, u32[]{:S(2)}) collective-permute-start(bf16[80,1024]{1,0:T(8,128)(2,1)S(1)} %get-tuple-element.96.refs_1_), channel_id=1, source_target_pairs={{0,8},{1,9},{2,10},{3,11},{4,12},{5,13},{6,14},{7,15},{8,0},{9,1},... | collective-permute-start | bytes 491528 | tf_op jit(solution)/shard_map/ppermute | solution.py:370
  63.2 15.7 %collective-permute-start.12 = (bf16[80,1024]{1,0:T(8,128)(2,1)S(1)}, bf16[80,1024]{1,0:T(8,128)(2,1)S(1)}, u32[]{:S(2)}, u32[]{:S(2)}) collective-permute-start(bf16[80,1024]{1,0:T(8,128)(2,1)S(1)} %get-tuple-element.95.refs_4_.refs_0_), channel_id=1, source_target_pairs={{0,8},{1,9},{2,10},{3,11},{4,12},{5,13},{6,14},{7,15},{8,0},{9,1},... | collective-permute-start | bytes 491528 | tf_op jit(solution)/shard_map/ppermute | solution.py:370
  67.2 13.0 %collective-permute-start.18 = (bf16[160,1024]{1,0:T(8,128)(2,1)S(1)}, bf16[160,1024]{1,0:T(8,128)(2,1)S(1)}, u32[]{:S(2)}, u32[]{:S(2)}) collective-permute-start(bf16[160,1024]{1,0:T(8,128)(2,1)S(1)} %get-tuple-element.98.refs_4_.refs_0_), channel_id=1, source_target_pairs={{0,2},{1,3},{2,0},{3,1},{4,6},{5,7},{6,4},{7,5},{8,10},{9,11},{10,... | collective-permute-start | bytes 983048 | tf_op jit(solution)/shard_map/ppermute | solution.py:370
  68.6 11.6 %collective-permute-start.19 = (bf16[96,1024]{1,0:T(8,128)(2,1)S(1)}, bf16[96,1024]{1,0:T(8,128)(2,1)S(1)}, u32[]{:S(2)}, u32[]{:S(2)}) collective-permute-start(bf16[96,1024]{1,0:T(8,128)(2,1)S(1)} %get-tuple-element.101.refs_2_), channel_id=1, source_target_pairs={{0,4},{1,5},{2,6},{3,7},{4,0},{5,1},{6,2},{7,3},{8,12},{9,13},{10,... | collective-permute-start | bytes 589832 | tf_op jit(solution)/shard_map/ppermute | solution.py:370
  78.9 5.4 %collective-permute-start.17 = (bf16[80,1024]{1,0:T(8,128)(2,1)S(1)}, bf16[80,1024]{1,0:T(8,128)(2,1)S(1)}, u32[]{:S(2)}, u32[]{:S(2)}) collective-permute-start(bf16[80,1024]{1,0:T(8,128)(2,1)S(1)} %get-tuple-element.100.refs_2_), channel_id=1, source_target_pairs={{0,2},{1,3},{2,0},{3,1},{4,6},{5,7},{6,4},{7,5},{8,10},{9,11},{10,... | collective-permute-start | bytes 491528 | tf_op jit(solution)/shard_map/ppermute | solution.py:370
  79.7 5.3 %collective-permute-start.16 = (bf16[80,1024]{1,0:T(8,128)(2,1)S(1)}, bf16[80,1024]{1,0:T(8,128)(2,1)S(1)}, u32[]{:S(2)}, u32[]{:S(2)}) collective-permute-start(bf16[80,1024]{1,0:T(8,128)(2,1)S(1)} %get-tuple-element.99.refs_4_.refs_0_), channel_id=1, source_target_pairs={{0,4},{1,5},{2,6},{3,7},{4,0},{5,1},{6,2},{7,3},{8,12},{9,13},{10,... | collective-permute-start | bytes 491528 | tf_op jit(solution)/shard_map/ppermute | solution.py:370
  85.0 2.9 %collective-permute-start.22 = (bf16[512,1024]{1,0:T(8,128)(2,1)S(1)}, bf16[512,1024]{1,0:T(8,128)(2,1)S(1)}, u32[]{:S(2)}, u32[]{:S(2)}) collective-permute-start(bf16[512,1024]{1,0:T(8,128)(2,1)S(1)} %get-tuple-element.104.refs_0_), channel_id=1, source_target_pairs={{0,1},{1,0},{2,3},{3,2},{4,5},{5,4},{6,7},{7,6},{8,9},{9,8},{10,11... | collective-permute-start | bytes 3145736 | tf_op jit(solution)/shard_map/ppermute | solution.py:370
  85.1 10.1 %collective-permute-start.21 = (bf16[160,1024]{1,0:T(8,128)(2,1)S(1)}, bf16[160,1024]{1,0:T(8,128)(2,1)S(1)}, u32[]{:S(2)}, u32[]{:S(2)}) collective-permute-start(bf16[160,1024]{1,0:T(8,128)(2,1)S(1)} %get-tuple-element.103.refs_2_), channel_id=1, source_target_pairs={{0,4},{1,5},{2,6},{3,7},{4,0},{5,1},{6,2},{7,3},{8,12},{9,13},{10,... | collective-permute-start | bytes 983048 | tf_op jit(solution)/shard_map/ppermute | solution.py:370
  85.2 10.1 %collective-permute-start.20 = (bf16[160,1024]{1,0:T(8,128)(2,1)S(1)}, bf16[160,1024]{1,0:T(8,128)(2,1)S(1)}, u32[]{:S(2)}, u32[]{:S(2)}) collective-permute-start(bf16[160,1024]{1,0:T(8,128)(2,1)S(1)} %get-tuple-element.102.refs_1_.refs_0_), channel_id=1, source_target_pairs={{0,2},{1,3},{2,0},{3,1},{4,6},{5,7},{6,4},{7,5},{8,10},{9,11},{10,... | collective-permute-start | bytes 983048 | tf_op jit(solution)/shard_map/ppermute | solution.py:370
  95.4 3.1 %collective-permute-start.23 = (bf16[640,1024]{1,0:T(8,128)(2,1)S(1)}, bf16[640,1024]{1,0:T(8,128)(2,1)S(1)}, u32[]{:S(2)}, u32[]{:S(2)}) collective-permute-start(bf16[640,1024]{1,0:T(8,128)(2,1)S(1)} %shard_map.162.refs_0_), channel_id=1, source_target_pairs={{0,1},{1,0},{2,3},{3,2},{4,5},{5,4},{6,7},{7,6},{8,9},{9,8},{10,11... | collective-permute-start | bytes 3932168 | tf_op jit(solution)/shard_map/ppermute | solution.py:370
